TPU v7x, 512 devices: a whole 4x4x16 slice. The times are simulated.
512 devices in a mesh: row: 64 (over x, z_hi, y), col: 8 (over z_lo, core).
Axes of the slice: x: 4, y: 4, z: 16 (z_hi: 4, z_lo: 4; z = z_hi * 4 + z_lo), core: 2. Of those that a mesh axis runs over, the one named last changes fastest.
Arguments:
- inputs: bfloat16 [512, 12288], P('row', 'col'), may hold values from -6 to 6
- cotangent: bfloat16 [512, 12288], P('row', 'col'), may hold values from -6 to 6
- w1_blocks: bfloat16 [4608, 128, 128], P(('row', 'col')), may hold values from -0.15625 to 0.15625
- w1_where: int32 [4608], P(('row', 'col')), may hold values from 0 to 36863, as said below
- w2_blocks: bfloat16 [4608, 128, 128], P(('row', 'col')), may hold values from -0.078125 to 0.078125
- w2_where: int32 [4608], P(('row', 'col')), may hold values from 0 to 36863, as said below
Outputs:
- input_grad: bfloat16 [512, 12288], P('row', 'col')
- w1_grad: float32 [4608, 128, 128], P(('row', 'col'))
- w2_grad: float32 [4608, 128, 128], P(('row', 'col'))
Inputs may be any that keep to these rules, and one draw needn't show every extreme that they name: Let the device at row index r and col index c hold entries r * 8 + c of the blocks' dimension, 9 of them. Its entries of w1_where name 9 distinct blocks whose block row lies in c * 12 up to (c + 1) * 12 - 1 and whose block column lies in r * 6 up to (r + 1) * 6 - 1; one eighth of the blocks of that region. Likewise the device's entries of w2_where name 9 distinct blocks with block row in r * 6 up to (r + 1) * 6 - 1 and block column in c * 12 up to (c + 1) * 12 - 1.
All inputs are finite; a program needn't handle non-finite values.
Results may differ from a plain program's by a relative error of at most 0.0049.
Values may be sent and summed in bfloat16 or wider, within the bound.
No kernel may reach another device: no remote copies, remote signals or barrier semaphores. Data moves between devices by JAX's collectives and lax.ppermute only.
A program may use at most 64 MiB of HBM per device.

v0:
```python
import math

import jax
import jax.numpy as jnp
from jax import lax
from jax.sharding import PartitionSpec as P

D = 12288
H = 49152


def gelu_value(value):
    inner = math.sqrt(2.0 / math.pi) * (value + 0.044715 * value * value * value)
    return 0.5 * value * (1.0 + jnp.tanh(inner))


def gelu_slope(value):
    inner = math.sqrt(2.0 / math.pi) * (value + 0.044715 * value * value * value)
    tangent = jnp.tanh(inner)
    derive = math.sqrt(2.0 / math.pi) * (1.0 + 3.0 * 0.044715 * value * value)
    return 0.5 * (1.0 + tangent) + 0.5 * value * (1.0 - tangent * tangent) * derive


def apply_blocks(operand, blocks, source, target, width, transpose):
    row_total = operand.shape[0]
    block_size = blocks.shape[1]
    pieces = jnp.take(operand.reshape(row_total, -1, block_size), source, axis=1)
    if transpose:
        product = jnp.einsum("tnm,nkm->tnk", pieces, blocks, preferred_element_type=jnp.float32)
    else:
        product = jnp.einsum("tnk,nkm->tnm", pieces, blocks, preferred_element_type=jnp.float32)
    placement = (target[:, None] == jnp.arange(width, dtype=jnp.int32)[None, :]).astype(jnp.float32)
    result = jnp.einsum("tnm,nc->tcm", product, placement, precision=lax.Precision.HIGHEST)
    return result.reshape(row_total, width * block_size)


def block_grads(left_side, right_side, left_index, right_index, block_size):
    row_total = left_side.shape[0]
    left_part = jnp.take(left_side.reshape(row_total, -1, block_size), left_index, axis=1)
    right_part = jnp.take(right_side.reshape(row_total, -1, block_size), right_index, axis=1)
    return jnp.einsum("tnk,tnm->nkm", left_part, right_part, preferred_element_type=jnp.float32)


def shards(inputs, cotangent, w1_blocks, w1_where, w2_blocks, w2_where):
    block_size = w1_blocks.shape[1]
    row_index = lax.axis_index("row")
    col_index = lax.axis_index("col")
    width_tile = inputs.shape[1]
    hidden_tile = H // lax.axis_size("row")
    tile_rows = width_tile // block_size
    tile_cols = hidden_tile // block_size
    w1_in = w1_where // (H // block_size) - col_index * tile_rows
    w1_hid = w1_where % (H // block_size) - row_index * tile_cols
    w2_hid = w2_where // (D // block_size) - row_index * tile_cols
    w2_in = w2_where % (D // block_size) - col_index * tile_rows
    whole_inputs, whole_cotangent = (
        lax.all_gather(inputs, "row", axis=0, tiled=True),
        lax.all_gather(cotangent, "row", axis=0, tiled=True),
    )
    hidden_terms = apply_blocks(whole_inputs, w1_blocks, w1_in, w1_hid, tile_cols, False)
    back_terms = apply_blocks(whole_cotangent, w2_blocks, w2_in, w2_hid, tile_cols, True)
    hidden = lax.psum(hidden_terms, "col")
    activated = gelu_value(hidden).astype(jnp.bfloat16)
    act_grad = lax.psum(back_terms, "col")
    hidden_grad = (act_grad * gelu_slope(hidden)).astype(jnp.bfloat16)
    w2_grad = block_grads(activated, whole_cotangent, w2_hid, w2_in, block_size)
    w1_grad = block_grads(whole_inputs, hidden_grad, w1_in, w1_hid, block_size)
    input_grad = lax.psum_scatter(
        apply_blocks(hidden_grad, w1_blocks, w1_hid, w1_in, tile_rows, True),
        "row",
        scatter_dimension=0,
        tiled=True,
    )
    return (input_grad.astype(jnp.bfloat16), w1_grad, w2_grad)


def solution(mesh):
    in_specs = (
        P("row", "col"),
        P("row", "col"),
        P(("row", "col"), None, None),
        P(("row", "col")),
        P(("row", "col"), None, None),
        P(("row", "col")),
    )
    out_specs = (P("row", "col"), P(("row", "col"), None, None), P(("row", "col"), None, None))
    return jax.shard_map(shards, mesh=mesh, in_specs=in_specs, out_specs=out_specs, check_vma=False)
```

profile of v0, /device:TPU:1, one launch (start us, length us, event | category | flops | bytes accessed | tf_op | source)
XLA Modules:
  0.0 689.0 jit_solution(11049634851068978262)
XLA Ops:
  7.2 0.7 all-gather.5.cloned.1.call-update
  8.0 0.7 all-gather.3.cloned.1.call-update
  8.7 0.7 compare_and_fusion
  9.5 115.6 %all-gather.5.cloned.1.call-done = bf16[512,1536]{1,0:T(8,128)(2,1)} async-done(((bf16[8,1536]{1,0:T(8,128)(2,1)}), bf16[512,1536]{1,0:T(8,128)(2,1)}) %all-gather.5.cloned.1.call-update) | async-done | bytes 1572880 | tf_op jit(solution)/shard_map/all_gather | solution.py:57
  125.1 1.7 copy.25
  126.8 0.9 copy.26
  127.7 103.5 %all-gather.3.cloned.1.call-done = bf16[512,1536]{1,0:T(8,128)(2,1)} async-done(((bf16[8,1536]{1,0:T(8,128)(2,1)}), bf16[512,1536]{1,0:T(8,128)(2,1)}) %all-gather.3.cloned.1.call-update) | async-done | bytes 1572880 | tf_op jit(solution)/shard_map/all_gather | solution.py:58
  231.2 1.7 copy.21
  232.9 1.6 copy.22
  234.5 2.2 gather_fusion
  236.8 0.5 convolution_bitcast_fusion.2
  237.8 4.1 fusion.9
  241.8 2.7 copy.24
  244.6 0.8 gather_fusion.1
  245.4 0.5 convolution_bitcast_fusion.1
  245.9 0.6 copy-done.3
  246.5 2.7 fusion.12
  249.2 1.7 copy.28
  251.1 94.6 %all-reduce.3.cloned.1.call-done = (f32[512,768]{0,1:T(8,128)}, f32[512,768]{0,1:T(8,128)}) async-done(((f32[512,768]{0,1:T(8,128)}, f32[512,768]{0,1:T(8,128)}), (f32[512,768]{0,1:T(8,128)}, f32[512,768]{0,1:T(8,128)})) %all-reduce.3.cloned.1.call-update) | async-done | bytes 3145744 | tf_op jit(solution)/shard_map/psum | solution.py:64
  345.7 3.9 multiply_convert_fusion
  349.9 0.8 gather_fusion.2
  351.2 0.5 copy-done.5
  351.8 5.2 fusion.6
  357.0 3.4 copy.31
  360.4 2.4 copy.38
  362.8 1.1 copy-done.8
  364.3 1.8 gather_fusion.3
  366.1 1.4 fusion.25
  367.9 1.4 fusion.23
  369.4 311.3 %reduce-scatter.4.cloned.1.call-done = f32[8,1536]{1,0:T(8,128)} async-done(((f32[512,1536]{1,0:T(8,128)}), f32[8,1536]{1,0:T(8,128)}) %reduce-scatter.4.cloned.1.call-update) | async-done | bytes 49168
  680.7 1.0 copy.39
  681.7 0.8 copy.35
  (33 shorter events, 2.5 us)
Async XLA Ops:
  7.2 238.2 %copy-start = (bf16[9,128,128]{2,1,0:T(8,128)(2,1)S(1)}, bf16[9,128,128]{2,1,0:T(8,128)(2,1)}, u32[]{:S(2)}) copy-start(bf16[9,128,128]{2,1,0:T(8,128)(2,1)} %param.12) | copy-start | bytes 884740
  7.2 117.9 %all-gather.5.cloned.1.call-start = ((), (), s32[]{:S(2)}) async-start(), calls=%async_computation.2 | async-start | bytes 1597440 | tf_op jit(solution)/shard_map/all_gather | solution.py:57
  7.9 223.3 %all-gather.3.cloned.1.call-start = ((), (), s32[]{:S(2)}) async-start(), calls=%async_computation.1 | async-start | bytes 1597440 | tf_op jit(solution)/shard_map/all_gather | solution.py:58
  8.7 337.0 %all-reduce.3.cloned.1.call-start = ((), (), s32[]{:S(2)}) async-start(), calls=%async_computation.4 | async-start | bytes 6291456 | tf_op jit(solution)/shard_map/psum | solution.py:64
  234.5 2.2 copy-start.9
  236.7 1.0 copy-start.1
  245.3 1.1 copy-start.3
  250.9 429.8 %reduce-scatter.4.cloned.1.call-start = ((), (), s32[]{:S(2)}) async-start(), calls=%async_computation.3 | async-start | bytes 3194880
  350.7 1.1 copy-start.5
  362.8 1.1 copy-start.8
  364.3 1.9 copy-start.4
  364.3 1.8 copy-start.6
  366.1 1.4 copy-start.2
  366.1 1.8 copy-start.7
Sparse Core Ops, SparseCore 0:
  12.2 112.8 all-gather.4
  129.2 101.8 all-gather.2
  251.0 94.6 all-reduce.2
  362.9 317.7 reduce-scatter.3
where the time goes:
time: 690 us; the launch traced here: 689 us
  waiting for transfers between devices  626 us (91%)
  local copies, waits for them, and re-layouts  27.3 us (4%)
  matrix products  16.4 us (2%)
  between operations  14 us (2%)
    unnamed x5, waiting for transfers between devices  313 us
    all_gather x1, waiting for transfers between devices, shards(): lax.all_gather(inputs, 'row', axis=0, tiled=True)  116 us
    all_gather x1, waiting for transfers between devices, shards(): lax.all_gather(cotangent, 'row', axis=0, tiled=True)  103 us
    psum x1, waiting for transfers between devices, shards(): act_grad = lax.psum(back_terms, 'col')  94.6 us
  transfers between devices with their start and end apart: 4, of which 4 were waited for; matrix products, arithmetic and copies ran while one was open for 1% of the time, Pallas kernels for 0%

commit v1 on v0

v1 whole, which is shorter than its diff:
```python
import math

import jax
import jax.numpy as jnp
from jax import lax
from jax.experimental import pallas as pl
from jax.experimental.pallas import tpu as pltpu
from jax.sharding import Mesh, PartitionSpec as P

BF, F32 = jnp.bfloat16, jnp.float32
BS = 128
TOK = 512
WT = 1536
HT = 768
NI = WT // BS
NJ = HT // BS
NB = 9
W1_COLS = 384
W2_COLS = 96
SIZE = {"x": 4, "y": 4, "zh": 4, "zl": 4, "core": 2}
C0 = math.sqrt(2.0 / math.pi)

VM = pl.BlockSpec(memory_space=pltpu.VMEM)
SM = pl.BlockSpec(memory_space=pltpu.SMEM)


def shift(value, axis, step):
    n = SIZE[axis]
    return lax.ppermute(value, axis, [(i, (i + step) % n) for i in range(n)])


def call(body, ins, outs, scratch=(), flops=0, nbytes=0):
    return pl.pallas_call(
        body,
        out_shape=[jax.ShapeDtypeStruct(s, d) for s, d in outs],
        in_specs=[SM if a.dtype == jnp.int32 else VM for a in ins],
        out_specs=[VM] * len(outs),
        scratch_shapes=list(scratch),
        compiler_params=pltpu.CompilerParams(vmem_limit_bytes=40 * 1024 * 1024),
        cost_estimate=pl.CostEstimate(flops=flops, bytes_accessed=nbytes, transcendentals=0),
    )(*ins)


def w1_pos(where):
    return lax.rem(where // W1_COLS, NI), lax.rem(lax.rem(where, W1_COLS), NJ)


def w2_pos(where):
    return lax.rem(lax.rem(where, W2_COLS), NI), lax.rem(where // W2_COLS, NJ)


def lanes(index):
    return pl.ds(pl.multiple_of(index * BS, BS), BS)


NN = (((1,), (0,)), ((), ()))
NT = (((1,), (1,)), ((), ()))
TN = (((0,), (0,)), ((), ()))


def dot(a, b, dims):
    return lax.dot_general(a, b, dims, preferred_element_type=F32)


def partial_body(pos, dims, where, ids, act, blocks, keep, send, acc):
    acc[...] = jnp.zeros_like(acc)
    for b in range(NB):
        i, j = pos(where[b])
        acc[j] += dot(act[:, lanes(i)], blocks[b], dims)
    core = ids[0]
    half = TOK // 2
    mine = pl.ds(pl.multiple_of(core * half, half), half)
    other = pl.ds(pl.multiple_of((1 - core) * half, half), half)
    for j in range(NJ):
        keep[:, j * BS : (j + 1) * BS] = acc[j, mine]
        send[:, j * BS : (j + 1) * BS] = acc[j, other].astype(BF)


def partial_sums(pos, dims, where, ids, act, blocks):
    half = TOK // 2
    return call(
        lambda *refs: partial_body(pos, dims, *refs),
        (where, ids, act, blocks),
        [((half, HT), F32), ((half, HT), BF)],
        [pltpu.VMEM((NJ, TOK, BS), F32)],
        flops=2 * NB * TOK * BS * BS * 4,
        nbytes=3 << 20,
    )


def split_body(ids, keep, got, mine, s1, s2, s3):
    zl = ids[1]
    q = TOK // 8
    own = pl.ds(pl.multiple_of(zl * q, q), q)
    mine[...] = keep[own] + got[own].astype(F32)
    for k, ref in ((1, s1), (2, s2), (3, s3)):
        part = pl.ds(pl.multiple_of(lax.rem(zl + k, 4) * q, q), q)
        ref[...] = (keep[part] + got[part].astype(F32)).astype(BF)


def column_reduce(ids, keep, send):
    got = shift(send, "core", 1)
    q = TOK // 8
    mine, s1, s2, s3 = call(
        split_body,
        (ids, keep, got),
        [((q, HT), F32)] + [((q, HT), BF)] * 3,
        flops=1 << 20,
        nbytes=2 << 20,
    )
    return [mine, shift(s1, "zl", 1), shift(s2, "zl", 2), shift(s3, "zl", 3)]


def gelu_body(h0, h1, h2, h3, a0, a1, a2, a3, activated, hidden_grad):
    v = h0[...] + h1[...].astype(F32) + h2[...].astype(F32) + h3[...].astype(F32)
    g = a0[...] + a1[...].astype(F32) + a2[...].astype(F32) + a3[...].astype(F32)
    t = jnp.tanh(C0 * (v + 0.044715 * v * v * v))
    derive = C0 * (1.0 + 3.0 * 0.044715 * v * v)
    activated[...] = (0.5 * v * (1.0 + t)).astype(BF)
    slope = 0.5 * (1.0 + t) + 0.5 * v * (1.0 - t * t) * derive
    hidden_grad[...] = (g * slope).astype(BF)


def join_body(ids, p0, p1, p2, p3, out):
    zl = ids[1]
    q = TOK // 8
    for k, ref in enumerate((p0, p1, p2, p3)):
        out[pl.ds(pl.multiple_of(lax.rem(zl + 4 - k, 4) * q, q), q)] = ref[...]


def column_gather(ids, piece):
    parts = (piece, shift(piece, "zl", 1), shift(piece, "zl", 2), shift(piece, "zl", 3))
    (own,) = call(join_body, (ids, *parts), [((TOK // 2, HT), BF)], flops=1 << 20, nbytes=1 << 20)
    return own, shift(own, "core", 1)


def whole_tokens(ids, own, got, whole):
    half = TOK // 2
    core = ids[0]
    whole[pl.ds(pl.multiple_of(core * half, half), half)] = own[...]
    whole[pl.ds(pl.multiple_of((1 - core) * half, half), half)] = got[...]


def input_grad_body(where, ids, own, got, blocks, out, whole, acc):
    whole_tokens(ids, own, got, whole)
    acc[...] = jnp.zeros_like(acc)
    for b in range(NB):
        i, j = w1_pos(where[b])
        acc[i] += dot(whole[:, lanes(j)], blocks[b], NT)
    for i in range(NI):
        out[:, i * BS : (i + 1) * BS] = acc[i].astype(BF)


def input_grad_partial(where, ids, own, got, blocks):
    (out,) = call(
        input_grad_body,
        (where, ids, own, got, blocks),
        [((TOK, WT), BF)],
        [pltpu.VMEM((TOK, HT), BF), pltpu.VMEM((NI, TOK, BS), F32)],
        flops=2 * NB * TOK * BS * BS * 4,
        nbytes=4 << 20,
    )
    return out


def block_grad_body(pos, hidden_left, where, ids, own, got, act, out, whole):
    whole_tokens(ids, own, got, whole)
    for b in range(NB):
        i, j = pos(where[b])
        left, right = act[:, lanes(i)], whole[:, lanes(j)]
        if hidden_left:
            left, right = right, left
        out[b] = dot(left, right, TN)


def block_grads(pos, hidden_left, where, ids, own, got, act):
    (out,) = call(
        lambda *refs: block_grad_body(pos, hidden_left, *refs),
        (where, ids, own, got, act),
        [((NB, BS, BS), F32)],
        [pltpu.VMEM((TOK, HT), BF)],
        flops=2 * NB * TOK * BS * BS * 4,
        nbytes=4 << 20,
    )
    return out


def row_gather(shard):
    near = jnp.concatenate([shard] + [shift(shard, "zh", k) for k in (1, 2, 3)], axis=0)
    sixteen = jnp.broadcast_to(near[None], (16, *near.shape)).reshape(TOK, WT)
    return lax.all_to_all(sixteen, ("x", "y"), 0, 0, tiled=True)


def row_reduce(partial):
    parts = lax.all_to_all(partial, ("x", "y"), 0, 0, tiled=True)
    mine = jnp.sum(parts.reshape(16, 4, 8, WT).astype(F32), axis=0)
    sent = mine.astype(BF)
    total = mine[0]
    for k in (1, 2, 3):
        total = total + shift(sent[k], "zh", -k).astype(F32)
    return total.astype(BF)


def shards(inputs, cotangent, w1_blocks, w1_where, w2_blocks, w2_where):
    ids = jnp.stack([lax.axis_index("core"), lax.axis_index("zl")]).astype(jnp.int32)
    whole_inputs = row_gather(inputs)
    whole_cotangent = row_gather(cotangent)
    hidden = column_reduce(ids, *partial_sums(w1_pos, NN, w1_where, ids, whole_inputs, w1_blocks))
    act_grad = column_reduce(
        ids, *partial_sums(w2_pos, NT, w2_where, ids, whole_cotangent, w2_blocks)
    )
    q = TOK // 8
    activated, hidden_grad = call(
        gelu_body, (*hidden, *act_grad), [((q, HT), BF)] * 2, flops=1 << 22, nbytes=1 << 20
    )
    hg = column_gather(ids, hidden_grad)
    partial = input_grad_partial(w1_where, ids, *hg, w1_blocks)
    input_grad = row_reduce(partial)
    av = column_gather(ids, activated)
    w1_grad = block_grads(w1_pos, False, w1_where, ids, *hg, whole_inputs)
    w2_grad = block_grads(w2_pos, True, w2_where, ids, *av, whole_cotangent)
    return input_grad, w1_grad, w2_grad


def solution(mesh):
    fine = Mesh(mesh.devices.reshape(4, 4, 4, 4, 2), ("x", "zh", "y", "zl", "core"))
    row, col = ("x", "zh", "y"), ("zl", "core")
    both = row + col
    return jax.shard_map(
        shards,
        mesh=fine,
        in_specs=(P(row, col), P(row, col), P(both, None, None), P(both), P(both, None, None), P(both)),
        out_specs=(P(row, col), P(both, None, None), P(both, None, None)),
        check_vma=False,
    )
```

time: 690 us -> 198 us (0.29)
  waiting for transfers between devices: 626 us -> 41.6 us
  starting transfers between devices: 0.34 us -> 129 us
  local copies, waits for them, and re-layouts: 27.3 us -> 7.28 us
  matrix products: 16.4 us -> 0 us
  Pallas kernels: 0 us -> 13.8 us
  between operations: 14 us -> 1.1 us
    unnamed x5 -> x0, waiting for transfers between devices: 313 us -> none
    all_gather x2 -> x0, waiting for transfers between devices: 219 us -> none  [the longest x1 116 us: shards(): lax.all_gather(inputs, 'row', axis=0, tiled=True)]
    ppermute x0 -> x25, starting transfers between devices: none -> 112 us  [shift(): return lax.ppermute(value, axis, [(i, (i + step) % n) for i in range(n)])]
    psum x1 -> x0, waiting for transfers between devices: 94.6 us -> none  [shards(): act_grad = lax.psum(back_terms, 'col')]
    ppermute x0 -> x25, waiting for transfers between devices: none -> 31.6 us  [shift(): return lax.ppermute(value, axis, [(i, (i + step) % n) for i in range(n)])]
    all_to_all x0 -> x3, starting transfers between devices: none -> 17.8 us  [the longest x2 13.4 us: row_gather(): return lax.all_to_all(sixteen, ('x', 'y'), 0, 0, tiled=True)]
    dot_general x8 -> x0, matrix products: 16.4 us -> none  [the longest x3 12 us: apply_blocks(): jnp.einsum('tnm,nc->tcm', product, placement, precision=lax.Precision.HIG...]
    pallas_call x0 -> x10, Pallas kernels: none -> 13.8 us  [call(): pl.pallas_call(body, out_shape=[jax.ShapeDtypeStruct(s, d) for s, d in ou...]
  transfers between devices with their start and end apart: 4 -> 28, of which waited for: 4 -> 11; matrix products, arithmetic and copies ran while one was open for 1% -> 1% of each run, Pallas kernels for 0% -> 5%
where the time goes in v1:
time: 198 us; the launch traced here: 196 us
  starting transfers between devices  129 us (65%)
  waiting for transfers between devices  41.6 us (21%)
  Pallas kernels  13.8 us (7%)
  local copies, waits for them, and re-layouts  7.28 us (4%)
  other arithmetic  3.11 us (2%)
    ppermute x25, starting transfers between devices, shift(): return lax.ppermute(value, axis, [(i, (i + step) % n) for i in range(n)])  112 us
    ppermute x25, waiting for transfers between devices, shift(): return lax.ppermute(value, axis, [(i, (i + step) % n) for i in range(n)])  31.6 us
    pallas_call x10, Pallas kernels, call(): pl.pallas_call(body, out_shape=[jax.ShapeDtypeStruct(s, d) for s, d in ou...  13.8 us
    all_to_all x2, starting transfers between devices, row_gather(): return lax.all_to_all(sixteen, ('x', 'y'), 0, 0, tiled=True)  13.4 us
    all_to_all x2, waiting for transfers between devices, row_gather(): return lax.all_to_all(sixteen, ('x', 'y'), 0, 0, tiled=True)  8.22 us
    unnamed x24, local copies, waits for them, and re-layouts  4.6 us
    all_to_all x1, starting transfers between devices, row_reduce(): parts = lax.all_to_all(partial, ('x', 'y'), 0, 0, tiled=True)  4.4 us
  transfers between devices with their start and end apart: 28, of which 11 were waited for; matrix products, arithmetic and copies ran while one was open for 1% of the time, Pallas kernels for 5%

profile of v1, /device:TPU:1, one launch (start us, length us, event | category | flops | bytes accessed | tf_op | source)
XLA Modules:
  0.0 196.3 jit_solution(16155809605864452315)
XLA Ops:
  0.6 16.3 %collective-permute-start.8 = (bf16[8,1536]{1,0:T(8,128)(2,1)}, bf16[8,1536]{1,0:T(8,128)(2,1)S(1)}, u32[]{:S(2)}, u32[]{:S(2)}) collective-permute-start(bf16[8,1536]{1,0:T(8,128)(2,1)} %param.7), channel_id=1, source_target_pairs={{0,64},{32,96},{64,0},{96,32},{1,65},{33,97},{65,1},{97,33},{2,66}... | collective-permute-start | bytes 73736 | tf_op jit(solution)/shard_map/ppermute | solution.py:29
  16.9 4.0 %collective-permute-start.7 = (bf16[8,1536]{1,0:T(8,128)(2,1)}, bf16[8,1536]{1,0:T(8,128)(2,1)S(1)}, u32[]{:S(2)}, u32[]{:S(2)}) collective-permute-start(bf16[8,1536]{1,0:T(8,128)(2,1)} %param.7), channel_id=1, source_target_pairs={{0,32},{32,64},{64,96},{96,0},{1,33},{33,65},{65,97},{97,1},{2,34}... | collective-permute-start | bytes 73736 | tf_op jit(solution)/shard_map/ppermute | solution.py:29
  20.9 5.2 %collective-permute-start.9 = (bf16[8,1536]{1,0:T(8,128)(2,1)}, bf16[8,1536]{1,0:T(8,128)(2,1)S(1)}, u32[]{:S(2)}, u32[]{:S(2)}) collective-permute-start(bf16[8,1536]{1,0:T(8,128)(2,1)} %param.7), channel_id=1, source_target_pairs={{0,96},{32,0},{64,32},{96,64},{1,97},{33,1},{65,33},{97,65},{2,98}... | collective-permute-start | bytes 73736 | tf_op jit(solution)/shard_map/ppermute | solution.py:29
  26.1 3.5 %collective-permute-done.9 = bf16[8,1536]{1,0:T(8,128)(2,1)S(1)} collective-permute-done((bf16[8,1536]{1,0:T(8,128)(2,1)}, bf16[8,1536]{1,0:T(8,128)(2,1)S(1)}, u32[]{:S(2)}, u32[]{:S(2)}) %collective-permute-start.9) | collective-permute-done | bytes 24608 | tf_op jit(solution)/shard_map/ppermute | solution.py:29
  31.7 6.9 %all-to-all-start.1 = ((bf16[16,32,1536]{2,1,0:T(8,128)(2,1)}), bf16[16,32,1536]{2,1,0:T(8,128)(2,1)S(1)}, u32[]{:S(2)}, u32[]{:S(2)}) async-start(bf16[16,32,1536]{2,1,0:T(8,128)(2,1)} %broadcast_in_dim.5), calls=%async_computation.1 | async-start | bytes 3145728 | tf_op jit(solution)/shard_map/all_to_all | solution.py:191
  38.6 5.0 %collective-permute-start.1 = (bf16[8,1536]{1,0:T(8,128)(2,1)S(1)}, bf16[8,1536]{1,0:T(8,128)(2,1)S(1)}, u32[]{:S(2)}, u32[]{:S(2)}) collective-permute-start(bf16[8,1536]{1,0:T(8,128)(2,1)S(1)} %copy-done.11), channel_id=1, source_target_pairs={{0,64},{32,96},{64,0},{96,32},{1,65},{33,97},{65,1},{97,33},{2,66}... | collective-permute-start | bytes 73736 | tf_op jit(solution)/shard_map/ppermute | solution.py:29
  43.6 7.2 %collective-permute-start = (bf16[8,1536]{1,0:T(8,128)(2,1)S(1)}, bf16[8,1536]{1,0:T(8,128)(2,1)S(1)}, u32[]{:S(2)}, u32[]{:S(2)}) collective-permute-start(bf16[8,1536]{1,0:T(8,128)(2,1)S(1)} %copy-done.11), channel_id=1, source_target_pairs={{0,32},{32,64},{64,96},{96,0},{1,33},{33,65},{65,97},{97,1},{2,34}... | collective-permute-start | bytes 73736 | tf_op jit(solution)/shard_map/ppermute | solution.py:29
  52.8 6.8 %collective-permute-done.2 = bf16[8,1536]{1,0:T(8,128)(2,1)S(1)} collective-permute-done((bf16[8,1536]{1,0:T(8,128)(2,1)S(1)}, bf16[8,1536]{1,0:T(8,128)(2,1)S(1)}, u32[]{:S(2)}, u32[]{:S(2)}) %collective-permute-start.2) | collective-permute-done | bytes 24608 | tf_op jit(solution)/shard_map/ppermute | solution.py:29
  60.9 6.5 %all-to-all-start = ((bf16[16,32,1536]{2,1,0:T(8,128)(2,1)}), bf16[16,32,1536]{2,1,0:T(8,128)(2,1)S(1)}, u32[]{:S(2)}, u32[]{:S(2)}) async-start(bf16[16,32,1536]{2,1,0:T(8,128)(2,1)} %broadcast_in_dim.4), calls=%async_computation | async-start | bytes 3145728 | tf_op jit(solution)/shard_map/all_to_all | solution.py:191
  70.4 6.8 %collective-permute-start.10 = (bf16[256,768]{1,0:T(8,128)(2,1)}, bf16[256,768]{1,0:T(8,128)(2,1)S(1)}, u32[]{:S(2)}, u32[]{:S(2)}) collective-permute-start(bf16[256,768]{1,0:T(8,128)(2,1)} %get-tuple-element.24), channel_id=1, source_target_pairs={{0,1},{1,0},{2,3},{3,2},{4,5},{5,4},{6,7},{7,6},{8,9},{9,8},{10,11... | collective-permute-start | bytes 1179656 | tf_op jit(solution)/shard_map/ppermute | solution.py:29
  77.2 8.2 %all-to-all-done = bf16[16,32,1536]{2,1,0:T(8,128)(2,1)S(1)} async-done(((bf16[16,32,1536]{2,1,0:T(8,128)(2,1)}), bf16[16,32,1536]{2,1,0:T(8,128)(2,1)S(1)}, u32[]{:S(2)}, u32[]{:S(2)}) %all-to-all-start) | async-done | bytes 1572896 | tf_op jit(solution)/shard_map/all_to_all | solution.py:191
  87.6 7.9 %collective-permute-start.3 = (bf16[256,768]{1,0:T(8,128)(2,1)S(1)}, bf16[256,768]{1,0:T(8,128)(2,1)S(1)}, u32[]{:S(2)}, u32[]{:S(2)}) collective-permute-start(bf16[256,768]{1,0:T(8,128)(2,1)S(1)} %get-tuple-element.18), channel_id=1, source_target_pairs={{0,1},{1,0},{2,3},{3,2},{4,5},{5,4},{6,7},{7,6},{8,9},{9,8},{10,11... | collective-permute-start | bytes 1179656 | tf_op jit(solution)/shard_map/ppermute | solution.py:29
  96.2 2.8 %collective-permute-start.11 = (bf16[64,768]{1,0:T(8,128)(2,1)S(1)}, bf16[64,768]{1,0:T(8,128)(2,1)S(1)}, u32[]{:S(2)}, u32[]{:S(2)}) collective-permute-start(bf16[64,768]{1,0:T(8,128)(2,1)S(1)} %get-tuple-element.26), channel_id=1, source_target_pairs={{0,2},{2,4},{4,6},{6,0},{1,3},{3,5},{5,7},{7,1},{8,10},{10,12},{12... | collective-permute-start | bytes 294920 | tf_op jit(solution)/shard_map/ppermute | solution.py:29
  99.0 3.1 %collective-permute-start.12 = (bf16[64,768]{1,0:T(8,128)(2,1)S(1)}, bf16[64,768]{1,0:T(8,128)(2,1)S(1)}, u32[]{:S(2)}, u32[]{:S(2)}) collective-permute-start(bf16[64,768]{1,0:T(8,128)(2,1)S(1)} %get-tuple-element.27), channel_id=1, source_target_pairs={{0,4},{2,6},{4,0},{6,2},{1,5},{3,7},{5,1},{7,3},{8,12},{10,14},{12... | collective-permute-start | bytes 294920 | tf_op jit(solution)/shard_map/ppermute | solution.py:29
  102.1 3.5 %collective-permute-start.13 = (bf16[64,768]{1,0:T(8,128)(2,1)S(1)}, bf16[64,768]{1,0:T(8,128)(2,1)S(1)}, u32[]{:S(2)}, u32[]{:S(2)}) collective-permute-start(bf16[64,768]{1,0:T(8,128)(2,1)S(1)} %get-tuple-element.28), channel_id=1, source_target_pairs={{0,6},{2,0},{4,2},{6,4},{1,7},{3,1},{5,3},{7,5},{8,14},{10,8},{12,... | collective-permute-start | bytes 294920 | tf_op jit(solution)/shard_map/ppermute | solution.py:29
  108.2 3.1 %collective-permute-start.5 = (bf16[64,768]{1,0:T(8,128)(2,1)S(1)}, bf16[64,768]{1,0:T(8,128)(2,1)S(1)}, u32[]{:S(2)}, u32[]{:S(2)}) collective-permute-start(bf16[64,768]{1,0:T(8,128)(2,1)S(1)} %get-tuple-element.21), channel_id=1, source_target_pairs={{0,4},{2,6},{4,0},{6,2},{1,5},{3,7},{5,1},{7,3},{8,12},{10,14},{12... | collective-permute-start | bytes 294920 | tf_op jit(solution)/shard_map/ppermute | solution.py:29
  111.3 4.3 %collective-permute-start.6 = (bf16[64,768]{1,0:T(8,128)(2,1)S(1)}, bf16[64,768]{1,0:T(8,128)(2,1)S(1)}, u32[]{:S(2)}, u32[]{:S(2)}) collective-permute-start(bf16[64,768]{1,0:T(8,128)(2,1)S(1)} %get-tuple-element.22), channel_id=1, source_target_pairs={{0,6},{2,0},{4,2},{6,4},{1,7},{3,1},{5,3},{7,5},{8,14},{10,8},{12,... | collective-permute-start | bytes 294920 | tf_op jit(solution)/shard_map/ppermute | solution.py:29
  115.6 3.1 %collective-permute-done.5.h2 = bf16[64,768]{1,0:T(8,128)(2,1)S(1)} collective-permute-done((bf16[64,768]{1,0:T(8,128)(2,1)S(1)}, bf16[64,768]{1,0:T(8,128)(2,1)S(1)}, u32[]{:S(2)}, u32[]{:S(2)}) %collective-permute-start.5) | collective-permute-done | bytes 98336 | tf_op jit(solution)/shard_map/ppermute | solution.py:29
  119.8 3.2 %collective-permute-start.16 = (bf16[64,768]{1,0:T(8,128)(2,1)S(1)}, bf16[64,768]{1,0:T(8,128)(2,1)S(1)}, u32[]{:S(2)}, u32[]{:S(2)}) collective-permute-start(bf16[64,768]{1,0:T(8,128)(2,1)S(1)} %get-tuple-element.29.p0), channel_id=1, source_target_pairs={{0,6},{2,0},{4,2},{6,4},{1,7},{3,1},{5,3},{7,5},{8,14},{10,8},{12,... | collective-permute-start | bytes 294920 | tf_op jit(solution)/shard_map/ppermute | solution.py:29
  123.0 2.7 %collective-permute-start.15 = (bf16[64,768]{1,0:T(8,128)(2,1)S(1)}, bf16[64,768]{1,0:T(8,128)(2,1)S(1)}, u32[]{:S(2)}, u32[]{:S(2)}) collective-permute-start(bf16[64,768]{1,0:T(8,128)(2,1)S(1)} %get-tuple-element.29.p0), channel_id=1, source_target_pairs={{0,4},{2,6},{4,0},{6,2},{1,5},{3,7},{5,1},{7,3},{8,12},{10,14},{12... | collective-permute-start | bytes 294920 | tf_op jit(solution)/shard_map/ppermute | solution.py:29
  127.6 3.6 %collective-permute-done.15.p2 = bf16[64,768]{1,0:T(8,128)(2,1)S(1)} collective-permute-done((bf16[64,768]{1,0:T(8,128)(2,1)S(1)}, bf16[64,768]{1,0:T(8,128)(2,1)S(1)}, u32[]{:S(2)}, u32[]{:S(2)}) %collective-permute-start.15) | collective-permute-done | bytes 98336 | tf_op jit(solution)/shard_map/ppermute | solution.py:29
  133.6 5.0 %collective-permute-start.17 = (bf16[256,768]{1,0:T(8,128)(2,1)S(1)}, bf16[256,768]{1,0:T(8,128)(2,1)S(1)}, u32[]{:S(2)}, u32[]{:S(2)}) collective-permute-start(bf16[256,768]{1,0:T(8,128)(2,1)S(1)} %shard_map.90.own.refs_2_), channel_id=1, source_target_pairs={{0,1},{1,0},{2,3},{3,2},{4,5},{5,4},{6,7},{7,6},{8,9},{9,8},{10,11... | collective-permute-start | bytes 1179656 | tf_op jit(solution)/shard_map/ppermute | solution.py:29
  139.9 2.7 %shard_map.91 = bf16[512,1536]{1,0:T(8,128)(2,1)} custom-call(s32[9]{0:T(128)S(1)} %copy-done.8, s32[2]{0:T(128)S(1)} %pad_add_fusion.refs_1_.ids, bf16[256,768]{1,0:T(8,128)(2,1)S(1)} %shard_map.90.own.refs_2_, bf16[256,768]{1,0:T(8,128)(2,1)S(1)} %collective-permute-done.17.got.refs_3_, bf16[9,128,128]{2,1,0:T(8,128)(2,1)S(1)} %copy-done.5), custom_call_target="tpu_custom_call" | custom-call | flops 603979776 | bytes 4194304 | tf_op jit(solution)/shard_map/pallas_call | solution.py:33
  143.3 4.4 %all-to-all-start.2 = ((bf16[16,32,1536]{2,1,0:T(8,128)(2,1)}), bf16[16,32,1536]{2,1,0:T(8,128)(2,1)}, u32[]{:S(2)}, u32[]{:S(2)}) async-start(bf16[16,32,1536]{2,1,0:T(8,128)(2,1)} %bitcast.4), calls=%async_computation.2 | async-start | bytes 3145728 | tf_op jit(solution)/shard_map/all_to_all | solution.py:195
  152.4 3.4 %collective-permute-start.21 = (bf16[64,768]{1,0:T(8,128)(2,1)}, bf16[64,768]{1,0:T(8,128)(2,1)S(1)}, u32[]{:S(2)}, u32[]{:S(2)}) collective-permute-start(bf16[64,768]{1,0:T(8,128)(2,1)} %copy-done.6), channel_id=1, source_target_pairs={{0,2},{2,4},{4,6},{6,0},{1,3},{3,5},{5,7},{7,1},{8,10},{10,12},{12... | collective-permute-start | bytes 294920 | tf_op jit(solution)/shard_map/ppermute | solution.py:29
  155.8 4.5 %collective-permute-done.22.p2 = bf16[64,768]{1,0:T(8,128)(2,1)S(1)} collective-permute-done((bf16[64,768]{1,0:T(8,128)(2,1)}, bf16[64,768]{1,0:T(8,128)(2,1)S(1)}, u32[]{:S(2)}, u32[]{:S(2)}) %collective-permute-start.22) | collective-permute-done | bytes 98336 | tf_op jit(solution)/shard_map/ppermute | solution.py:29
  162.5 4.1 %collective-permute-start.24 = (bf16[256,768]{1,0:T(8,128)(2,1)}, bf16[256,768]{1,0:T(8,128)(2,1)}, u32[]{:S(2)}, u32[]{:S(2)}) collective-permute-start(bf16[256,768]{1,0:T(8,128)(2,1)} %shard_map.93.refs_2_), channel_id=1, source_target_pairs={{0,1},{1,0},{2,3},{3,2},{4,5},{5,4},{6,7},{7,6},{8,9},{9,8},{10,11... | collective-permute-start | bytes 1179656 | tf_op jit(solution)/shard_map/ppermute | solution.py:29
  173.1 3.2 %collective-permute-start.18 = (bf16[8,1536]{1,0:T(8,128)(2,1)S(1)}, bf16[8,1536]{1,0:T(8,128)(2,1)S(1)}, u32[]{:S(2)}, u32[]{:S(2)}) collective-permute-start(bf16[8,1536]{1,0:T(8,128)(2,1)S(1)} %get-tuple-element.31), channel_id=1, source_target_pairs={{0,96},{32,0},{64,32},{96,64},{1,97},{33,1},{65,33},{97,65},{2,98}... | collective-permute-start | bytes 73736 | tf_op jit(solution)/shard_map/ppermute | solution.py:29
  176.3 6.0 %collective-permute-start.20 = (bf16[8,1536]{1,0:T(8,128)(2,1)S(1)}, bf16[8,1536]{1,0:T(8,128)(2,1)S(1)}, u32[]{:S(2)}, u32[]{:S(2)}) collective-permute-start(bf16[8,1536]{1,0:T(8,128)(2,1)S(1)} %get-tuple-element.32), channel_id=1, source_target_pairs={{0,32},{32,64},{64,96},{96,0},{1,33},{33,65},{65,97},{97,1},{2,34}... | collective-permute-start | bytes 73736 | tf_op jit(solution)/shard_map/ppermute | solution.py:29
  182.3 4.5 %collective-permute-start.19 = (bf16[8,1536]{1,0:T(8,128)(2,1)S(1)}, bf16[8,1536]{1,0:T(8,128)(2,1)S(1)}, u32[]{:S(2)}, u32[]{:S(2)}) collective-permute-start(bf16[8,1536]{1,0:T(8,128)(2,1)S(1)} %get-tuple-element.33), channel_id=1, source_target_pairs={{0,64},{32,96},{64,0},{96,32},{1,65},{33,97},{65,1},{97,33},{2,66}... | collective-permute-start | bytes 73736 | tf_op jit(solution)/shard_map/ppermute | solution.py:29
  186.8 2.6 %shard_map.94 = f32[9,128,128]{2,1,0:T(8,128)} custom-call(s32[9]{0:T(128)S(1)} %copy-done.9, s32[2]{0:T(128)S(1)} %pad_add_fusion.refs_1_.ids, bf16[256,768]{1,0:T(8,128)(2,1)} %shard_map.93.refs_2_, bf16[256,768]{1,0:T(8,128)(2,1)} %collective-permute-done.24.refs_3_, bf16[512,1536]{1,0:T(8,128)(2,1)S(1)} %bitcast.6), custom_call_target="tpu_custom_call" | custom-call | flops 603979776 | bytes 4194304 | tf_op jit(solution)/shard_map/pallas_call | solution.py:33
  189.4 6.3 %collective-permute-done.19 = bf16[8,1536]{1,0:T(8,128)(2,1)S(1)} collective-permute-done((bf16[8,1536]{1,0:T(8,128)(2,1)S(1)}, bf16[8,1536]{1,0:T(8,128)(2,1)S(1)}, u32[]{:S(2)}, u32[]{:S(2)}) %collective-permute-start.19) | collective-permute-done | bytes 24608 | tf_op jit(solution)/shard_map/ppermute | solution.py:29
  (67 shorter events, 35.0 us)
Async XLA Ops:
  0.6 25.5 %collective-permute-start.8 = (bf16[8,1536]{1,0:T(8,128)(2,1)}, bf16[8,1536]{1,0:T(8,128)(2,1)S(1)}, u32[]{:S(2)}, u32[]{:S(2)}) collective-permute-start(bf16[8,1536]{1,0:T(8,128)(2,1)} %param.7), channel_id=1, source_target_pairs={{0,64},{32,96},{64,0},{96,32},{1,65},{33,97},{65,1},{97,33},{2,66}... | collective-permute-start | bytes 73736 | tf_op jit(solution)/shard_map/ppermute | solution.py:29
  16.9 9.2 %collective-permute-start.7 = (bf16[8,1536]{1,0:T(8,128)(2,1)}, bf16[8,1536]{1,0:T(8,128)(2,1)S(1)}, u32[]{:S(2)}, u32[]{:S(2)}) collective-permute-start(bf16[8,1536]{1,0:T(8,128)(2,1)} %param.7), channel_id=1, source_target_pairs={{0,32},{32,64},{64,96},{96,0},{1,33},{33,65},{65,97},{97,1},{2,34}... | collective-permute-start | bytes 73736 | tf_op jit(solution)/shard_map/ppermute | solution.py:29
  20.9 8.7 %collective-permute-start.9 = (bf16[8,1536]{1,0:T(8,128)(2,1)}, bf16[8,1536]{1,0:T(8,128)(2,1)S(1)}, u32[]{:S(2)}, u32[]{:S(2)}) collective-permute-start(bf16[8,1536]{1,0:T(8,128)(2,1)} %param.7), channel_id=1, source_target_pairs={{0,96},{32,0},{64,32},{96,64},{1,97},{33,1},{65,33},{97,65},{2,98}... | collective-permute-start | bytes 73736 | tf_op jit(solution)/shard_map/ppermute | solution.py:29
  31.7 27.9 %all-to-all-start.1 = ((bf16[16,32,1536]{2,1,0:T(8,128)(2,1)}), bf16[16,32,1536]{2,1,0:T(8,128)(2,1)S(1)}, u32[]{:S(2)}, u32[]{:S(2)}) async-start(bf16[16,32,1536]{2,1,0:T(8,128)(2,1)} %broadcast_in_dim.5), calls=%async_computation.1 | async-start | bytes 3145728 | tf_op jit(solution)/shard_map/all_to_all | solution.py:191
  38.6 14.2 %collective-permute-start.1 = (bf16[8,1536]{1,0:T(8,128)(2,1)S(1)}, bf16[8,1536]{1,0:T(8,128)(2,1)S(1)}, u32[]{:S(2)}, u32[]{:S(2)}) collective-permute-start(bf16[8,1536]{1,0:T(8,128)(2,1)S(1)} %copy-done.11), channel_id=1, source_target_pairs={{0,64},{32,96},{64,0},{96,32},{1,65},{33,97},{65,1},{97,33},{2,66}... | collective-permute-start | bytes 73736 | tf_op jit(solution)/shard_map/ppermute | solution.py:29
  43.6 9.2 %collective-permute-start = (bf16[8,1536]{1,0:T(8,128)(2,1)S(1)}, bf16[8,1536]{1,0:T(8,128)(2,1)S(1)}, u32[]{:S(2)}, u32[]{:S(2)}) collective-permute-start(bf16[8,1536]{1,0:T(8,128)(2,1)S(1)} %copy-done.11), channel_id=1, source_target_pairs={{0,32},{32,64},{64,96},{96,0},{1,33},{33,65},{65,97},{97,1},{2,34}... | collective-permute-start | bytes 73736 | tf_op jit(solution)/shard_map/ppermute | solution.py:29
  50.8 8.8 %collective-permute-start.2 = (bf16[8,1536]{1,0:T(8,128)(2,1)S(1)}, bf16[8,1536]{1,0:T(8,128)(2,1)S(1)}, u32[]{:S(2)}, u32[]{:S(2)}) collective-permute-start(bf16[8,1536]{1,0:T(8,128)(2,1)S(1)} %copy-done.11), channel_id=1, source_target_pairs={{0,96},{32,0},{64,32},{96,64},{1,97},{33,1},{65,33},{97,65},{2,98}... | collective-permute-start | bytes 73736 | tf_op jit(solution)/shard_map/ppermute | solution.py:29
  60.9 24.5 %all-to-all-start = ((bf16[16,32,1536]{2,1,0:T(8,128)(2,1)}), bf16[16,32,1536]{2,1,0:T(8,128)(2,1)S(1)}, u32[]{:S(2)}, u32[]{:S(2)}) async-start(bf16[16,32,1536]{2,1,0:T(8,128)(2,1)} %broadcast_in_dim.4), calls=%async_computation | async-start | bytes 3145728 | tf_op jit(solution)/shard_map/all_to_all | solution.py:191
  67.5 18.0 %copy-start.8 = (s32[9]{0:T(128)S(1)}, s32[9]{0:T(128)}, u32[]{:S(2)}) copy-start(s32[9]{0:T(128)} %refs_0_.6) | copy-start | bytes 112
  70.4 25.1 %collective-permute-start.10 = (bf16[256,768]{1,0:T(8,128)(2,1)}, bf16[256,768]{1,0:T(8,128)(2,1)S(1)}, u32[]{:S(2)}, u32[]{:S(2)}) collective-permute-start(bf16[256,768]{1,0:T(8,128)(2,1)} %get-tuple-element.24), channel_id=1, source_target_pairs={{0,1},{1,0},{2,3},{3,2},{4,5},{5,4},{6,7},{7,6},{8,9},{9,8},{10,11... | collective-permute-start | bytes 1179656 | tf_op jit(solution)/shard_map/ppermute | solution.py:29
  85.4 10.1 %copy-start.3 = (f32[256,768]{1,0:T(8,128)S(1)}, f32[256,768]{1,0:T(8,128)}, u32[]{:S(2)}) copy-start(f32[256,768]{1,0:T(8,128)} %copy-done.2) | copy-start | bytes 2359300
  87.6 18.0 %collective-permute-start.3 = (bf16[256,768]{1,0:T(8,128)(2,1)S(1)}, bf16[256,768]{1,0:T(8,128)(2,1)S(1)}, u32[]{:S(2)}, u32[]{:S(2)}) collective-permute-start(bf16[256,768]{1,0:T(8,128)(2,1)S(1)} %get-tuple-element.18), channel_id=1, source_target_pairs={{0,1},{1,0},{2,3},{3,2},{4,5},{5,4},{6,7},{7,6},{8,9},{9,8},{10,11... | collective-permute-start | bytes 1179656 | tf_op jit(solution)/shard_map/ppermute | solution.py:29
  96.2 43.7 %copy-start.5 = (bf16[9,128,128]{2,1,0:T(8,128)(2,1)S(1)}, bf16[9,128,128]{2,1,0:T(8,128)(2,1)}, u32[]{:S(2)}) copy-start(bf16[9,128,128]{2,1,0:T(8,128)(2,1)} %blocks.1) | copy-start | bytes 884740
  96.2 15.1 %collective-permute-start.11 = (bf16[64,768]{1,0:T(8,128)(2,1)S(1)}, bf16[64,768]{1,0:T(8,128)(2,1)S(1)}, u32[]{:S(2)}, u32[]{:S(2)}) collective-permute-start(bf16[64,768]{1,0:T(8,128)(2,1)S(1)} %get-tuple-element.26), channel_id=1, source_target_pairs={{0,2},{2,4},{4,6},{6,0},{1,3},{3,5},{5,7},{7,1},{8,10},{10,12},{12... | collective-permute-start | bytes 294920 | tf_op jit(solution)/shard_map/ppermute | solution.py:29
  99.0 16.6 %collective-permute-start.12 = (bf16[64,768]{1,0:T(8,128)(2,1)S(1)}, bf16[64,768]{1,0:T(8,128)(2,1)S(1)}, u32[]{:S(2)}, u32[]{:S(2)}) collective-permute-start(bf16[64,768]{1,0:T(8,128)(2,1)S(1)} %get-tuple-element.27), channel_id=1, source_target_pairs={{0,4},{2,6},{4,0},{6,2},{1,5},{3,7},{5,1},{7,3},{8,12},{10,14},{12... | collective-permute-start | bytes 294920 | tf_op jit(solution)/shard_map/ppermute | solution.py:29
  102.1 13.5 %collective-permute-start.13 = (bf16[64,768]{1,0:T(8,128)(2,1)S(1)}, bf16[64,768]{1,0:T(8,128)(2,1)S(1)}, u32[]{:S(2)}, u32[]{:S(2)}) collective-permute-start(bf16[64,768]{1,0:T(8,128)(2,1)S(1)} %get-tuple-element.28), channel_id=1, source_target_pairs={{0,6},{2,0},{4,2},{6,4},{1,7},{3,1},{5,3},{7,5},{8,14},{10,8},{12,... | collective-permute-start | bytes 294920 | tf_op jit(solution)/shard_map/ppermute | solution.py:29
  106.3 9.3 %collective-permute-start.4 = (bf16[64,768]{1,0:T(8,128)(2,1)S(1)}, bf16[64,768]{1,0:T(8,128)(2,1)S(1)}, u32[]{:S(2)}, u32[]{:S(2)}) collective-permute-start(bf16[64,768]{1,0:T(8,128)(2,1)S(1)} %get-tuple-element.20), channel_id=1, source_target_pairs={{0,2},{2,4},{4,6},{6,0},{1,3},{3,5},{5,7},{7,1},{8,10},{10,12},{12... | collective-permute-start | bytes 294920 | tf_op jit(solution)/shard_map/ppermute | solution.py:29
  108.2 10.5 %collective-permute-start.5 = (bf16[64,768]{1,0:T(8,128)(2,1)S(1)}, bf16[64,768]{1,0:T(8,128)(2,1)S(1)}, u32[]{:S(2)}, u32[]{:S(2)}) collective-permute-start(bf16[64,768]{1,0:T(8,128)(2,1)S(1)} %get-tuple-element.21), channel_id=1, source_target_pairs={{0,4},{2,6},{4,0},{6,2},{1,5},{3,7},{5,1},{7,3},{8,12},{10,14},{12... | collective-permute-start | bytes 294920 | tf_op jit(solution)/shard_map/ppermute | solution.py:29
  111.3 8.3 %collective-permute-start.6 = (bf16[64,768]{1,0:T(8,128)(2,1)S(1)}, bf16[64,768]{1,0:T(8,128)(2,1)S(1)}, u32[]{:S(2)}, u32[]{:S(2)}) collective-permute-start(bf16[64,768]{1,0:T(8,128)(2,1)S(1)} %get-tuple-element.22), channel_id=1, source_target_pairs={{0,6},{2,0},{4,2},{6,4},{1,7},{3,1},{5,3},{7,5},{8,14},{10,8},{12,... | collective-permute-start | bytes 294920 | tf_op jit(solution)/shard_map/ppermute | solution.py:29
  119.8 13.7 %copy-start.6 = (bf16[64,768]{1,0:T(8,128)(2,1)}, bf16[64,768]{1,0:T(8,128)(2,1)S(1)}, u32[]{:S(2)}) copy-start(bf16[64,768]{1,0:T(8,128)(2,1)S(1)} %get-tuple-element.30.p0) | copy-start | bytes 294916
  119.8 7.8 %collective-permute-start.16 = (bf16[64,768]{1,0:T(8,128)(2,1)S(1)}, bf16[64,768]{1,0:T(8,128)(2,1)S(1)}, u32[]{:S(2)}, u32[]{:S(2)}) collective-permute-start(bf16[64,768]{1,0:T(8,128)(2,1)S(1)} %get-tuple-element.29.p0), channel_id=1, source_target_pairs={{0,6},{2,0},{4,2},{6,4},{1,7},{3,1},{5,3},{7,5},{8,14},{10,8},{12,... | collective-permute-start | bytes 294920 | tf_op jit(solution)/shard_map/ppermute | solution.py:29
  123.0 8.3 %collective-permute-start.15 = (bf16[64,768]{1,0:T(8,128)(2,1)S(1)}, bf16[64,768]{1,0:T(8,128)(2,1)S(1)}, u32[]{:S(2)}, u32[]{:S(2)}) collective-permute-start(bf16[64,768]{1,0:T(8,128)(2,1)S(1)} %get-tuple-element.29.p0), channel_id=1, source_target_pairs={{0,4},{2,6},{4,0},{6,2},{1,5},{3,7},{5,1},{7,3},{8,12},{10,14},{12... | collective-permute-start | bytes 294920 | tf_op jit(solution)/shard_map/ppermute | solution.py:29
  125.7 7.3 %collective-permute-start.14 = (bf16[64,768]{1,0:T(8,128)(2,1)S(1)}, bf16[64,768]{1,0:T(8,128)(2,1)S(1)}, u32[]{:S(2)}, u32[]{:S(2)}) collective-permute-start(bf16[64,768]{1,0:T(8,128)(2,1)S(1)} %get-tuple-element.29.p0), channel_id=1, source_target_pairs={{0,2},{2,4},{4,6},{6,0},{1,3},{3,5},{5,7},{7,1},{8,10},{10,12},{12... | collective-permute-start | bytes 294920 | tf_op jit(solution)/shard_map/ppermute | solution.py:29
  133.6 6.3 %collective-permute-start.17 = (bf16[256,768]{1,0:T(8,128)(2,1)S(1)}, bf16[256,768]{1,0:T(8,128)(2,1)S(1)}, u32[]{:S(2)}, u32[]{:S(2)}) collective-permute-start(bf16[256,768]{1,0:T(8,128)(2,1)S(1)} %shard_map.90.own.refs_2_), channel_id=1, source_target_pairs={{0,1},{1,0},{2,3},{3,2},{4,5},{5,4},{6,7},{7,6},{8,9},{9,8},{10,11... | collective-permute-start | bytes 1179656 | tf_op jit(solution)/shard_map/ppermute | solution.py:29
  143.3 28.0 %all-to-all-start.2 = ((bf16[16,32,1536]{2,1,0:T(8,128)(2,1)}), bf16[16,32,1536]{2,1,0:T(8,128)(2,1)}, u32[]{:S(2)}, u32[]{:S(2)}) async-start(bf16[16,32,1536]{2,1,0:T(8,128)(2,1)} %bitcast.4), calls=%async_computation.2 | async-start | bytes 3145728 | tf_op jit(solution)/shard_map/all_to_all | solution.py:195
  147.8 8.0 %collective-permute-start.23 = (bf16[64,768]{1,0:T(8,128)(2,1)}, bf16[64,768]{1,0:T(8,128)(2,1)S(1)}, u32[]{:S(2)}, u32[]{:S(2)}) collective-permute-start(bf16[64,768]{1,0:T(8,128)(2,1)} %copy-done.6), channel_id=1, source_target_pairs={{0,6},{2,0},{4,2},{6,4},{1,7},{3,1},{5,3},{7,5},{8,14},{10,8},{12,... | collective-permute-start | bytes 294920 | tf_op jit(solution)/shard_map/ppermute | solution.py:29
  150.1 10.2 %collective-permute-start.22 = (bf16[64,768]{1,0:T(8,128)(2,1)}, bf16[64,768]{1,0:T(8,128)(2,1)S(1)}, u32[]{:S(2)}, u32[]{:S(2)}) collective-permute-start(bf16[64,768]{1,0:T(8,128)(2,1)} %copy-done.6), channel_id=1, source_target_pairs={{0,4},{2,6},{4,0},{6,2},{1,5},{3,7},{5,1},{7,3},{8,12},{10,14},{12... | collective-permute-start | bytes 294920 | tf_op jit(solution)/shard_map/ppermute | solution.py:29
  152.4 7.8 %collective-permute-start.21 = (bf16[64,768]{1,0:T(8,128)(2,1)}, bf16[64,768]{1,0:T(8,128)(2,1)S(1)}, u32[]{:S(2)}, u32[]{:S(2)}) collective-permute-start(bf16[64,768]{1,0:T(8,128)(2,1)} %copy-done.6), channel_id=1, source_target_pairs={{0,2},{2,4},{4,6},{6,0},{1,3},{3,5},{5,7},{7,1},{8,10},{10,12},{12... | collective-permute-start | bytes 294920 | tf_op jit(solution)/shard_map/ppermute | solution.py:29
  162.5 24.3 %collective-permute-start.24 = (bf16[256,768]{1,0:T(8,128)(2,1)}, bf16[256,768]{1,0:T(8,128)(2,1)}, u32[]{:S(2)}, u32[]{:S(2)}) collective-permute-start(bf16[256,768]{1,0:T(8,128)(2,1)} %shard_map.93.refs_2_), channel_id=1, source_target_pairs={{0,1},{1,0},{2,3},{3,2},{4,5},{5,4},{6,7},{7,6},{8,9},{9,8},{10,11... | collective-permute-start | bytes 1179656 | tf_op jit(solution)/shard_map/ppermute | solution.py:29
  173.1 16.3 %collective-permute-start.18 = (bf16[8,1536]{1,0:T(8,128)(2,1)S(1)}, bf16[8,1536]{1,0:T(8,128)(2,1)S(1)}, u32[]{:S(2)}, u32[]{:S(2)}) collective-permute-start(bf16[8,1536]{1,0:T(8,128)(2,1)S(1)} %get-tuple-element.31), channel_id=1, source_target_pairs={{0,96},{32,0},{64,32},{96,64},{1,97},{33,1},{65,33},{97,65},{2,98}... | collective-permute-start | bytes 73736 | tf_op jit(solution)/shard_map/ppermute | solution.py:29
  176.3 13.1 %collective-permute-start.20 = (bf16[8,1536]{1,0:T(8,128)(2,1)S(1)}, bf16[8,1536]{1,0:T(8,128)(2,1)S(1)}, u32[]{:S(2)}, u32[]{:S(2)}) collective-permute-start(bf16[8,1536]{1,0:T(8,128)(2,1)S(1)} %get-tuple-element.32), channel_id=1, source_target_pairs={{0,32},{32,64},{64,96},{96,0},{1,33},{33,65},{65,97},{97,1},{2,34}... | collective-permute-start | bytes 73736 | tf_op jit(solution)/shard_map/ppermute | solution.py:29
  182.3 13.4 %collective-permute-start.19 = (bf16[8,1536]{1,0:T(8,128)(2,1)S(1)}, bf16[8,1536]{1,0:T(8,128)(2,1)S(1)}, u32[]{:S(2)}, u32[]{:S(2)}) collective-permute-start(bf16[8,1536]{1,0:T(8,128)(2,1)S(1)} %get-tuple-element.33), channel_id=1, source_target_pairs={{0,64},{32,96},{64,0},{96,32},{1,65},{33,97},{65,1},{97,33},{2,66}... | collective-permute-start | bytes 73736 | tf_op jit(solution)/shard_map/ppermute | solution.py:29
  (8 other events, 24.7 us)

commit v2 on v1

v2 whole, which is shorter than its diff:
```python
import math

import jax
import jax.numpy as jnp
from jax import lax
from jax.experimental import pallas as pl
from jax.experimental.pallas import tpu as pltpu
from jax.sharding import Mesh, PartitionSpec as P

BF, F32 = jnp.bfloat16, jnp.float32
BS = 128
TOK = 512
WT = 1536
HT = 768
NI = WT // BS
NJ = HT // BS
NB = 9
Q = TOK // 8
W1_COLS = 384
W2_COLS = 96
SIZE = {"x": 4, "y": 4, "zh": 4, "zl": 4, "core": 2}
C0 = math.sqrt(2.0 / math.pi)

VM = pl.BlockSpec(memory_space=pltpu.VMEM)
SM = pl.BlockSpec(memory_space=pltpu.SMEM)


def shift(value, axis, step):
    n = SIZE[axis]
    return lax.ppermute(value, axis, [(i, (i + step) % n) for i in range(n)])


def call(body, ins, outs, scratch=(), flops=0, nbytes=0, vmem=16, after=()):
    return pl.pallas_call(
        body,
        out_shape=[jax.ShapeDtypeStruct(s, d) for s, d in outs],
        in_specs=[SM if a.dtype == jnp.int32 else VM for a in ins]
        + [pl.BlockSpec(memory_space=pl.ANY)] * len(after),
        out_specs=[VM] * len(outs),
        scratch_shapes=list(scratch),
        compiler_params=pltpu.CompilerParams(vmem_limit_bytes=vmem << 20),
        cost_estimate=pl.CostEstimate(flops=flops, bytes_accessed=nbytes, transcendentals=0),
    )(*ins, *after)


def w1_pos(where):
    return lax.rem(where // W1_COLS, NI), lax.rem(lax.rem(where, W1_COLS), NJ)


def w2_pos(where):
    return lax.rem(lax.rem(where, W2_COLS), NI), lax.rem(where // W2_COLS, NJ)


def lanes(index):
    return pl.ds(pl.multiple_of(index * BS, BS), BS)


NN = (((1,), (0,)), ((), ()))
NT = (((1,), (1,)), ((), ()))
TN = (((0,), (0,)), ((), ()))


def dot(a, b, dims):
    return lax.dot_general(a, b, dims, preferred_element_type=F32)


def partial_body(pos, dims, pieces, where, ids, *refs):
    core, y = ids[0], ids[2]
    if pieces == 1:
        act, blocks, keep, send, acc = refs
    else:
        parts, (blocks, keep, send, act, acc) = refs[:pieces], refs[pieces:]
        rows = TOK // pieces
        for k, part in enumerate(parts):
            place = lax.rem(y + 4 - k, 4) * rows
            act[pl.ds(pl.multiple_of(place, rows), rows)] = part[...]
    acc[...] = jnp.zeros_like(acc)
    for b in range(NB):
        i, j = pos(where[b])
        acc[j] += dot(act[:, lanes(i)], blocks[b], dims)
    for z in range(4):
        mine = pl.ds(pl.multiple_of((2 * z + core) * Q, Q), Q)
        other = pl.ds(pl.multiple_of((2 * z + 1 - core) * Q, Q), Q)
        for j in range(NJ):
            keep[z * Q : (z + 1) * Q, j * BS : (j + 1) * BS] = acc[j, mine]
            send[z * Q : (z + 1) * Q, j * BS : (j + 1) * BS] = acc[j, other]


def partial_sums(pos, dims, where, ids, parts, blocks):
    half = ((TOK // 2, HT), F32)
    whole = [((TOK, WT), BF)] if len(parts) > 1 else []
    return call(
        lambda *refs: partial_body(pos, dims, len(parts), *refs),
        (where, ids, *parts, blocks),
        [half, half] + whole,
        [pltpu.VMEM((NJ, TOK, BS), F32)],
        flops=2 * NB * TOK * BS * BS * 4,
        nbytes=3 << 20,
    )


def split_body(ids, keep_h, got_h, keep_a, got_a, mine_h, mine_a, s1, s2, s3):
    zl = ids[1]
    own = pl.ds(pl.multiple_of(zl * Q, Q), Q)
    mine_h[...] = keep_h[own] + got_h[own]
    mine_a[...] = keep_a[own] + got_a[own]
    for k, ref in ((1, s1), (2, s2), (3, s3)):
        part = pl.ds(pl.multiple_of(lax.rem(zl + k, 4) * Q, Q), Q)
        ref[:, :HT] = (keep_h[part] + got_h[part]).astype(BF)
        ref[:, HT:] = (keep_a[part] + got_a[part]).astype(BF)


def gelu_body(h0, a0, r1, r2, r3, activated, hidden_grad):
    v, g = h0[...], a0[...]
    for ref in (r1, r2, r3):
        v = v + ref[:, :HT].astype(F32)
        g = g + ref[:, HT:].astype(F32)
    t = jnp.tanh(C0 * (v + 0.044715 * v * v * v))
    derive = C0 * (1.0 + 3.0 * 0.044715 * v * v)
    activated[...] = (0.5 * v * (1.0 + t)).astype(BF)
    slope = 0.5 * (1.0 + t) + 0.5 * v * (1.0 - t * t) * derive
    hidden_grad[...] = (g * slope).astype(BF)


def input_grad_body(where, hg, blocks, out, acc):
    acc[...] = jnp.zeros_like(acc)
    for b in range(NB):
        i, j = w1_pos(where[b])
        acc[i] += dot(hg[:, lanes(j)], blocks[b], NT)
    for i in range(NI):
        out[:, i * BS : (i + 1) * BS] = acc[i].astype(BF)


def input_grad_partial(where, hg, blocks):
    (out,) = call(
        input_grad_body,
        (where, hg, blocks),
        [((TOK, WT), BF)],
        [pltpu.VMEM((NI, TOK, BS), F32)],
        flops=2 * NB * TOK * BS * BS * 4,
        nbytes=4 << 20,
    )
    return out


def block_grad_body(pos, hidden_left, where, hid, act, out):
    for b in range(NB):
        i, j = pos(where[b])
        left, right = act[:, lanes(i)], hid[:, lanes(j)]
        if hidden_left:
            left, right = right, left
        out[b] = dot(left, right, TN)


def block_grads(pos, hidden_left, where, hid, act):
    (out,) = call(
        lambda *refs: block_grad_body(pos, hidden_left, *refs),
        (where, hid, act),
        [((NB, BS, BS), F32)],
        flops=2 * NB * TOK * BS * BS * 4,
        nbytes=4 << 20,
    )
    return out


def sum_body(parts, *refs):
    total = parts[0].astype(F32)
    for k in range(1, 16):
        total = total + parts[k].astype(F32)
    refs[-1][...] = total.astype(BF)


def row_reduce(partial, after):
    parts = lax.all_to_all(partial, ("y", "x"), 0, 0, tiled=True)
    (mine,) = call(
        sum_body,
        (parts.reshape(16, 32, WT),),
        [((32, WT), BF)],
        flops=1 << 20,
        nbytes=2 << 20,
        after=after,
    )
    last = lax.all_to_all(mine, "zh", 0, 0, tiled=True)
    return jnp.sum(last.reshape(4, 8, WT).astype(F32), axis=0).astype(BF)


def shards(inputs, cotangent, w1_blocks, w1_where, w2_blocks, w2_where):
    ids = jnp.stack([lax.axis_index(a) for a in ("core", "zl", "y")]).astype(jnp.int32)
    near = lax.all_gather(jnp.concatenate([inputs, cotangent], axis=0), "zh", axis=0)
    near_inputs = near[:, :8].reshape(32, WT)
    near_cotangent = near[:, 8:].reshape(32, WT)
    sixteen = jnp.broadcast_to(near_inputs[None], (16, 32, WT)).reshape(TOK, WT)
    whole_inputs = lax.all_to_all(sixteen, ("y", "x"), 0, 0, tiled=True)
    along = lax.all_gather(near_cotangent, "x", axis=0, tiled=True)
    quarters = [along] + [shift(along, "y", k) for k in (1, 2, 3)]
    keep_h, send_h = partial_sums(w1_pos, NN, w1_where, ids, [whole_inputs], w1_blocks)
    got_h = shift(send_h, "core", 1)
    keep_a, send_a, whole_cotangent = partial_sums(w2_pos, NT, w2_where, ids, quarters, w2_blocks)
    got_a = shift(send_a, "core", 1)
    mine_h, mine_a, s1, s2, s3 = call(
        split_body,
        (ids, keep_h, got_h, keep_a, got_a),
        [((Q, HT), F32)] * 2 + [((Q, WT), BF)] * 3,
        flops=1 << 20,
        nbytes=2 << 20,
    )
    activated, hidden_grad = call(
        gelu_body,
        (mine_h, mine_a, shift(s1, "zl", 1), shift(s2, "zl", 2), shift(s3, "zl", 3)),
        [((Q, HT), BF)] * 2,
        flops=1 << 22,
        nbytes=1 << 20,
    )
    whole_hg = lax.all_gather(hidden_grad, ("zl", "core"), axis=0, tiled=True)
    whole_av = lax.all_gather(activated, ("zl", "core"), axis=0, tiled=True)
    partial = input_grad_partial(w1_where, whole_hg, w1_blocks)
    w1_grad = block_grads(w1_pos, False, w1_where, whole_hg, whole_inputs)
    w2_grad = block_grads(w2_pos, True, w2_where, whole_av, whole_cotangent)
    input_grad = row_reduce(partial, (whole_av,))
    return input_grad, w1_grad, w2_grad


def solution(mesh):
    fine = Mesh(mesh.devices.reshape(4, 4, 4, 4, 2), ("x", "zh", "y", "zl", "core"))
    row, col = ("x", "zh", "y"), ("zl", "core")
    both = row + col
    return jax.shard_map(
        shards,
        mesh=fine,
        in_specs=(P(row, col), P(row, col), P(both, None, None), P(both), P(both, None, None), P(both)),
        out_specs=(P(row, col), P(both, None, None), P(both, None, None)),
        check_vma=False,
    )
```

time: 198 us -> 195 us (0.985)
  starting transfers between devices: 129 us -> 42.2 us
  blocking collectives: 0 us -> 82.8 us
  waiting for transfers between devices: 41.6 us -> 46 us
    ppermute x25 -> x8, starting transfers between devices: 112 us -> 24.7 us  [shift(): return lax.ppermute(value, axis, [(i, (i + step) % n) for i in range(n)])]
    all_gather x0 -> x4, blocking collectives: none -> 82.8 us  [the longest x1 25.2 us: shards(): along = lax.all_gather(near_cotangent, 'x', axis=0, tiled=True)]
    all_to_all x3, waiting for transfers between devices: 10 us -> 19.6 us  [the longest x1 10.8 us: row_reduce(): parts = lax.all_to_all(partial, ('y', 'x'), 0, 0, tiled=True)]
    ppermute x25 -> x8, waiting for transfers between devices: 31.6 us -> 26.4 us  [shift(): return lax.ppermute(value, axis, [(i, (i + step) % n) for i in range(n)])]
    unnamed x24 -> x22, local copies, waits for them, and re-layouts: 4.6 us -> 6.81 us
    pallas_call x10 -> x8, Pallas kernels: 13.8 us -> 11.9 us  [call(): pl.pallas_call(body, out_shape=[jax.ShapeDtypeStruct(s, d) for s, d in ou...]
  transfers between devices with their start and end apart: 28 -> 11, of which waited for: 11 -> 8; matrix products, arithmetic and copies ran while one was open for 1% -> 0% of each run, Pallas kernels for 5% -> 4%
where the time goes in v2:
time: 195 us; the launch traced here: 193 us
  blocking collectives  82.8 us (42%)
  waiting for transfers between devices  46 us (24%)
  starting transfers between devices  42.2 us (22%)
  Pallas kernels  11.9 us (6%)
  local copies, waits for them, and re-layouts  8.13 us (4%)
    ppermute x8, waiting for transfers between devices, shift(): return lax.ppermute(value, axis, [(i, (i + step) % n) for i in range(n)])  26.4 us
    all_gather x1, blocking collectives, shards(): along = lax.all_gather(near_cotangent, 'x', axis=0, tiled=True)  25.2 us
    ppermute x8, starting transfers between devices, shift(): return lax.ppermute(value, axis, [(i, (i + step) % n) for i in range(n)])  24.7 us
    all_gather x1, blocking collectives, shards(): lax.all_gather(jnp.concatenate([inputs, cotangent], axis=0), 'zh', axis=0)  24.5 us
    all_gather x1, blocking collectives, shards(): whole_hg = lax.all_gather(hidden_grad, ('zl', 'core'), axis=0, tiled=True)  17.5 us
    all_gather x1, blocking collectives, shards(): whole_av = lax.all_gather(activated, ('zl', 'core'), axis=0, tiled=True)  15.6 us
    pallas_call x8, Pallas kernels, call(): pl.pallas_call(body, out_shape=[jax.ShapeDtypeStruct(s, d) for s, d in ou...  11.9 us
    all_to_all x1, waiting for transfers between devices, row_reduce(): parts = lax.all_to_all(partial, ('y', 'x'), 0, 0, tiled=True)  10.8 us
  transfers between devices with their start and end apart: 11, of which 8 were waited for; matrix products, arithmetic and copies ran while one was open for 0% of the time, Pallas kernels for 4%

profile of v2, /device:TPU:1, one launch (start us, length us, event | category | flops | bytes accessed | tf_op | source)
XLA Modules:
  0.0 193.5 jit_solution(13141816725176917205)
XLA Ops:
  1.4 24.5 %all-gather = bf16[64,1536]{1,0:T(8,128)(2,1)S(1)} all-gather(bf16[16,1536]{1,0:T(8,128)(2,1)S(1)} %pad_maximum_fusion), channel_id=2, replica_groups=mesh['x'=4,'zh'=4,'y'=4,'zl'=4,'core'=2] {'zh'}, dimensions={0}, use_global_device_ids=true | all-gather | bytes 245760 | tf_op jit(solution)/shard_map/all_gather | solution.py:189
  25.9 1.3 broadcast_in_dim.8
  27.2 6.9 %all-to-all-start = ((bf16[16,32,1536]{2,1,0:T(8,128)(2,1)}), bf16[16,32,1536]{2,1,0:T(8,128)(2,1)S(1)}, u32[]{:S(2)}, u32[]{:S(2)}) async-start(bf16[16,32,1536]{2,1,0:T(8,128)(2,1)} %broadcast_in_dim.8), calls=%async_computation | async-start | bytes 3145728 | tf_op jit(solution)/shard_map/all_to_all | solution.py:193
  34.2 25.2 %all_gather.17.refs_2_ = bf16[128,1536]{1,0:T(8,128)(2,1)S(1)} all-gather(bf16[32,1536]{1,0:T(8,128)(2,1)S(1)} %get-tuple-element.27), channel_id=1, replica_groups=mesh['x'=4,'zh'=4,'y'=4,'zl'=4,'core'=2] {'x'}, dimensions={0}, use_global_device_ids=true | all-gather | bytes 491520 | tf_op jit(solution)/shard_map/all_gather | solution.py:194
  59.4 3.6 %collective-permute-start.3 = (bf16[128,1536]{1,0:T(8,128)(2,1)S(1)}, bf16[128,1536]{1,0:T(8,128)(2,1)S(1)}, u32[]{:S(2)}, u32[]{:S(2)}) collective-permute-start(bf16[128,1536]{1,0:T(8,128)(2,1)S(1)} %all_gather.17.refs_2_), channel_id=1, source_target_pairs={{0,24},{8,0},{16,8},{24,16},{1,25},{9,1},{17,9},{25,17},{2,26},{10... | collective-permute-start | bytes 1179656 | tf_op jit(solution)/shard_map/ppermute | solution.py:30
  62.9 2.5 %collective-permute-start.2 = (bf16[128,1536]{1,0:T(8,128)(2,1)S(1)}, bf16[128,1536]{1,0:T(8,128)(2,1)S(1)}, u32[]{:S(2)}, u32[]{:S(2)}) collective-permute-start(bf16[128,1536]{1,0:T(8,128)(2,1)S(1)} %all_gather.17.refs_2_), channel_id=1, source_target_pairs={{0,16},{8,24},{16,0},{24,8},{1,17},{9,25},{17,1},{25,9},{2,18},{10... | collective-permute-start | bytes 1179656 | tf_op jit(solution)/shard_map/ppermute | solution.py:30
  65.4 2.8 %collective-permute-start.1 = (bf16[128,1536]{1,0:T(8,128)(2,1)S(1)}, bf16[128,1536]{1,0:T(8,128)(2,1)S(1)}, u32[]{:S(2)}, u32[]{:S(2)}) collective-permute-start(bf16[128,1536]{1,0:T(8,128)(2,1)S(1)} %all_gather.17.refs_2_), channel_id=1, source_target_pairs={{0,8},{8,16},{16,24},{24,0},{1,9},{9,17},{17,25},{25,1},{2,10},{10... | collective-permute-start | bytes 1179656 | tf_op jit(solution)/shard_map/ppermute | solution.py:30
  68.8 4.3 %collective-permute-done.2.refs_4_ = bf16[128,1536]{1,0:T(8,128)(2,1)S(1)} collective-permute-done((bf16[128,1536]{1,0:T(8,128)(2,1)S(1)}, bf16[128,1536]{1,0:T(8,128)(2,1)S(1)}, u32[]{:S(2)}, u32[]{:S(2)}) %collective-permute-start.2) | collective-permute-done | bytes 393248 | tf_op jit(solution)/shard_map/ppermute | solution.py:30
  73.8 9.4 %collective-permute-done.1.refs_3_ = bf16[128,1536]{1,0:T(8,128)(2,1)S(1)} collective-permute-done((bf16[128,1536]{1,0:T(8,128)(2,1)S(1)}, bf16[128,1536]{1,0:T(8,128)(2,1)S(1)}, u32[]{:S(2)}, u32[]{:S(2)}) %collective-permute-start.1) | collective-permute-done | bytes 393248 | tf_op jit(solution)/shard_map/ppermute | solution.py:30
  84.0 1.0 copy-done.7
  87.0 2.3 %shard_map.86 = (f32[256,768]{1,0:T(8,128)S(1)}, f32[256,768]{1,0:T(8,128)}, bf16[512,1536]{1,0:T(8,128)(2,1)S(1)}) custom-call(s32[9]{0:T(128)S(1)} %copy-done.5, s32[3]{0:T(128)S(1)} %pad_add_fusion.refs_1_.ids, bf16[128,1536]{1,0:T(8,128)(2,1)S(1)} %all_gather.17.refs_2_, bf16[128,1536]{1,0:T(8,128)(2,1)S(1)} %copy-done.9, ...), custom_call_target="tpu_custom_call" | custom-call | flops 603979776 | bytes 3145728 | tf_op jit(solution)/shard_map/pallas_call | solution.py:34
  89.2 1.2 copy-done.1
  90.4 5.0 %collective-permute-start.4 = (f32[256,768]{1,0:T(8,128)}, f32[256,768]{1,0:T(8,128)S(1)}, u32[]{:S(2)}, u32[]{:S(2)}) collective-permute-start(f32[256,768]{1,0:T(8,128)} %get-tuple-element.18), channel_id=1, source_target_pairs={{0,1},{1,0},{2,3},{3,2},{4,5},{5,4},{6,7},{7,6},{8,9},{9,8},{10,11... | collective-permute-start | bytes 2359304 | tf_op jit(solution)/shard_map/ppermute | solution.py:30
  95.4 1.2 shard_map.85
  96.6 1.9 collective-permute-start
  98.5 2.2 %collective-permute-done.got_h = f32[256,768]{1,0:T(8,128)S(1)} collective-permute-done((f32[256,768]{1,0:T(8,128)S(1)}, f32[256,768]{1,0:T(8,128)S(1)}, u32[]{:S(2)}, u32[]{:S(2)}) %collective-permute-start) | collective-permute-done | bytes 786464 | tf_op jit(solution)/shard_map/ppermute | solution.py:30
  101.4 2.7 %collective-permute-start.5 = (bf16[64,1536]{1,0:T(8,128)(2,1)S(1)}, bf16[64,1536]{1,0:T(8,128)(2,1)S(1)}, u32[]{:S(2)}, u32[]{:S(2)}) collective-permute-start(bf16[64,1536]{1,0:T(8,128)(2,1)S(1)} %get-tuple-element.21), channel_id=1, source_target_pairs={{0,2},{2,4},{4,6},{6,0},{1,3},{3,5},{5,7},{7,1},{8,10},{10,12},{12... | collective-permute-start | bytes 589832 | tf_op jit(solution)/shard_map/ppermute | solution.py:30
  104.2 3.0 %collective-permute-start.6 = (bf16[64,1536]{1,0:T(8,128)(2,1)S(1)}, bf16[64,1536]{1,0:T(8,128)(2,1)S(1)}, u32[]{:S(2)}, u32[]{:S(2)}) collective-permute-start(bf16[64,1536]{1,0:T(8,128)(2,1)S(1)} %get-tuple-element.22), channel_id=1, source_target_pairs={{0,4},{2,6},{4,0},{6,2},{1,5},{3,7},{5,1},{7,3},{8,12},{10,14},{12... | collective-permute-start | bytes 589832 | tf_op jit(solution)/shard_map/ppermute | solution.py:30
  107.2 3.3 %collective-permute-start.7 = (bf16[64,1536]{1,0:T(8,128)(2,1)S(1)}, bf16[64,1536]{1,0:T(8,128)(2,1)S(1)}, u32[]{:S(2)}, u32[]{:S(2)}) collective-permute-start(bf16[64,1536]{1,0:T(8,128)(2,1)S(1)} %get-tuple-element.23), channel_id=1, source_target_pairs={{0,6},{2,0},{4,2},{6,4},{1,7},{3,1},{5,3},{7,5},{8,14},{10,8},{12,... | collective-permute-start | bytes 589832 | tf_op jit(solution)/shard_map/ppermute | solution.py:30
  110.5 1.1 collective-permute-done.5.r1
  111.5 8.9 %collective-permute-done.6.r2 = bf16[64,1536]{1,0:T(8,128)(2,1)S(1)} collective-permute-done((bf16[64,1536]{1,0:T(8,128)(2,1)S(1)}, bf16[64,1536]{1,0:T(8,128)(2,1)S(1)}, u32[]{:S(2)}, u32[]{:S(2)}) %collective-permute-start.6) | collective-permute-done | bytes 196640 | tf_op jit(solution)/shard_map/ppermute | solution.py:30
  120.7 17.5 %all_gather.18.hg.refs_1_ = bf16[512,768]{1,0:T(8,128)(2,1)S(1)} all-gather(bf16[64,768]{1,0:T(8,128)(2,1)S(1)} %get-tuple-element.24), channel_id=1, replica_groups=mesh['x'=4,'zh'=4,'y'=4,'zl'=4,'core'=2] {'zl','core'}, dimensions={0}, use_global_device_ids=true | all-gather | bytes 884736 | tf_op jit(solution)/shard_map/all_gather | solution.py:214
  138.1 1.4 shard_map.89
  139.6 1.2 copy-done
  140.8 4.4 %all-to-all-start.1 = ((bf16[16,32,1536]{2,1,0:T(8,128)(2,1)}), bf16[16,32,1536]{2,1,0:T(8,128)(2,1)}, u32[]{:S(2)}, u32[]{:S(2)}) async-start(bf16[16,32,1536]{2,1,0:T(8,128)(2,1)} %bitcast.13), calls=%async_computation.1 | async-start | bytes 3145728 | tf_op jit(solution)/shard_map/all_to_all | solution.py:174
  145.2 15.6 %all_gather.19.refs_0_.refs_1_ = bf16[512,768]{1,0:T(8,128)(2,1)S(1)} all-gather(bf16[64,768]{1,0:T(8,128)(2,1)S(1)} %get-tuple-element.25), channel_id=1, replica_groups=mesh['x'=4,'zh'=4,'y'=4,'zl'=4,'core'=2] {'zl','core'}, dimensions={0}, use_global_device_ids=true | all-gather | bytes 884736 | tf_op jit(solution)/shard_map/all_gather | solution.py:215
  160.8 10.8 %all-to-all-done.1.parts = bf16[16,32,1536]{2,1,0:T(8,128)(2,1)} async-done(((bf16[16,32,1536]{2,1,0:T(8,128)(2,1)}), bf16[16,32,1536]{2,1,0:T(8,128)(2,1)}, u32[]{:S(2)}, u32[]{:S(2)}) %all-to-all-start.1) | async-done | bytes 1572896 | tf_op jit(solution)/shard_map/all_to_all | solution.py:174
  171.6 2.2 %shard_map.90 = bf16[32,1536]{1,0:T(8,128)(2,1)} custom-call(bf16[16,32,1536]{2,1,0:T(8,128)(2,1)} %all-to-all-done.1.parts, bf16[512,768]{1,0:T(8,128)(2,1)S(1)} %all_gather.19.refs_0_.refs_1_), custom_call_target="tpu_custom_call" | custom-call | flops 1048576 | bytes 2097152 | tf_op jit(solution)/shard_map/pallas_call | solution.py:34
  173.8 6.3 %all-to-all-start.2 = ((bf16[4,8,1536]{2,1,0:T(8,128)(2,1)}), bf16[4,8,1536]{2,1,0:T(8,128)(2,1)S(1)}, u32[]{:S(2)}, u32[]{:S(2)}) async-start(bf16[4,8,1536]{2,1,0:T(8,128)(2,1)} %bitcast.8), calls=%async_computation.2 | async-start | bytes 196608 | tf_op jit(solution)/shard_map/all_to_all | solution.py:183
  180.1 1.9 %shard_map.91 = f32[9,128,128]{2,1,0:T(8,128)} custom-call(s32[9]{0:T(128)S(1)} %copy-done.4, bf16[512,768]{1,0:T(8,128)(2,1)S(1)} %all_gather.18.hg.refs_1_, bf16[512,1536]{1,0:T(8,128)(2,1)S(1)} %bitcast.12), custom_call_target="tpu_custom_call" | custom-call | flops 603979776 | bytes 4194304 | tf_op jit(solution)/shard_map/pallas_call | solution.py:34
  182.1 2.0 %shard_map.92 = f32[9,128,128]{2,1,0:T(8,128)} custom-call(s32[9]{0:T(128)S(1)} %copy-done.5, bf16[512,768]{1,0:T(8,128)(2,1)S(1)} %all_gather.19.refs_0_.refs_1_, bf16[512,1536]{1,0:T(8,128)(2,1)S(1)} %copy-done.2), custom_call_target="tpu_custom_call" | custom-call | flops 603979776 | bytes 4194304 | tf_op jit(solution)/shard_map/pallas_call | solution.py:34
  184.0 8.8 %all-to-all-done.2 = bf16[4,8,1536]{2,1,0:T(8,128)(2,1)S(1)} async-done(((bf16[4,8,1536]{2,1,0:T(8,128)(2,1)}), bf16[4,8,1536]{2,1,0:T(8,128)(2,1)S(1)}, u32[]{:S(2)}, u32[]{:S(2)}) %all-to-all-start.2) | async-done | bytes 98336 | tf_op jit(solution)/shard_map/all_to_all | solution.py:183
  (29 shorter events, 6.4 us)
Async XLA Ops:
  27.2 56.8 %copy-start.5 = (s32[9]{0:T(128)S(1)}, s32[9]{0:T(128)}, u32[]{:S(2)}) copy-start(s32[9]{0:T(128)} %refs_0_.7) | copy-start | bytes 112
  27.2 68.1 %all-to-all-start = ((bf16[16,32,1536]{2,1,0:T(8,128)(2,1)}), bf16[16,32,1536]{2,1,0:T(8,128)(2,1)S(1)}, u32[]{:S(2)}, u32[]{:S(2)}) async-start(bf16[16,32,1536]{2,1,0:T(8,128)(2,1)} %broadcast_in_dim.8), calls=%async_computation | async-start | bytes 3145728 | tf_op jit(solution)/shard_map/all_to_all | solution.py:193
  34.1 61.2 %copy-start.3 = (bf16[9,128,128]{2,1,0:T(8,128)(2,1)S(1)}, bf16[9,128,128]{2,1,0:T(8,128)(2,1)}, u32[]{:S(2)}) copy-start(bf16[9,128,128]{2,1,0:T(8,128)(2,1)} %blocks.1) | copy-start | bytes 884740
  34.2 61.2 %copy-start.4 = (s32[9]{0:T(128)S(1)}, s32[9]{0:T(128)}, u32[]{:S(2)}) copy-start(s32[9]{0:T(128)} %refs_0_.6) | copy-start | bytes 112
  59.4 9.4 %collective-permute-start.3 = (bf16[128,1536]{1,0:T(8,128)(2,1)S(1)}, bf16[128,1536]{1,0:T(8,128)(2,1)S(1)}, u32[]{:S(2)}, u32[]{:S(2)}) collective-permute-start(bf16[128,1536]{1,0:T(8,128)(2,1)S(1)} %all_gather.17.refs_2_), channel_id=1, source_target_pairs={{0,24},{8,0},{16,8},{24,16},{1,25},{9,1},{17,9},{25,17},{2,26},{10... | collective-permute-start | bytes 1179656 | tf_op jit(solution)/shard_map/ppermute | solution.py:30
  62.9 10.1 %collective-permute-start.2 = (bf16[128,1536]{1,0:T(8,128)(2,1)S(1)}, bf16[128,1536]{1,0:T(8,128)(2,1)S(1)}, u32[]{:S(2)}, u32[]{:S(2)}) collective-permute-start(bf16[128,1536]{1,0:T(8,128)(2,1)S(1)} %all_gather.17.refs_2_), channel_id=1, source_target_pairs={{0,16},{8,24},{16,0},{24,8},{1,17},{9,25},{17,1},{25,9},{2,18},{10... | collective-permute-start | bytes 1179656 | tf_op jit(solution)/shard_map/ppermute | solution.py:30
  65.4 17.8 %collective-permute-start.1 = (bf16[128,1536]{1,0:T(8,128)(2,1)S(1)}, bf16[128,1536]{1,0:T(8,128)(2,1)S(1)}, u32[]{:S(2)}, u32[]{:S(2)}) collective-permute-start(bf16[128,1536]{1,0:T(8,128)(2,1)S(1)} %all_gather.17.refs_2_), channel_id=1, source_target_pairs={{0,8},{8,16},{16,24},{24,0},{1,9},{9,17},{17,25},{25,1},{2,10},{10... | collective-permute-start | bytes 1179656 | tf_op jit(solution)/shard_map/ppermute | solution.py:30
  73.1 0.7 copy-start.6
  83.2 0.7 copy-start.8
  84.0 1.0 copy-start.7
  85.0 1.0 copy-start.9
  86.0 1.0 copy-start.10
  89.2 1.2 copy-start.1
  90.4 8.1 %collective-permute-start.4 = (f32[256,768]{1,0:T(8,128)}, f32[256,768]{1,0:T(8,128)S(1)}, u32[]{:S(2)}, u32[]{:S(2)}) collective-permute-start(f32[256,768]{1,0:T(8,128)} %get-tuple-element.18), channel_id=1, source_target_pairs={{0,1},{1,0},{2,3},{3,2},{4,5},{5,4},{6,7},{7,6},{8,9},{9,8},{10,11... | collective-permute-start | bytes 2359304 | tf_op jit(solution)/shard_map/ppermute | solution.py:30
  96.6 4.2 %collective-permute-start = (f32[256,768]{1,0:T(8,128)S(1)}, f32[256,768]{1,0:T(8,128)S(1)}, u32[]{:S(2)}, u32[]{:S(2)}) collective-permute-start(f32[256,768]{1,0:T(8,128)S(1)} %get-tuple-element.16), channel_id=1, source_target_pairs={{0,1},{1,0},{2,3},{3,2},{4,5},{5,4},{6,7},{7,6},{8,9},{9,8},{10,11... | collective-permute-start | bytes 2359304 | tf_op jit(solution)/shard_map/ppermute | solution.py:30
  101.4 10.1 %collective-permute-start.5 = (bf16[64,1536]{1,0:T(8,128)(2,1)S(1)}, bf16[64,1536]{1,0:T(8,128)(2,1)S(1)}, u32[]{:S(2)}, u32[]{:S(2)}) collective-permute-start(bf16[64,1536]{1,0:T(8,128)(2,1)S(1)} %get-tuple-element.21), channel_id=1, source_target_pairs={{0,2},{2,4},{4,6},{6,0},{1,3},{3,5},{5,7},{7,1},{8,10},{10,12},{12... | collective-permute-start | bytes 589832 | tf_op jit(solution)/shard_map/ppermute | solution.py:30
  104.2 16.2 %collective-permute-start.6 = (bf16[64,1536]{1,0:T(8,128)(2,1)S(1)}, bf16[64,1536]{1,0:T(8,128)(2,1)S(1)}, u32[]{:S(2)}, u32[]{:S(2)}) collective-permute-start(bf16[64,1536]{1,0:T(8,128)(2,1)S(1)} %get-tuple-element.22), channel_id=1, source_target_pairs={{0,4},{2,6},{4,0},{6,2},{1,5},{3,7},{5,1},{7,3},{8,12},{10,14},{12... | collective-permute-start | bytes 589832 | tf_op jit(solution)/shard_map/ppermute | solution.py:30
  107.2 13.3 %collective-permute-start.7 = (bf16[64,1536]{1,0:T(8,128)(2,1)S(1)}, bf16[64,1536]{1,0:T(8,128)(2,1)S(1)}, u32[]{:S(2)}, u32[]{:S(2)}) collective-permute-start(bf16[64,1536]{1,0:T(8,128)(2,1)S(1)} %get-tuple-element.23), channel_id=1, source_target_pairs={{0,6},{2,0},{4,2},{6,4},{1,7},{3,1},{5,3},{7,5},{8,14},{10,8},{12,... | collective-permute-start | bytes 589832 | tf_op jit(solution)/shard_map/ppermute | solution.py:30
  139.6 1.2 copy-start
  140.8 30.8 %all-to-all-start.1 = ((bf16[16,32,1536]{2,1,0:T(8,128)(2,1)}), bf16[16,32,1536]{2,1,0:T(8,128)(2,1)}, u32[]{:S(2)}, u32[]{:S(2)}) async-start(bf16[16,32,1536]{2,1,0:T(8,128)(2,1)} %bitcast.13), calls=%async_computation.1 | async-start | bytes 3145728 | tf_op jit(solution)/shard_map/all_to_all | solution.py:174
  173.8 19.0 %all-to-all-start.2 = ((bf16[4,8,1536]{2,1,0:T(8,128)(2,1)}), bf16[4,8,1536]{2,1,0:T(8,128)(2,1)S(1)}, u32[]{:S(2)}, u32[]{:S(2)}) async-start(bf16[4,8,1536]{2,1,0:T(8,128)(2,1)} %bitcast.8), calls=%async_computation.2 | async-start | bytes 196608 | tf_op jit(solution)/shard_map/all_to_all | solution.py:183
  180.1 1.9 %copy-start.2 = (bf16[512,1536]{1,0:T(8,128)(2,1)S(1)}, bf16[512,1536]{1,0:T(8,128)(2,1)}, u32[]{:S(2)}) copy-start(bf16[512,1536]{1,0:T(8,128)(2,1)} %copy-done.1) | copy-start | bytes 4718596

commit v3 on v2

--- a/solution.py
+++ b/solution.py
@@ -64,54 +64,37 @@
     return lax.dot_general(a, b, dims, preferred_element_type=F32)
 
 
-def partial_body(pos, dims, pieces, where, ids, *refs):
-    core, y = ids[0], ids[2]
-    if pieces == 1:
-        act, blocks, keep, send, acc = refs
-    else:
-        parts, (blocks, keep, send, act, acc) = refs[:pieces], refs[pieces:]
-        rows = TOK // pieces
-        for k, part in enumerate(parts):
-            place = lax.rem(y + 4 - k, 4) * rows
-            act[pl.ds(pl.multiple_of(place, rows), rows)] = part[...]
+def rows_of(parts, first, index):
+    return parts[:, first : first + 32, lanes(index)].reshape(TOK, BS)
+
+
+def partial_body(where1, where2, ids, parts, blocks1, blocks2, keep, send, acc):
+    core = ids[0]
     acc[...] = jnp.zeros_like(acc)
     for b in range(NB):
-        i, j = pos(where[b])
-        acc[j] += dot(act[:, lanes(i)], blocks[b], dims)
+        i, j = w1_pos(where1[b])
+        acc[j] += dot(rows_of(parts, 0, i), blocks1[b], NN)
+        i, j = w2_pos(where2[b])
+        acc[NJ + j] += dot(rows_of(parts, 32, i), blocks2[b], NT)
     for z in range(4):
         mine = pl.ds(pl.multiple_of((2 * z + core) * Q, Q), Q)
         other = pl.ds(pl.multiple_of((2 * z + 1 - core) * Q, Q), Q)
-        for j in range(NJ):
+        for j in range(2 * NJ):
             keep[z * Q : (z + 1) * Q, j * BS : (j + 1) * BS] = acc[j, mine]
             send[z * Q : (z + 1) * Q, j * BS : (j + 1) * BS] = acc[j, other]
 
 
-def partial_sums(pos, dims, where, ids, parts, blocks):
-    half = ((TOK // 2, HT), F32)
-    whole = [((TOK, WT), BF)] if len(parts) > 1 else []
-    return call(
-        lambda *refs: partial_body(pos, dims, len(parts), *refs),
-        (where, ids, *parts, blocks),
-        [half, half] + whole,
-        [pltpu.VMEM((NJ, TOK, BS), F32)],
-        flops=2 * NB * TOK * BS * BS * 4,
-        nbytes=3 << 20,
-    )
-
-
-def split_body(ids, keep_h, got_h, keep_a, got_a, mine_h, mine_a, s1, s2, s3):
+def split_body(ids, keep, got, mine, s1, s2, s3):
     zl = ids[1]
     own = pl.ds(pl.multiple_of(zl * Q, Q), Q)
-    mine_h[...] = keep_h[own] + got_h[own]
-    mine_a[...] = keep_a[own] + got_a[own]
+    mine[...] = keep[own] + got[own]
     for k, ref in ((1, s1), (2, s2), (3, s3)):
         part = pl.ds(pl.multiple_of(lax.rem(zl + k, 4) * Q, Q), Q)
-        ref[:, :HT] = (keep_h[part] + got_h[part]).astype(BF)
-        ref[:, HT:] = (keep_a[part] + got_a[part]).astype(BF)
-
-
-def gelu_body(h0, a0, r1, r2, r3, activated, hidden_grad):
-    v, g = h0[...], a0[...]
+        ref[...] = (keep[part] + got[part]).astype(BF)
+
+
+def gelu_body(own, r1, r2, r3, activated, hidden_grad):
+    v, g = own[:, :HT], own[:, HT:]
     for ref in (r1, r2, r3):
         v = v + ref[:, :HT].astype(F32)
         g = g + ref[:, HT:].astype(F32)
@@ -143,19 +126,19 @@
     return out
 
 
-def block_grad_body(pos, hidden_left, where, hid, act, out):
+def block_grad_body(pos, first, where, hid, parts, out):
     for b in range(NB):
         i, j = pos(where[b])
-        left, right = act[:, lanes(i)], hid[:, lanes(j)]
-        if hidden_left:
+        left, right = rows_of(parts, first, i), hid[:, lanes(j)]
+        if first:
             left, right = right, left
         out[b] = dot(left, right, TN)
 
 
-def block_grads(pos, hidden_left, where, hid, act):
+def block_grads(pos, first, where, hid, parts):
     (out,) = call(
-        lambda *refs: block_grad_body(pos, hidden_left, *refs),
-        (where, hid, act),
+        lambda *refs: block_grad_body(pos, first, *refs),
+        (where, hid, parts),
         [((NB, BS, BS), F32)],
         flops=2 * NB * TOK * BS * BS * 4,
         nbytes=4 << 20,
@@ -185,28 +168,30 @@
 
 
 def shards(inputs, cotangent, w1_blocks, w1_where, w2_blocks, w2_where):
-    ids = jnp.stack([lax.axis_index(a) for a in ("core", "zl", "y")]).astype(jnp.int32)
+    ids = jnp.stack([lax.axis_index(a) for a in ("core", "zl")]).astype(jnp.int32)
     near = lax.all_gather(jnp.concatenate([inputs, cotangent], axis=0), "zh", axis=0)
-    near_inputs = near[:, :8].reshape(32, WT)
-    near_cotangent = near[:, 8:].reshape(32, WT)
-    sixteen = jnp.broadcast_to(near_inputs[None], (16, 32, WT)).reshape(TOK, WT)
-    whole_inputs = lax.all_to_all(sixteen, ("y", "x"), 0, 0, tiled=True)
-    along = lax.all_gather(near_cotangent, "x", axis=0, tiled=True)
-    quarters = [along] + [shift(along, "y", k) for k in (1, 2, 3)]
-    keep_h, send_h = partial_sums(w1_pos, NN, w1_where, ids, [whole_inputs], w1_blocks)
-    got_h = shift(send_h, "core", 1)
-    keep_a, send_a, whole_cotangent = partial_sums(w2_pos, NT, w2_where, ids, quarters, w2_blocks)
-    got_a = shift(send_a, "core", 1)
-    mine_h, mine_a, s1, s2, s3 = call(
+    near = near.reshape(4, 2, 8, WT).swapaxes(0, 1).reshape(64, WT)
+    sixteen = jnp.broadcast_to(near[None], (16, 64, WT))
+    parts = lax.all_to_all(sixteen, ("y", "x"), 0, 0, tiled=True)
+    keep, send = call(
+        partial_body,
+        (w1_where, w2_where, ids, parts, w1_blocks, w2_blocks),
+        [((TOK // 2, WT), F32)] * 2,
+        [pltpu.VMEM((2 * NJ, TOK, BS), F32)],
+        flops=2 * NB * TOK * BS * BS * 8,
+        nbytes=6 << 20,
+        vmem=24,
+    )
+    mine, s1, s2, s3 = call(
         split_body,
-        (ids, keep_h, got_h, keep_a, got_a),
-        [((Q, HT), F32)] * 2 + [((Q, WT), BF)] * 3,
+        (ids, keep, shift(send, "core", 1)),
+        [((Q, WT), F32)] + [((Q, WT), BF)] * 3,
         flops=1 << 20,
         nbytes=2 << 20,
     )
     activated, hidden_grad = call(
         gelu_body,
-        (mine_h, mine_a, shift(s1, "zl", 1), shift(s2, "zl", 2), shift(s3, "zl", 3)),
+        (mine, shift(s1, "zl", 1), shift(s2, "zl", 2), shift(s3, "zl", 3)),
         [((Q, HT), BF)] * 2,
         flops=1 << 22,
         nbytes=1 << 20,
@@ -214,9 +199,9 @@
     whole_hg = lax.all_gather(hidden_grad, ("zl", "core"), axis=0, tiled=True)
     whole_av = lax.all_gather(activated, ("zl", "core"), axis=0, tiled=True)
     partial = input_grad_partial(w1_where, whole_hg, w1_blocks)
-    w1_grad = block_grads(w1_pos, False, w1_where, whole_hg, whole_inputs)
-    w2_grad = block_grads(w2_pos, True, w2_where, whole_av, whole_cotangent)
-    input_grad = row_reduce(partial, (whole_av,))
+    w1_grad = block_grads(w1_pos, 0, w1_where, whole_hg, parts)
+    w2_grad = block_grads(w2_pos, 32, w2_where, whole_av, parts)
+    input_grad = row_reduce(partial, (whole_av[:16, :BS],))
     return input_grad, w1_grad, w2_grad
 
 

time: 195 us -> 182 us (0.933)
  blocking collectives: 82.8 us -> 57.6 us
  waiting for transfers between devices: 46 us -> 67.5 us
  starting transfers between devices: 42.2 us -> 35.3 us
    all_to_all x1, waiting for transfers between devices: 0.01 us -> 37.1 us  [shards(): parts = lax.all_to_all(sixteen, ('y', 'x'), 0, 0, tiled=True)]
    all_gather x1 -> x0, blocking collectives: 25.2 us -> none  [shards(): along = lax.all_gather(near_cotangent, 'x', axis=0, tiled=True)]
    ppermute x8 -> x4, waiting for transfers between devices: 26.4 us -> 13 us  [shift(): return lax.ppermute(value, axis, [(i, (i + step) % n) for i in range(n)])]
    ppermute x8 -> x4, starting transfers between devices: 24.7 us -> 17.7 us  [shift(): return lax.ppermute(value, axis, [(i, (i + step) % n) for i in range(n)])]
    unnamed x22 -> x18, local copies, waits for them, and re-layouts: 6.81 us -> 5.01 us
    pallas_call x8 -> x7, Pallas kernels: 11.9 us -> 10.4 us  [call(): pl.pallas_call(body, out_shape=[jax.ShapeDtypeStruct(s, d) for s, d in ou...]
  transfers between devices with their start and end apart: 11 -> 7, of which waited for: 8 -> 6; matrix products, arithmetic and copies ran while one was open for 0% -> 0% of each run, Pallas kernels for 4% -> 2%
where the time goes in v3:
time: 182 us; the launch traced here: 180 us
  waiting for transfers between devices  67.5 us (37%)
  blocking collectives  57.6 us (32%)
  starting transfers between devices  35.3 us (19%)
  Pallas kernels  10.4 us (6%)
  local copies, waits for them, and re-layouts  6.97 us (4%)
    all_to_all x1, waiting for transfers between devices, shards(): parts = lax.all_to_all(sixteen, ('y', 'x'), 0, 0, tiled=True)  37.1 us
    all_gather x1, blocking collectives, shards(): lax.all_gather(jnp.concatenate([inputs, cotangent], axis=0), 'zh', axis=0)  24.5 us
    ppermute x4, starting transfers between devices, shift(): return lax.ppermute(value, axis, [(i, (i + step) % n) for i in range(n)])  17.7 us
    all_gather x1, blocking collectives, shards(): whole_hg = lax.all_gather(hidden_grad, ('zl', 'core'), axis=0, tiled=True)  17.3 us
    all_gather x1, blocking collectives, shards(): whole_av = lax.all_gather(activated, ('zl', 'core'), axis=0, tiled=True)  15.7 us
    ppermute x4, waiting for transfers between devices, shift(): return lax.ppermute(value, axis, [(i, (i + step) % n) for i in range(n)])  13 us
    pallas_call x7, Pallas kernels, call(): pl.pallas_call(body, out_shape=[jax.ShapeDtypeStruct(s, d) for s, d in ou...  10.4 us
    all_to_all x1, waiting for transfers between devices, row_reduce(): parts = lax.all_to_all(partial, ('y', 'x'), 0, 0, tiled=True)  9.85 us
  transfers between devices with their start and end apart: 7, of which 6 were waited for; matrix products, arithmetic and copies ran while one was open for 0% of the time, Pallas kernels for 2%

profile of v3, /device:TPU:1, one launch (start us, length us, event | category | flops | bytes accessed | tf_op | source)
XLA Modules:
  0.0 180.0 jit_solution(1460642285516816225)
XLA Ops:
  0.6 0.8 pad_maximum_fusion
  1.4 24.5 %all-gather = bf16[64,1536]{1,0:T(8,128)(2,1)S(1)} all-gather(bf16[16,1536]{1,0:T(8,128)(2,1)S(1)} %pad_maximum_fusion), channel_id=2, replica_groups=mesh['x'=4,'zh'=4,'y'=4,'zl'=4,'core'=2] {'zh'}, dimensions={0}, use_global_device_ids=true | all-gather | bytes 245760 | tf_op jit(solution)/shard_map/all_gather | solution.py:172
  25.9 1.9 %broadcast_in_dim.8 = bf16[16,64,1536]{2,1,0:T(8,128)(2,1)} broadcast(bf16[64,1536]{1,0:T(8,128)(2,1)S(1)} %bitcast.9), dimensions={1,2} | broadcast | bytes 3342336 | tf_op jit(solution)/shard_map/broadcast_in_dim | solution.py:174
  27.9 6.9 %all-to-all-start = ((bf16[16,64,1536]{2,1,0:T(8,128)(2,1)}), bf16[16,64,1536]{2,1,0:T(8,128)(2,1)S(1)}, u32[]{:S(2)}, u32[]{:S(2)}) async-start(bf16[16,64,1536]{2,1,0:T(8,128)(2,1)} %broadcast_in_dim.8), calls=%async_computation | async-start | bytes 6291456 | tf_op jit(solution)/shard_map/all_to_all | solution.py:175
  34.8 0.1 pad_add_fusion.ids
  34.9 37.1 %all-to-all-done.parts.refs_2_ = bf16[16,64,1536]{2,1,0:T(8,128)(2,1)S(1)} async-done(((bf16[16,64,1536]{2,1,0:T(8,128)(2,1)}), bf16[16,64,1536]{2,1,0:T(8,128)(2,1)S(1)}, u32[]{:S(2)}, u32[]{:S(2)}) %all-to-all-start) | async-done | bytes 3145760 | tf_op jit(solution)/shard_map/all_to_all | solution.py:175
  72.0 1.0 copy-done.8
  72.9 1.9 %shard_map.85 = (f32[256,1536]{1,0:T(8,128)S(1)}, f32[256,1536]{1,0:T(8,128)S(1)}) custom-call(s32[9]{0:T(128)S(1)} %copy-done.6, s32[9]{0:T(128)S(1)} %copy-done.7, s32[2]{0:T(128)S(1)} %pad_add_fusion.ids, bf16[16,64,1536]{2,1,0:T(8,128)(2,1)S(1)} %all-to-all-done.parts.refs_2_, bf16[9,128,128]{2,1,0:T(8,128)(2,1)S(1)} %copy-done.5, ...), custom_call_target="tpu_custom_call" | custom-call | flops 1207959552 | bytes 6291456 | tf_op jit(solution)/shard_map/pallas_call | solution.py:34
  74.9 8.7 %collective-permute-start = (f32[256,1536]{1,0:T(8,128)S(1)}, f32[256,1536]{1,0:T(8,128)S(1)}, u32[]{:S(2)}, u32[]{:S(2)}) collective-permute-start(f32[256,1536]{1,0:T(8,128)S(1)} %get-tuple-element.12), channel_id=1, source_target_pairs={{0,1},{1,0},{2,3},{3,2},{4,5},{5,4},{6,7},{7,6},{8,9},{9,8},{10,11... | collective-permute-start | bytes 4718600 | tf_op jit(solution)/shard_map/ppermute | solution.py:30
  83.5 3.0 %collective-permute-done.got = f32[256,1536]{1,0:T(8,128)S(1)} collective-permute-done((f32[256,1536]{1,0:T(8,128)S(1)}, f32[256,1536]{1,0:T(8,128)S(1)}, u32[]{:S(2)}, u32[]{:S(2)}) %collective-permute-start) | collective-permute-done | bytes 1572896 | tf_op jit(solution)/shard_map/ppermute | solution.py:30
  86.6 0.7 shard_map.86
  87.3 1.9 %collective-permute-start.1 = (bf16[64,1536]{1,0:T(8,128)(2,1)S(1)}, bf16[64,1536]{1,0:T(8,128)(2,1)S(1)}, u32[]{:S(2)}, u32[]{:S(2)}) collective-permute-start(bf16[64,1536]{1,0:T(8,128)(2,1)S(1)} %get-tuple-element.14), channel_id=1, source_target_pairs={{0,2},{2,4},{4,6},{6,0},{1,3},{3,5},{5,7},{7,1},{8,10},{10,12},{12... | collective-permute-start | bytes 589832 | tf_op jit(solution)/shard_map/ppermute | solution.py:30
  89.2 3.7 %collective-permute-start.2 = (bf16[64,1536]{1,0:T(8,128)(2,1)S(1)}, bf16[64,1536]{1,0:T(8,128)(2,1)S(1)}, u32[]{:S(2)}, u32[]{:S(2)}) collective-permute-start(bf16[64,1536]{1,0:T(8,128)(2,1)S(1)} %get-tuple-element.15), channel_id=1, source_target_pairs={{0,4},{2,6},{4,0},{6,2},{1,5},{3,7},{5,1},{7,3},{8,12},{10,14},{12... | collective-permute-start | bytes 589832 | tf_op jit(solution)/shard_map/ppermute | solution.py:30
  92.9 3.3 %collective-permute-start.3 = (bf16[64,1536]{1,0:T(8,128)(2,1)S(1)}, bf16[64,1536]{1,0:T(8,128)(2,1)S(1)}, u32[]{:S(2)}, u32[]{:S(2)}) collective-permute-start(bf16[64,1536]{1,0:T(8,128)(2,1)S(1)} %get-tuple-element.16), channel_id=1, source_target_pairs={{0,6},{2,0},{4,2},{6,4},{1,7},{3,1},{5,3},{7,5},{8,14},{10,8},{12,... | collective-permute-start | bytes 589832 | tf_op jit(solution)/shard_map/ppermute | solution.py:30
  96.3 0.8 collective-permute-done.1.r1
  97.1 9.1 %collective-permute-done.2.r2 = bf16[64,1536]{1,0:T(8,128)(2,1)S(1)} collective-permute-done((bf16[64,1536]{1,0:T(8,128)(2,1)S(1)}, bf16[64,1536]{1,0:T(8,128)(2,1)S(1)}, u32[]{:S(2)}, u32[]{:S(2)}) %collective-permute-start.2) | collective-permute-done | bytes 196640 | tf_op jit(solution)/shard_map/ppermute | solution.py:30
  106.2 0.2 shard_map.87
  106.5 17.3 %all_gather.14.hg.refs_1_ = bf16[512,768]{1,0:T(8,128)(2,1)S(1)} all-gather(bf16[64,768]{1,0:T(8,128)(2,1)S(1)} %get-tuple-element.17), channel_id=1, replica_groups=mesh['x'=4,'zh'=4,'y'=4,'zl'=4,'core'=2] {'zl','core'}, dimensions={0}, use_global_device_ids=true | all-gather | bytes 884736 | tf_op jit(solution)/shard_map/all_gather | solution.py:199
  123.8 1.4 shard_map.88
  125.3 0.9 copy-done
  126.2 1.1 copy-done.2
  127.3 4.4 %all-to-all-start.1 = ((bf16[16,32,1536]{2,1,0:T(8,128)(2,1)}), bf16[16,32,1536]{2,1,0:T(8,128)(2,1)}, u32[]{:S(2)}, u32[]{:S(2)}) async-start(bf16[16,32,1536]{2,1,0:T(8,128)(2,1)} %bitcast.8), calls=%async_computation.1 | async-start | bytes 3145728 | tf_op jit(solution)/shard_map/all_to_all | solution.py:157
  131.7 15.7 %all_gather.15.refs_1_ = bf16[512,768]{1,0:T(8,128)(2,1)S(1)} all-gather(bf16[64,768]{1,0:T(8,128)(2,1)S(1)} %get-tuple-element.18), channel_id=1, replica_groups=mesh['x'=4,'zh'=4,'y'=4,'zl'=4,'core'=2] {'zl','core'}, dimensions={0}, use_global_device_ids=true | all-gather | bytes 884736 | tf_op jit(solution)/shard_map/all_gather | solution.py:200
  147.4 0.9 copy-done.3
  148.3 9.8 %all-to-all-done.1.parts = bf16[16,32,1536]{2,1,0:T(8,128)(2,1)} async-done(((bf16[16,32,1536]{2,1,0:T(8,128)(2,1)}), bf16[16,32,1536]{2,1,0:T(8,128)(2,1)}, u32[]{:S(2)}, u32[]{:S(2)}) %all-to-all-start.1) | async-done | bytes 1572896 | tf_op jit(solution)/shard_map/all_to_all | solution.py:157
  158.1 2.2 %shard_map.89 = bf16[32,1536]{1,0:T(8,128)(2,1)} custom-call(bf16[16,32,1536]{2,1,0:T(8,128)(2,1)} %all-to-all-done.1.parts, bf16[16,128]{1,0:T(8,128)(2,1)S(1)} %slice.4.refs_0_), custom_call_target="tpu_custom_call" | custom-call | flops 1048576 | bytes 2097152 | tf_op jit(solution)/shard_map/pallas_call | solution.py:34
  160.4 6.4 %all-to-all-start.2 = ((bf16[4,8,1536]{2,1,0:T(8,128)(2,1)}), bf16[4,8,1536]{2,1,0:T(8,128)(2,1)S(1)}, u32[]{:S(2)}, u32[]{:S(2)}) async-start(bf16[4,8,1536]{2,1,0:T(8,128)(2,1)} %bitcast.6), calls=%async_computation.2 | async-start | bytes 196608 | tf_op jit(solution)/shard_map/all_to_all | solution.py:166
  166.7 1.1 copy-done.1
  167.9 1.9 %shard_map.90 = f32[9,128,128]{2,1,0:T(8,128)} custom-call(s32[9]{0:T(128)S(1)} %copy-done.6, bf16[512,768]{1,0:T(8,128)(2,1)S(1)} %copy-done.1, bf16[16,64,1536]{2,1,0:T(8,128)(2,1)S(1)} %all-to-all-done.parts.refs_2_), custom_call_target="tpu_custom_call" | custom-call | flops 603979776 | bytes 4194304 | tf_op jit(solution)/shard_map/pallas_call | solution.py:34
  169.8 2.0 %shard_map.91 = f32[9,128,128]{2,1,0:T(8,128)} custom-call(s32[9]{0:T(128)S(1)} %copy-done.7, bf16[512,768]{1,0:T(8,128)(2,1)S(1)} %copy-done.4, bf16[16,64,1536]{2,1,0:T(8,128)(2,1)S(1)} %all-to-all-done.parts.refs_2_), custom_call_target="tpu_custom_call" | custom-call | flops 603979776 | bytes 4194304 | tf_op jit(solution)/shard_map/pallas_call | solution.py:34
  171.8 7.6 %all-to-all-done.2 = bf16[4,8,1536]{2,1,0:T(8,128)(2,1)S(1)} async-done(((bf16[4,8,1536]{2,1,0:T(8,128)(2,1)}), bf16[4,8,1536]{2,1,0:T(8,128)(2,1)S(1)}, u32[]{:S(2)}, u32[]{:S(2)}) %all-to-all-start.2) | async-done | bytes 98336 | tf_op jit(solution)/shard_map/all_to_all | solution.py:166
  179.4 0.6 reduce_sum.12
  (16 shorter events, 0.0 us)
Async XLA Ops:
  27.9 44.1 %copy-start.5 = (bf16[9,128,128]{2,1,0:T(8,128)(2,1)S(1)}, bf16[9,128,128]{2,1,0:T(8,128)(2,1)}, u32[]{:S(2)}) copy-start(bf16[9,128,128]{2,1,0:T(8,128)(2,1)} %blocks.1) | copy-start | bytes 884740
  27.9 44.1 %copy-start.6 = (s32[9]{0:T(128)S(1)}, s32[9]{0:T(128)}, u32[]{:S(2)}) copy-start(s32[9]{0:T(128)} %refs_0_.2) | copy-start | bytes 112
  27.9 44.1 %copy-start.7 = (s32[9]{0:T(128)S(1)}, s32[9]{0:T(128)}, u32[]{:S(2)}) copy-start(s32[9]{0:T(128)} %refs_0_.3) | copy-start | bytes 112
  27.9 44.1 %all-to-all-start = ((bf16[16,64,1536]{2,1,0:T(8,128)(2,1)}), bf16[16,64,1536]{2,1,0:T(8,128)(2,1)S(1)}, u32[]{:S(2)}, u32[]{:S(2)}) async-start(bf16[16,64,1536]{2,1,0:T(8,128)(2,1)} %broadcast_in_dim.8), calls=%async_computation | async-start | bytes 6291456 | tf_op jit(solution)/shard_map/all_to_all | solution.py:175
  72.0 1.0 copy-start.8
  74.9 11.7 %collective-permute-start = (f32[256,1536]{1,0:T(8,128)S(1)}, f32[256,1536]{1,0:T(8,128)S(1)}, u32[]{:S(2)}, u32[]{:S(2)}) collective-permute-start(f32[256,1536]{1,0:T(8,128)S(1)} %get-tuple-element.12), channel_id=1, source_target_pairs={{0,1},{1,0},{2,3},{3,2},{4,5},{5,4},{6,7},{7,6},{8,9},{9,8},{10,11... | collective-permute-start | bytes 4718600 | tf_op jit(solution)/shard_map/ppermute | solution.py:30
  87.3 9.8 %collective-permute-start.1 = (bf16[64,1536]{1,0:T(8,128)(2,1)S(1)}, bf16[64,1536]{1,0:T(8,128)(2,1)S(1)}, u32[]{:S(2)}, u32[]{:S(2)}) collective-permute-start(bf16[64,1536]{1,0:T(8,128)(2,1)S(1)} %get-tuple-element.14), channel_id=1, source_target_pairs={{0,2},{2,4},{4,6},{6,0},{1,3},{3,5},{5,7},{7,1},{8,10},{10,12},{12... | collective-permute-start | bytes 589832 | tf_op jit(solution)/shard_map/ppermute | solution.py:30
  89.2 17.1 %collective-permute-start.2 = (bf16[64,1536]{1,0:T(8,128)(2,1)S(1)}, bf16[64,1536]{1,0:T(8,128)(2,1)S(1)}, u32[]{:S(2)}, u32[]{:S(2)}) collective-permute-start(bf16[64,1536]{1,0:T(8,128)(2,1)S(1)} %get-tuple-element.15), channel_id=1, source_target_pairs={{0,4},{2,6},{4,0},{6,2},{1,5},{3,7},{5,1},{7,3},{8,12},{10,14},{12... | collective-permute-start | bytes 589832 | tf_op jit(solution)/shard_map/ppermute | solution.py:30
  92.9 13.3 %collective-permute-start.3 = (bf16[64,1536]{1,0:T(8,128)(2,1)S(1)}, bf16[64,1536]{1,0:T(8,128)(2,1)S(1)}, u32[]{:S(2)}, u32[]{:S(2)}) collective-permute-start(bf16[64,1536]{1,0:T(8,128)(2,1)S(1)} %get-tuple-element.16), channel_id=1, source_target_pairs={{0,6},{2,0},{4,2},{6,4},{1,7},{3,1},{5,3},{7,5},{8,14},{10,8},{12,... | collective-permute-start | bytes 589832 | tf_op jit(solution)/shard_map/ppermute | solution.py:30
  125.3 0.9 copy-start
  126.2 1.1 copy-start.2
  127.3 30.9 %all-to-all-start.1 = ((bf16[16,32,1536]{2,1,0:T(8,128)(2,1)}), bf16[16,32,1536]{2,1,0:T(8,128)(2,1)}, u32[]{:S(2)}, u32[]{:S(2)}) async-start(bf16[16,32,1536]{2,1,0:T(8,128)(2,1)} %bitcast.8), calls=%async_computation.1 | async-start | bytes 3145728 | tf_op jit(solution)/shard_map/all_to_all | solution.py:157
  147.4 0.9 copy-start.3
  160.4 19.0 %all-to-all-start.2 = ((bf16[4,8,1536]{2,1,0:T(8,128)(2,1)}), bf16[4,8,1536]{2,1,0:T(8,128)(2,1)S(1)}, u32[]{:S(2)}, u32[]{:S(2)}) async-start(bf16[4,8,1536]{2,1,0:T(8,128)(2,1)} %bitcast.6), calls=%async_computation.2 | async-start | bytes 196608 | tf_op jit(solution)/shard_map/all_to_all | solution.py:166
  166.7 1.1 copy-start.1
  167.9 2.0 %copy-start.4 = (bf16[512,768]{1,0:T(8,128)(2,1)S(1)}, bf16[512,768]{1,0:T(8,128)(2,1)}, u32[]{:S(2)}) copy-start(bf16[512,768]{1,0:T(8,128)(2,1)} %copy-done.3) | copy-start | bytes 2359300

commit v4 on v3

v4 whole, which is shorter than its diff:
```python
import math

import jax
import jax.numpy as jnp
from jax import lax
from jax.experimental import pallas as pl
from jax.experimental.pallas import tpu as pltpu
from jax.sharding import Mesh, PartitionSpec as P

BF, F32 = jnp.bfloat16, jnp.float32
BS = 128
TOK = 512
WT = 1536
HT = 768
NI = WT // BS
NJ = HT // BS
NB = 9
Q = TOK // 8
STEPS = (0, 1, 3, 2)
FIRST = 3 * Q // 4
W1_COLS = 384
W2_COLS = 96
SIZE = {"x": 4, "y": 4, "zh": 4, "zl": 4, "core": 2}
C0 = math.sqrt(2.0 / math.pi)

VM = pl.BlockSpec(memory_space=pltpu.VMEM)
SM = pl.BlockSpec(memory_space=pltpu.SMEM)


def shift(value, axis, step):
    n = SIZE[axis]
    return lax.ppermute(value, axis, [(i, (i + step) % n) for i in range(n)])


def call(body, ins, outs, scratch=(), flops=0, nbytes=0, vmem=16, after=()):
    n, m = len(ins), len(ins) + len(after)
    return pl.pallas_call(
        lambda *refs: body(*refs[:n], *refs[m:]),
        out_shape=[jax.ShapeDtypeStruct(s, d) for s, d in outs],
        in_specs=[SM if a.dtype == jnp.int32 else VM for a in ins]
        + [pl.BlockSpec(memory_space=pl.ANY)] * len(after),
        out_specs=[VM] * len(outs),
        scratch_shapes=list(scratch),
        compiler_params=pltpu.CompilerParams(vmem_limit_bytes=vmem << 20),
        cost_estimate=pl.CostEstimate(flops=flops, bytes_accessed=nbytes, transcendentals=0),
    )(*ins, *after)


def w1_pos(where):
    return lax.rem(where // W1_COLS, NI), lax.rem(lax.rem(where, W1_COLS), NJ)


def w2_pos(where):
    return lax.rem(lax.rem(where, W2_COLS), NI), lax.rem(where // W2_COLS, NJ)


def lanes(index):
    return pl.ds(pl.multiple_of(index * BS, BS), BS)


NN = (((1,), (0,)), ((), ()))
NT = (((1,), (1,)), ((), ()))
TN = (((0,), (0,)), ((), ()))


def dot(a, b, dims):
    return lax.dot_general(a, b, dims, preferred_element_type=F32)


def rows_of(parts, first, index):
    at = lanes(index)
    return jnp.concatenate([p[:, first : first + 32, at].reshape(4 * 32, BS) for p in parts], axis=0)


def partial_body(where1, where2, ids, *refs):
    parts, (blocks1, blocks2, keep, send, acc) = refs[:-5], refs[-5:]
    n = len(parts) * 16
    core = ids[0]
    acc[...] = jnp.zeros_like(acc)
    for b in range(NB):
        i, j = w1_pos(where1[b])
        acc[j] += dot(rows_of(parts, 0, i), blocks1[b], NN)
        i, j = w2_pos(where2[b])
        acc[NJ + j] += dot(rows_of(parts, 32, i), blocks2[b], NT)
    for z in range(4):
        mine = pl.ds(pl.multiple_of((2 * z + core) * n, n), n)
        other = pl.ds(pl.multiple_of((2 * z + 1 - core) * n, n), n)
        for j in range(2 * NJ):
            keep[z * n : (z + 1) * n, j * BS : (j + 1) * BS] = acc[j, mine]
            send[z * n : (z + 1) * n, j * BS : (j + 1) * BS] = acc[j, other]


def split_body(ids, keep, got, mine, s1, s2, s3):
    n = mine.shape[0]
    zl = ids[1]
    own = pl.ds(pl.multiple_of(zl * n, n), n)
    mine[...] = keep[own] + got[own]
    for k, ref in ((1, s1), (2, s2), (3, s3)):
        part = pl.ds(pl.multiple_of(lax.rem(zl + k, 4) * n, n), n)
        ref[...] = (keep[part] + got[part]).astype(BF)


def product_terms(ids, where1, where2, parts, blocks1, blocks2, after=()):
    n = len(parts)
    return call(
        partial_body,
        (where1, where2, ids, *parts, blocks1, blocks2),
        [((n * Q, WT), F32)] * 2,
        [pltpu.VMEM((2 * NJ, n * 128, BS), F32)],
        flops=2 * NB * n * 128 * BS * BS * 8,
        nbytes=n << 21,
        after=after,
        vmem=20,
    )


def column_sums(ids, keep, got):
    n = keep.shape[0] // 4
    mine, s1, s2, s3 = call(
        split_body,
        (ids, keep, got),
        [((n, WT), F32)] + [((n, WT), BF)] * 3,
        flops=1 << 20,
        nbytes=1 << 20,
    )
    return mine, shift(s1, "zl", 1), shift(s2, "zl", 2), shift(s3, "zl", 3)


def gelu_body(*refs):
    activated, hidden_grad = refs[8:]
    for h in range(2):
        own, r1, r2, r3 = refs[4 * h : 4 * h + 4]
        v, g = own[:, :HT], own[:, HT:]
        for ref in (r1, r2, r3):
            v = v + ref[:, :HT].astype(F32)
            g = g + ref[:, HT:].astype(F32)
        t = jnp.tanh(C0 * (v + 0.044715 * v * v * v))
        derive = C0 * (1.0 + 3.0 * 0.044715 * v * v)
        slope = 0.5 * (1.0 + t) + 0.5 * v * (1.0 - t * t) * derive
        at = slice(0, FIRST) if h == 0 else slice(FIRST, Q)
        activated[at] = (0.5 * v * (1.0 + t)).astype(BF)
        hidden_grad[at] = (g * slope).astype(BF)


def tokens_of(hid, index):
    at = lanes(index)
    return jnp.concatenate(
        [hid[:, :FIRST, at].reshape(8 * FIRST, BS), hid[:, FIRST:, at].reshape(8 * (Q - FIRST), BS)], axis=0
    )


def input_grad_body(where, ids, hg, blocks, out, acc):
    y = ids[2]
    acc[...] = jnp.zeros_like(acc)
    for b in range(NB):
        i, j = w1_pos(where[b])
        acc[i] += dot(tokens_of(hg, j), blocks[b], NT)
    for q, step in enumerate(STEPS):
        owner = lax.rem(y + 4 - step, 4) * 4
        for x in range(4):
            row = (4 * q + x) * 32
            for i in range(NI):
                out[owner + x, :, i * BS : (i + 1) * BS] = acc[i, row : row + 32].astype(BF)


def input_grad_partial(where, ids, hg, blocks):
    (out,) = call(
        input_grad_body,
        (where, ids, hg, blocks),
        [((16, 32, WT), BF)],
        [pltpu.VMEM((NI, TOK, BS), F32)],
        flops=2 * NB * TOK * BS * BS * 4,
        nbytes=4 << 20,
    )
    return out


def block_grad_body(pos, first, where, hid, *refs):
    parts, out = refs[:4], refs[4]
    for b in range(NB):
        i, j = pos(where[b])
        left, right = rows_of(parts, first, i), tokens_of(hid, j)
        if first:
            left, right = right, left
        out[b] = dot(left, right, TN)


def block_grads(pos, first, where, hid, parts):
    (out,) = call(
        lambda *refs: block_grad_body(pos, first, *refs),
        (where, hid, *parts),
        [((NB, BS, BS), F32)],
        flops=2 * NB * TOK * BS * BS * 4,
        nbytes=4 << 20,
    )
    return out


def sum_body(parts, out):
    total = parts[0].astype(F32)
    for k in range(1, 16):
        total = total + parts[k].astype(F32)
    out[...] = total.astype(BF)


def row_reduce(partial, after):
    parts = lax.all_to_all(partial, ("y", "x"), 0, 0, tiled=True)
    (mine,) = call(
        sum_body,
        (parts,),
        [((32, WT), BF)],
        flops=1 << 20,
        nbytes=2 << 20,
        after=after,
    )
    last = lax.all_to_all(mine, "zh", 0, 0, tiled=True)
    return jnp.sum(last.reshape(4, 8, WT).astype(F32), axis=0).astype(BF)


def shards(inputs, cotangent, w1_blocks, w1_where, w2_blocks, w2_where):
    ids = jnp.stack([lax.axis_index(a) for a in ("core", "zl", "y")]).astype(jnp.int32)
    near = lax.all_gather(jnp.concatenate([inputs, cotangent], axis=0), "zh", axis=0)
    near = near.reshape(4, 2, 8, WT).swapaxes(0, 1).reshape(64, WT)
    along = lax.all_gather(near, "x", axis=0)
    parts = [along, shift(along, "y", 1), shift(along, "y", 3)]
    weights = (w1_blocks, w2_blocks)
    parts.append(shift(along, "y", 2))
    keep, send = product_terms(ids, w1_where, w2_where, parts[:3], *weights)
    first = column_sums(ids, keep, shift(send, "core", 1))
    keep, send = product_terms(ids, w1_where, w2_where, parts[3:], *weights, after=first[1:])
    second = column_sums(ids, keep, shift(send, "core", 1))
    activated, hidden_grad = call(
        gelu_body, (*first, *second), [((Q, HT), BF)] * 2, flops=1 << 22, nbytes=1 << 20
    )
    whole_hg = lax.all_gather(hidden_grad, ("zl", "core"), axis=0, tiled=True).reshape(8, Q, HT)
    whole_av = lax.all_gather(activated, ("zl", "core"), axis=0, tiled=True).reshape(8, Q, HT)
    partial = input_grad_partial(w1_where, ids, whole_hg, w1_blocks)
    w1_grad = block_grads(w1_pos, 0, w1_where, whole_hg, parts)
    w2_grad = block_grads(w2_pos, 32, w2_where, whole_av, parts)
    input_grad = row_reduce(partial, (whole_av[0, :16, :BS],))
    return input_grad, w1_grad, w2_grad


def solution(mesh):
    fine = Mesh(mesh.devices.reshape(4, 4, 4, 4, 2), ("x", "zh", "y", "zl", "core"))
    row, col = ("x", "zh", "y"), ("zl", "core")
    both = row + col
    return jax.shard_map(
        shards,
        mesh=fine,
        in_specs=(P(row, col), P(row, col), P(both, None, None), P(both), P(both, None, None), P(both)),
        out_specs=(P(row, col), P(both, None, None), P(both, None, None)),
        check_vma=False,
    )
```

time: 182 us -> 180 us (0.989)
  waiting for transfers between devices: 67.5 us -> 40 us
  starting transfers between devices: 35.3 us -> 53.5 us
  blocking collectives: 57.6 us -> 67.9 us
  local copies, waits for them, and re-layouts: 6.97 us -> 3.44 us
    all_to_all x1 -> x0, waiting for transfers between devices: 37.1 us -> none  [shards(): parts = lax.all_to_all(sixteen, ('y', 'x'), 0, 0, tiled=True)]
    ppermute x4 -> x11, starting transfers between devices: 17.7 us -> 41.3 us  [shift(): return lax.ppermute(value, axis, [(i, (i + step) % n) for i in range(n)])]
    ppermute x4 -> x11, waiting for transfers between devices: 13 us -> 24.4 us  [shift(): return lax.ppermute(value, axis, [(i, (i + step) % n) for i in range(n)])]
    all_gather x2 -> x3, blocking collectives: 33 us -> 43.4 us  [the longest x1 16.5 us: shards(): lax.all_gather(hidden_grad, ('zl', 'core'), axis=0, tiled=True)]
    all_to_all x1 -> x0, starting transfers between devices: 6.89 us -> none  [shards(): parts = lax.all_to_all(sixteen, ('y', 'x'), 0, 0, tiled=True)]
    broadcast_in_dim x1 -> x0, local copies, waits for them, and re-layouts: 1.95 us -> none  [shards(): sixteen = jnp.broadcast_to(near[None], (16, 64, WT))]
    pallas_call x7 -> x9, Pallas kernels: 10.4 us -> 11.6 us  [call(): pl.pallas_call(lambda *refs: body(*refs[:n], *refs[m:]), out_shape=[jax.S...]
  transfers between devices with their start and end apart: 7 -> 13, of which waited for: 6 -> 8; matrix products, arithmetic and copies ran while one was open for 0% -> 0% of each run, Pallas kernels for 2% -> 3%
where the time goes in v4:
time: 180 us; the launch traced here: 179 us
  blocking collectives  67.9 us (38%)
  starting transfers between devices  53.5 us (30%)
  waiting for transfers between devices  40 us (22%)
  Pallas kernels  11.6 us (6%)
  local copies, waits for them, and re-layouts  3.44 us (2%)
    ppermute x11, starting transfers between devices, shift(): return lax.ppermute(value, axis, [(i, (i + step) % n) for i in range(n)])  41.3 us
    all_gather x1, blocking collectives, shards(): lax.all_gather(jnp.concatenate([inputs, cotangent], axis=0), 'zh', axis=0)  24.5 us
    ppermute x11, waiting for transfers between devices, shift(): return lax.ppermute(value, axis, [(i, (i + step) % n) for i in range(n)])  24.4 us
    all_gather x1, blocking collectives, shards(): lax.all_gather(hidden_grad, ('zl', 'core'), axis=0, tiled=True)  16.5 us
    all_gather x1, blocking collectives, shards(): lax.all_gather(activated, ('zl', 'core'), axis=0, tiled=True)  15.8 us
    pallas_call x9, Pallas kernels, call(): pl.pallas_call(lambda *refs: body(*refs[:n], *refs[m:]), out_shape=[jax.S...  11.6 us
    all_gather x1, blocking collectives, shards(): along = lax.all_gather(near, 'x', axis=0)  11.1 us
    all_to_all x1, waiting for transfers between devices, row_reduce(): parts = lax.all_to_all(partial, ('y', 'x'), 0, 0, tiled=True)  9.06 us
  transfers between devices with their start and end apart: 13, of which 8 were waited for; matrix products, arithmetic and copies ran while one was open for 0% of the time, Pallas kernels for 3%

profile of v4, /device:TPU:1, one launch (start us, length us, event | category | flops | bytes accessed | tf_op | source)
XLA Modules:
  0.0 178.8 jit_solution(6401996963617753290)
XLA Ops:
  1.5 24.5 %all-gather = bf16[64,1536]{1,0:T(8,128)(2,1)S(1)} all-gather(bf16[16,1536]{1,0:T(8,128)(2,1)S(1)} %pad_maximum_fusion), channel_id=2, replica_groups=mesh['x'=4,'zh'=4,'y'=4,'zl'=4,'core'=2] {'zh'}, dimensions={0}, use_global_device_ids=true | all-gather | bytes 245760 | tf_op jit(solution)/shard_map/all_gather | solution.py:222
  26.0 11.1 %all_gather.17.refs_3_.refs_2_ = bf16[4,64,1536]{2,1,0:T(8,128)(2,1)S(1)} all-gather(bf16[1,64,1536]{2,1,0:T(8,128)(2,1)S(1)} %bitcast.17), channel_id=1, replica_groups=mesh['x'=4,'zh'=4,'y'=4,'zl'=4,'core'=2] {'x'}, dimensions={0}, use_global_device_ids=true | all-gather | bytes 983040 | tf_op jit(solution)/shard_map/all_gather | solution.py:224
  37.2 3.2 %collective-permute-start = (bf16[4,64,1536]{2,1,0:T(8,128)(2,1)S(1)}, bf16[4,64,1536]{2,1,0:T(8,128)(2,1)S(1)}, u32[]{:S(2)}, u32[]{:S(2)}) collective-permute-start(bf16[4,64,1536]{2,1,0:T(8,128)(2,1)S(1)} %all_gather.17.refs_3_.refs_2_), channel_id=1, source_target_pairs={{0,8},{8,16},{16,24},{24,0},{1,9},{9,17},{17,25},{25,1},{2,10},{10... | collective-permute-start | bytes 2359304 | tf_op jit(solution)/shard_map/ppermute | solution.py:32
  40.4 3.4 %collective-permute-start.1 = (bf16[4,64,1536]{2,1,0:T(8,128)(2,1)S(1)}, bf16[4,64,1536]{2,1,0:T(8,128)(2,1)S(1)}, u32[]{:S(2)}, u32[]{:S(2)}) collective-permute-start(bf16[4,64,1536]{2,1,0:T(8,128)(2,1)S(1)} %all_gather.17.refs_3_.refs_2_), channel_id=1, source_target_pairs={{0,24},{8,0},{16,8},{24,16},{1,25},{9,1},{17,9},{25,17},{2,26},{10... | collective-permute-start | bytes 2359304 | tf_op jit(solution)/shard_map/ppermute | solution.py:32
  43.8 8.8 %collective-permute-done.refs_4_.refs_3_ = bf16[4,64,1536]{2,1,0:T(8,128)(2,1)S(1)} collective-permute-done((bf16[4,64,1536]{2,1,0:T(8,128)(2,1)S(1)}, bf16[4,64,1536]{2,1,0:T(8,128)(2,1)S(1)}, u32[]{:S(2)}, u32[]{:S(2)}) %collective-permute-start) | collective-permute-done | bytes 786464 | tf_op jit(solution)/shard_map/ppermute | solution.py:32
  52.6 1.6 collective-permute-done.1.refs_5_.refs_4_
  54.2 1.5 shard_map.85
  55.7 9.9 %collective-permute-start.2 = (f32[192,1536]{1,0:T(8,128)S(1)}, f32[192,1536]{1,0:T(8,128)S(1)}, u32[]{:S(2)}, u32[]{:S(2)}) collective-permute-start(f32[192,1536]{1,0:T(8,128)S(1)} %get-tuple-element.18), channel_id=1, source_target_pairs={{0,1},{1,0},{2,3},{3,2},{4,5},{5,4},{6,7},{7,6},{8,9},{9,8},{10,11... | collective-permute-start | bytes 3538952 | tf_op jit(solution)/shard_map/ppermute | solution.py:32
  65.7 4.5 %collective-permute-start.6 = (bf16[4,64,1536]{2,1,0:T(8,128)(2,1)S(1)}, bf16[4,64,1536]{2,1,0:T(8,128)(2,1)S(1)}, u32[]{:S(2)}, u32[]{:S(2)}) collective-permute-start(bf16[4,64,1536]{2,1,0:T(8,128)(2,1)S(1)} %all_gather.17.refs_3_.refs_2_), channel_id=1, source_target_pairs={{0,16},{8,24},{16,0},{24,8},{1,17},{9,25},{17,1},{25,9},{2,18},{10... | collective-permute-start | bytes 2359304 | tf_op jit(solution)/shard_map/ppermute | solution.py:32
  70.9 2.3 %collective-permute-start.3 = (bf16[48,1536]{1,0:T(8,128)(2,1)S(1)}, bf16[48,1536]{1,0:T(8,128)(2,1)S(1)}, u32[]{:S(2)}, u32[]{:S(2)}) collective-permute-start(bf16[48,1536]{1,0:T(8,128)(2,1)S(1)} %get-tuple-element.20), channel_id=1, source_target_pairs={{0,2},{2,4},{4,6},{6,0},{1,3},{3,5},{5,7},{7,1},{8,10},{10,12},{12... | collective-permute-start | bytes 442376 | tf_op jit(solution)/shard_map/ppermute | solution.py:32
  73.2 3.4 %collective-permute-start.4 = (bf16[48,1536]{1,0:T(8,128)(2,1)S(1)}, bf16[48,1536]{1,0:T(8,128)(2,1)S(1)}, u32[]{:S(2)}, u32[]{:S(2)}) collective-permute-start(bf16[48,1536]{1,0:T(8,128)(2,1)S(1)} %get-tuple-element.21), channel_id=1, source_target_pairs={{0,4},{2,6},{4,0},{6,2},{1,5},{3,7},{5,1},{7,3},{8,12},{10,14},{12... | collective-permute-start | bytes 442376 | tf_op jit(solution)/shard_map/ppermute | solution.py:32
  76.6 3.4 %collective-permute-start.5 = (bf16[48,1536]{1,0:T(8,128)(2,1)S(1)}, bf16[48,1536]{1,0:T(8,128)(2,1)S(1)}, u32[]{:S(2)}, u32[]{:S(2)}) collective-permute-start(bf16[48,1536]{1,0:T(8,128)(2,1)S(1)} %get-tuple-element.22), channel_id=1, source_target_pairs={{0,6},{2,0},{4,2},{6,4},{1,7},{3,1},{5,3},{7,5},{8,14},{10,8},{12,... | collective-permute-start | bytes 442376 | tf_op jit(solution)/shard_map/ppermute | solution.py:32
  80.0 8.2 %collective-permute-done.6.refs_3_.refs_5_ = bf16[4,64,1536]{2,1,0:T(8,128)(2,1)S(1)} collective-permute-done((bf16[4,64,1536]{2,1,0:T(8,128)(2,1)S(1)}, bf16[4,64,1536]{2,1,0:T(8,128)(2,1)S(1)}, u32[]{:S(2)}, u32[]{:S(2)}) %collective-permute-start.6) | collective-permute-done | bytes 786464 | tf_op jit(solution)/shard_map/ppermute | solution.py:32
  89.3 2.7 %collective-permute-start.7 = (f32[64,1536]{1,0:T(8,128)S(1)}, f32[64,1536]{1,0:T(8,128)S(1)}, u32[]{:S(2)}, u32[]{:S(2)}) collective-permute-start(f32[64,1536]{1,0:T(8,128)S(1)} %get-tuple-element.24), channel_id=1, source_target_pairs={{0,1},{1,0},{2,3},{3,2},{4,5},{5,4},{6,7},{7,6},{8,9},{9,8},{10,11... | collective-permute-start | bytes 1179656 | tf_op jit(solution)/shard_map/ppermute | solution.py:32
  92.0 1.3 collective-permute-done.7.refs_2_
  93.9 3.8 %collective-permute-start.10 = (bf16[16,1536]{1,0:T(8,128)(2,1)S(1)}, bf16[16,1536]{1,0:T(8,128)(2,1)S(1)}, u32[]{:S(2)}, u32[]{:S(2)}) collective-permute-start(bf16[16,1536]{1,0:T(8,128)(2,1)S(1)} %get-tuple-element.28), channel_id=1, source_target_pairs={{0,6},{2,0},{4,2},{6,4},{1,7},{3,1},{5,3},{7,5},{8,14},{10,8},{12,... | collective-permute-start | bytes 147464 | tf_op jit(solution)/shard_map/ppermute | solution.py:32
  97.8 1.9 %collective-permute-start.8 = (bf16[16,1536]{1,0:T(8,128)(2,1)S(1)}, bf16[16,1536]{1,0:T(8,128)(2,1)S(1)}, u32[]{:S(2)}, u32[]{:S(2)}) collective-permute-start(bf16[16,1536]{1,0:T(8,128)(2,1)S(1)} %get-tuple-element.26), channel_id=1, source_target_pairs={{0,2},{2,4},{4,6},{6,0},{1,3},{3,5},{5,7},{7,1},{8,10},{10,12},{12... | collective-permute-start | bytes 147464 | tf_op jit(solution)/shard_map/ppermute | solution.py:32
  99.7 2.8 %collective-permute-start.9 = (bf16[16,1536]{1,0:T(8,128)(2,1)S(1)}, bf16[16,1536]{1,0:T(8,128)(2,1)S(1)}, u32[]{:S(2)}, u32[]{:S(2)}) collective-permute-start(bf16[16,1536]{1,0:T(8,128)(2,1)S(1)} %get-tuple-element.27), channel_id=1, source_target_pairs={{0,4},{2,6},{4,0},{6,2},{1,5},{3,7},{5,1},{7,3},{8,12},{10,14},{12... | collective-permute-start | bytes 147464 | tf_op jit(solution)/shard_map/ppermute | solution.py:32
  102.5 1.9 %collective-permute-done.8.refs_5_ = bf16[16,1536]{1,0:T(8,128)(2,1)S(1)} collective-permute-done((bf16[16,1536]{1,0:T(8,128)(2,1)S(1)}, bf16[16,1536]{1,0:T(8,128)(2,1)S(1)}, u32[]{:S(2)}, u32[]{:S(2)}) %collective-permute-start.8) | collective-permute-done | bytes 49184 | tf_op jit(solution)/shard_map/ppermute | solution.py:32
  104.4 2.5 %collective-permute-done.9.refs_6_ = bf16[16,1536]{1,0:T(8,128)(2,1)S(1)} collective-permute-done((bf16[16,1536]{1,0:T(8,128)(2,1)S(1)}, bf16[16,1536]{1,0:T(8,128)(2,1)S(1)}, u32[]{:S(2)}, u32[]{:S(2)}) %collective-permute-start.9) | collective-permute-done | bytes 49184 | tf_op jit(solution)/shard_map/ppermute | solution.py:32
  107.1 16.5 %all_gather.18 = bf16[512,768]{1,0:T(8,128)(2,1)S(1)} all-gather(bf16[64,768]{1,0:T(8,128)(2,1)S(1)} %get-tuple-element.29), channel_id=1, replica_groups=mesh['x'=4,'zh'=4,'y'=4,'zl'=4,'core'=2] {'zl','core'}, dimensions={0}, use_global_device_ids=true | all-gather | bytes 884736 | tf_op jit(solution)/shard_map/all_gather | solution.py:235
  123.6 1.4 shard_map.90
  126.2 5.7 %all-to-all-start = ((bf16[16,32,1536]{2,1,0:T(8,128)(2,1)}), bf16[16,32,1536]{2,1,0:T(8,128)(2,1)}, u32[]{:S(2)}, u32[]{:S(2)}) async-start(bf16[16,32,1536]{2,1,0:T(8,128)(2,1)} %copy-done), calls=%async_computation | async-start | bytes 3145728 | tf_op jit(solution)/shard_map/all_to_all | solution.py:207
  131.9 15.8 %all_gather.19 = bf16[512,768]{1,0:T(8,128)(2,1)S(1)} all-gather(bf16[64,768]{1,0:T(8,128)(2,1)S(1)} %get-tuple-element.30), channel_id=1, replica_groups=mesh['x'=4,'zh'=4,'y'=4,'zl'=4,'core'=2] {'zl','core'}, dimensions={0}, use_global_device_ids=true | all-gather | bytes 884736 | tf_op jit(solution)/shard_map/all_gather | solution.py:236
  147.7 9.1 %all-to-all-done.refs_0_ = bf16[16,32,1536]{2,1,0:T(8,128)(2,1)} async-done(((bf16[16,32,1536]{2,1,0:T(8,128)(2,1)}), bf16[16,32,1536]{2,1,0:T(8,128)(2,1)}, u32[]{:S(2)}, u32[]{:S(2)}) %all-to-all-start) | async-done | bytes 1572896 | tf_op jit(solution)/shard_map/all_to_all | solution.py:207
  156.8 2.2 %shard_map.91 = bf16[32,1536]{1,0:T(8,128)(2,1)} custom-call(bf16[16,32,1536]{2,1,0:T(8,128)(2,1)} %all-to-all-done.refs_0_, bf16[16,128]{1,0:T(8,128)(2,1)S(1)} %slice_bitcast_fusion.refs_1_), custom_call_target="tpu_custom_call" | custom-call | flops 1048576 | bytes 2097152 | tf_op jit(solution)/shard_map/pallas_call | solution.py:37
  159.1 6.4 %all-to-all-start.1 = ((bf16[4,8,1536]{2,1,0:T(8,128)(2,1)}), bf16[4,8,1536]{2,1,0:T(8,128)(2,1)S(1)}, u32[]{:S(2)}, u32[]{:S(2)}) async-start(bf16[4,8,1536]{2,1,0:T(8,128)(2,1)} %bitcast.9), calls=%async_computation.1 | async-start | bytes 196608 | tf_op jit(solution)/shard_map/all_to_all | solution.py:216
  165.5 1.1 copy-done.2
  166.6 1.1 copy-done.4
  167.7 2.0 %shard_map.93 = f32[9,128,128]{2,1,0:T(8,128)} custom-call(s32[9]{0:T(128)S(1)} %copy-done.8, bf16[8,64,768]{2,1,0:T(8,128)(2,1)S(1)} %bitcast.15, bf16[4,64,1536]{2,1,0:T(8,128)(2,1)S(1)} %all_gather.17.refs_3_.refs_2_, bf16[4,64,1536]{2,1,0:T(8,128)(2,1)S(1)} %copy-done.2, bf16[4,64,1536]{2,1,0:T(8,128)(2,1)S(1)} %copy-done.4, ...), custom_call_target="tpu_custom_call" | custom-call | flops 603979776 | bytes 4194304 | tf_op jit(solution)/shard_map/pallas_call | solution.py:37
  169.7 2.0 %shard_map.92 = f32[9,128,128]{2,1,0:T(8,128)} custom-call(s32[9]{0:T(128)S(1)} %copy-done.7, bf16[8,64,768]{2,1,0:T(8,128)(2,1)S(1)} %bitcast.13, bf16[4,64,1536]{2,1,0:T(8,128)(2,1)S(1)} %all_gather.17.refs_3_.refs_2_, bf16[4,64,1536]{2,1,0:T(8,128)(2,1)S(1)} %copy-done.2, bf16[4,64,1536]{2,1,0:T(8,128)(2,1)S(1)} %copy-done.4, ...), custom_call_target="tpu_custom_call" | custom-call | flops 603979776 | bytes 4194304 | tf_op jit(solution)/shard_map/pallas_call | solution.py:37
  171.7 6.6 %all-to-all-done.1 = bf16[4,8,1536]{2,1,0:T(8,128)(2,1)S(1)} async-done(((bf16[4,8,1536]{2,1,0:T(8,128)(2,1)}), bf16[4,8,1536]{2,1,0:T(8,128)(2,1)S(1)}, u32[]{:S(2)}, u32[]{:S(2)}) %all-to-all-start.1) | async-done | bytes 98336 | tf_op jit(solution)/shard_map/all_to_all | solution.py:216
  (30 shorter events, 5.2 us)
Async XLA Ops:
  0.6 53.5 %copy-start.6 = (bf16[9,128,128]{2,1,0:T(8,128)(2,1)S(1)}, bf16[9,128,128]{2,1,0:T(8,128)(2,1)}, u32[]{:S(2)}) copy-start(bf16[9,128,128]{2,1,0:T(8,128)(2,1)} %refs_5_.1) | copy-start | bytes 884740
  0.6 53.5 %copy-start.8 = (s32[9]{0:T(128)S(1)}, s32[9]{0:T(128)}, u32[]{:S(2)}) copy-start(s32[9]{0:T(128)} %refs_0_.9) | copy-start | bytes 112
  0.7 53.5 %copy-start.5 = (bf16[9,128,128]{2,1,0:T(8,128)(2,1)S(1)}, bf16[9,128,128]{2,1,0:T(8,128)(2,1)}, u32[]{:S(2)}) copy-start(bf16[9,128,128]{2,1,0:T(8,128)(2,1)} %refs_3_.1) | copy-start | bytes 884740
  0.7 53.5 %copy-start.7 = (s32[9]{0:T(128)S(1)}, s32[9]{0:T(128)}, u32[]{:S(2)}) copy-start(s32[9]{0:T(128)} %refs_0_.8) | copy-start | bytes 112
  37.2 15.4 %collective-permute-start = (bf16[4,64,1536]{2,1,0:T(8,128)(2,1)S(1)}, bf16[4,64,1536]{2,1,0:T(8,128)(2,1)S(1)}, u32[]{:S(2)}, u32[]{:S(2)}) collective-permute-start(bf16[4,64,1536]{2,1,0:T(8,128)(2,1)S(1)} %all_gather.17.refs_3_.refs_2_), channel_id=1, source_target_pairs={{0,8},{8,16},{16,24},{24,0},{1,9},{9,17},{17,25},{25,1},{2,10},{10... | collective-permute-start | bytes 2359304 | tf_op jit(solution)/shard_map/ppermute | solution.py:32
  40.4 13.8 %collective-permute-start.1 = (bf16[4,64,1536]{2,1,0:T(8,128)(2,1)S(1)}, bf16[4,64,1536]{2,1,0:T(8,128)(2,1)S(1)}, u32[]{:S(2)}, u32[]{:S(2)}) collective-permute-start(bf16[4,64,1536]{2,1,0:T(8,128)(2,1)S(1)} %all_gather.17.refs_3_.refs_2_), channel_id=1, source_target_pairs={{0,24},{8,0},{16,8},{24,16},{1,25},{9,1},{17,9},{25,17},{2,26},{10... | collective-permute-start | bytes 2359304 | tf_op jit(solution)/shard_map/ppermute | solution.py:32
  52.6 3.1 %copy-start.1 = (bf16[4,64,1536]{2,1,0:T(8,128)(2,1)}, bf16[4,64,1536]{2,1,0:T(8,128)(2,1)S(1)}, u32[]{:S(2)}) copy-start(bf16[4,64,1536]{2,1,0:T(8,128)(2,1)S(1)} %collective-permute-done.refs_4_.refs_3_) | copy-start | bytes 2359300
  54.2 1.5 copy-start.3
  55.7 14.5 %collective-permute-start.2 = (f32[192,1536]{1,0:T(8,128)S(1)}, f32[192,1536]{1,0:T(8,128)S(1)}, u32[]{:S(2)}, u32[]{:S(2)}) collective-permute-start(f32[192,1536]{1,0:T(8,128)S(1)} %get-tuple-element.18), channel_id=1, source_target_pairs={{0,1},{1,0},{2,3},{3,2},{4,5},{5,4},{6,7},{7,6},{8,9},{9,8},{10,11... | collective-permute-start | bytes 3538952 | tf_op jit(solution)/shard_map/ppermute | solution.py:32
  65.7 22.6 %collective-permute-start.6 = (bf16[4,64,1536]{2,1,0:T(8,128)(2,1)S(1)}, bf16[4,64,1536]{2,1,0:T(8,128)(2,1)S(1)}, u32[]{:S(2)}, u32[]{:S(2)}) collective-permute-start(bf16[4,64,1536]{2,1,0:T(8,128)(2,1)S(1)} %all_gather.17.refs_3_.refs_2_), channel_id=1, source_target_pairs={{0,16},{8,24},{16,0},{24,8},{1,17},{9,25},{17,1},{25,9},{2,18},{10... | collective-permute-start | bytes 2359304 | tf_op jit(solution)/shard_map/ppermute | solution.py:32
  70.9 17.4 %collective-permute-start.3 = (bf16[48,1536]{1,0:T(8,128)(2,1)S(1)}, bf16[48,1536]{1,0:T(8,128)(2,1)S(1)}, u32[]{:S(2)}, u32[]{:S(2)}) collective-permute-start(bf16[48,1536]{1,0:T(8,128)(2,1)S(1)} %get-tuple-element.20), channel_id=1, source_target_pairs={{0,2},{2,4},{4,6},{6,0},{1,3},{3,5},{5,7},{7,1},{8,10},{10,12},{12... | collective-permute-start | bytes 442376 | tf_op jit(solution)/shard_map/ppermute | solution.py:32
  73.2 15.1 %collective-permute-start.4 = (bf16[48,1536]{1,0:T(8,128)(2,1)S(1)}, bf16[48,1536]{1,0:T(8,128)(2,1)S(1)}, u32[]{:S(2)}, u32[]{:S(2)}) collective-permute-start(bf16[48,1536]{1,0:T(8,128)(2,1)S(1)} %get-tuple-element.21), channel_id=1, source_target_pairs={{0,4},{2,6},{4,0},{6,2},{1,5},{3,7},{5,1},{7,3},{8,12},{10,14},{12... | collective-permute-start | bytes 442376 | tf_op jit(solution)/shard_map/ppermute | solution.py:32
  76.6 11.7 %collective-permute-start.5 = (bf16[48,1536]{1,0:T(8,128)(2,1)S(1)}, bf16[48,1536]{1,0:T(8,128)(2,1)S(1)}, u32[]{:S(2)}, u32[]{:S(2)}) collective-permute-start(bf16[48,1536]{1,0:T(8,128)(2,1)S(1)} %get-tuple-element.22), channel_id=1, source_target_pairs={{0,6},{2,0},{4,2},{6,4},{1,7},{3,1},{5,3},{7,5},{8,14},{10,8},{12,... | collective-permute-start | bytes 442376 | tf_op jit(solution)/shard_map/ppermute | solution.py:32
  89.3 4.0 %collective-permute-start.7 = (f32[64,1536]{1,0:T(8,128)S(1)}, f32[64,1536]{1,0:T(8,128)S(1)}, u32[]{:S(2)}, u32[]{:S(2)}) collective-permute-start(f32[64,1536]{1,0:T(8,128)S(1)} %get-tuple-element.24), channel_id=1, source_target_pairs={{0,1},{1,0},{2,3},{3,2},{4,5},{5,4},{6,7},{7,6},{8,9},{9,8},{10,11... | collective-permute-start | bytes 1179656 | tf_op jit(solution)/shard_map/ppermute | solution.py:32
  93.9 8.5 %collective-permute-start.10 = (bf16[16,1536]{1,0:T(8,128)(2,1)S(1)}, bf16[16,1536]{1,0:T(8,128)(2,1)S(1)}, u32[]{:S(2)}, u32[]{:S(2)}) collective-permute-start(bf16[16,1536]{1,0:T(8,128)(2,1)S(1)} %get-tuple-element.28), channel_id=1, source_target_pairs={{0,6},{2,0},{4,2},{6,4},{1,7},{3,1},{5,3},{7,5},{8,14},{10,8},{12,... | collective-permute-start | bytes 147464 | tf_op jit(solution)/shard_map/ppermute | solution.py:32
  97.8 6.6 %collective-permute-start.8 = (bf16[16,1536]{1,0:T(8,128)(2,1)S(1)}, bf16[16,1536]{1,0:T(8,128)(2,1)S(1)}, u32[]{:S(2)}, u32[]{:S(2)}) collective-permute-start(bf16[16,1536]{1,0:T(8,128)(2,1)S(1)} %get-tuple-element.26), channel_id=1, source_target_pairs={{0,2},{2,4},{4,6},{6,0},{1,3},{3,5},{5,7},{7,1},{8,10},{10,12},{12... | collective-permute-start | bytes 147464 | tf_op jit(solution)/shard_map/ppermute | solution.py:32
  99.7 7.2 %collective-permute-start.9 = (bf16[16,1536]{1,0:T(8,128)(2,1)S(1)}, bf16[16,1536]{1,0:T(8,128)(2,1)S(1)}, u32[]{:S(2)}, u32[]{:S(2)}) collective-permute-start(bf16[16,1536]{1,0:T(8,128)(2,1)S(1)} %get-tuple-element.27), channel_id=1, source_target_pairs={{0,4},{2,6},{4,0},{6,2},{1,5},{3,7},{5,1},{7,3},{8,12},{10,14},{12... | collective-permute-start | bytes 147464 | tf_op jit(solution)/shard_map/ppermute | solution.py:32
  125.0 1.1 copy-start
  126.2 30.6 %all-to-all-start = ((bf16[16,32,1536]{2,1,0:T(8,128)(2,1)}), bf16[16,32,1536]{2,1,0:T(8,128)(2,1)}, u32[]{:S(2)}, u32[]{:S(2)}) async-start(bf16[16,32,1536]{2,1,0:T(8,128)(2,1)} %copy-done), calls=%async_computation | async-start | bytes 3145728 | tf_op jit(solution)/shard_map/all_to_all | solution.py:207
  159.1 19.2 %all-to-all-start.1 = ((bf16[4,8,1536]{2,1,0:T(8,128)(2,1)}), bf16[4,8,1536]{2,1,0:T(8,128)(2,1)S(1)}, u32[]{:S(2)}, u32[]{:S(2)}) async-start(bf16[4,8,1536]{2,1,0:T(8,128)(2,1)} %bitcast.9), calls=%async_computation.1 | async-start | bytes 196608 | tf_op jit(solution)/shard_map/all_to_all | solution.py:216
  165.5 1.1 copy-start.2
  166.6 1.1 copy-start.4

commit v5 on v4

--- a/solution.py
+++ b/solution.py
@@ -17,7 +17,7 @@
 NB = 9
 Q = TOK // 8
 STEPS = (0, 1, 3, 2)
-FIRST = 3 * Q // 4
+FIRST = Q // 4
 W1_COLS = 384
 W2_COLS = 96
 SIZE = {"x": 4, "y": 4, "zh": 4, "zl": 4, "core": 2}
@@ -222,12 +222,11 @@
     near = lax.all_gather(jnp.concatenate([inputs, cotangent], axis=0), "zh", axis=0)
     near = near.reshape(4, 2, 8, WT).swapaxes(0, 1).reshape(64, WT)
     along = lax.all_gather(near, "x", axis=0)
-    parts = [along, shift(along, "y", 1), shift(along, "y", 3)]
+    parts = [along] + [shift(along, "y", step) for step in STEPS[1:]]
     weights = (w1_blocks, w2_blocks)
-    parts.append(shift(along, "y", 2))
-    keep, send = product_terms(ids, w1_where, w2_where, parts[:3], *weights)
+    keep, send = product_terms(ids, w1_where, w2_where, parts[:1], *weights)
     first = column_sums(ids, keep, shift(send, "core", 1))
-    keep, send = product_terms(ids, w1_where, w2_where, parts[3:], *weights, after=first[1:])
+    keep, send = product_terms(ids, w1_where, w2_where, parts[1:], *weights, after=first[1:])
     second = column_sums(ids, keep, shift(send, "core", 1))
     activated, hidden_grad = call(
         gelu_body, (*first, *second), [((Q, HT), BF)] * 2, flops=1 << 22, nbytes=1 << 20

time: 180 us -> 176 us (0.978)
  waiting for transfers between devices: 40 us -> 30 us
  local copies, waits for them, and re-layouts: 3.44 us -> 7.61 us
  starting transfers between devices: 53.5 us -> 57.1 us
    ppermute x11, waiting for transfers between devices: 24.4 us -> 18 us  [shift(): return lax.ppermute(value, axis, [(i, (i + step) % n) for i in range(n)])]
    unnamed x18 -> x28, local copies, waits for them, and re-layouts: 3.42 us -> 7.6 us
    ppermute x11, starting transfers between devices: 41.3 us -> 44 us  [shift(): return lax.ppermute(value, axis, [(i, (i + step) % n) for i in range(n)])]
    all_to_all x1, waiting for transfers between devices: 6.55 us -> 4.17 us  [row_reduce(): last = lax.all_to_all(mine, 'zh', 0, 0, tiled=True)]
where the time goes in v5:
time: 176 us; the launch traced here: 175 us
  blocking collectives  67.8 us (39%)
  starting transfers between devices  57.1 us (32%)
  waiting for transfers between devices  30 us (17%)
  Pallas kernels  10.2 us (6%)
  local copies, waits for them, and re-layouts  7.61 us (4%)
    ppermute x11, starting transfers between devices, shift(): return lax.ppermute(value, axis, [(i, (i + step) % n) for i in range(n)])  44 us
    all_gather x1, blocking collectives, shards(): lax.all_gather(jnp.concatenate([inputs, cotangent], axis=0), 'zh', axis=0)  24.5 us
    ppermute x11, waiting for transfers between devices, shift(): return lax.ppermute(value, axis, [(i, (i + step) % n) for i in range(n)])  18 us
    all_gather x1, blocking collectives, shards(): lax.all_gather(activated, ('zl', 'core'), axis=0, tiled=True)  16.1 us
    all_gather x1, blocking collectives, shards(): lax.all_gather(hidden_grad, ('zl', 'core'), axis=0, tiled=True)  16 us
    all_gather x1, blocking collectives, shards(): along = lax.all_gather(near, 'x', axis=0)  11.1 us
    pallas_call x9, Pallas kernels, call(): pl.pallas_call(lambda *refs: body(*refs[:n], *refs[m:]), out_shape=[jax.S...  10.2 us
    all_to_all x1, waiting for transfers between devices, row_reduce(): parts = lax.all_to_all(partial, ('y', 'x'), 0, 0, tiled=True)  7.83 us
  transfers between devices with their start and end apart: 13, of which 8 were waited for; matrix products, arithmetic and copies ran while one was open for 0% of the time, Pallas kernels for 3%

profile of v5, /device:TPU:1, one launch (start us, length us, event | category | flops | bytes accessed | tf_op | source)
XLA Modules:
  0.0 175.1 jit_solution(965873049944734648)
XLA Ops:
  1.5 24.5 %all-gather = bf16[64,1536]{1,0:T(8,128)(2,1)S(1)} all-gather(bf16[16,1536]{1,0:T(8,128)(2,1)S(1)} %pad_maximum_fusion), channel_id=2, replica_groups=mesh['x'=4,'zh'=4,'y'=4,'zl'=4,'core'=2] {'zh'}, dimensions={0}, use_global_device_ids=true | all-gather | bytes 245760 | tf_op jit(solution)/shard_map/all_gather | solution.py:222
  26.0 11.1 %all_gather.17.refs_3_.refs_2_ = bf16[4,64,1536]{2,1,0:T(8,128)(2,1)S(1)} all-gather(bf16[1,64,1536]{2,1,0:T(8,128)(2,1)S(1)} %bitcast.17), channel_id=1, replica_groups=mesh['x'=4,'zh'=4,'y'=4,'zl'=4,'core'=2] {'x'}, dimensions={0}, use_global_device_ids=true | all-gather | bytes 983040 | tf_op jit(solution)/shard_map/all_gather | solution.py:224
  37.1 3.2 %collective-permute-start.4 = (bf16[4,64,1536]{2,1,0:T(8,128)(2,1)S(1)}, bf16[4,64,1536]{2,1,0:T(8,128)(2,1)S(1)}, u32[]{:S(2)}, u32[]{:S(2)}) collective-permute-start(bf16[4,64,1536]{2,1,0:T(8,128)(2,1)S(1)} %all_gather.17.refs_3_.refs_2_), channel_id=1, source_target_pairs={{0,8},{8,16},{16,24},{24,0},{1,9},{9,17},{17,25},{25,1},{2,10},{10... | collective-permute-start | bytes 2359304 | tf_op jit(solution)/shard_map/ppermute | solution.py:32
  40.3 3.4 %collective-permute-start.5 = (bf16[4,64,1536]{2,1,0:T(8,128)(2,1)S(1)}, bf16[4,64,1536]{2,1,0:T(8,128)(2,1)S(1)}, u32[]{:S(2)}, u32[]{:S(2)}) collective-permute-start(bf16[4,64,1536]{2,1,0:T(8,128)(2,1)S(1)} %all_gather.17.refs_3_.refs_2_), channel_id=1, source_target_pairs={{0,24},{8,0},{16,8},{24,16},{1,25},{9,1},{17,9},{25,17},{2,26},{10... | collective-permute-start | bytes 2359304 | tf_op jit(solution)/shard_map/ppermute | solution.py:32
  43.7 3.5 %collective-permute-start.6 = (bf16[4,64,1536]{2,1,0:T(8,128)(2,1)S(1)}, bf16[4,64,1536]{2,1,0:T(8,128)(2,1)S(1)}, u32[]{:S(2)}, u32[]{:S(2)}) collective-permute-start(bf16[4,64,1536]{2,1,0:T(8,128)(2,1)S(1)} %all_gather.17.refs_3_.refs_2_), channel_id=1, source_target_pairs={{0,16},{8,24},{16,0},{24,8},{1,17},{9,25},{17,1},{25,9},{2,18},{10... | collective-permute-start | bytes 2359304 | tf_op jit(solution)/shard_map/ppermute | solution.py:32
  49.4 9.6 %collective-permute-start = (f32[64,1536]{1,0:T(8,128)S(1)}, f32[64,1536]{1,0:T(8,128)S(1)}, u32[]{:S(2)}, u32[]{:S(2)}) collective-permute-start(f32[64,1536]{1,0:T(8,128)S(1)} %get-tuple-element.18), channel_id=1, source_target_pairs={{0,1},{1,0},{2,3},{3,2},{4,5},{5,4},{6,7},{7,6},{8,9},{9,8},{10,11... | collective-permute-start | bytes 1179656 | tf_op jit(solution)/shard_map/ppermute | solution.py:32
  58.9 1.3 collective-permute-done.refs_2_
  60.8 2.5 %collective-permute-start.1 = (bf16[16,1536]{1,0:T(8,128)(2,1)S(1)}, bf16[16,1536]{1,0:T(8,128)(2,1)S(1)}, u32[]{:S(2)}, u32[]{:S(2)}) collective-permute-start(bf16[16,1536]{1,0:T(8,128)(2,1)S(1)} %get-tuple-element.20), channel_id=1, source_target_pairs={{0,2},{2,4},{4,6},{6,0},{1,3},{3,5},{5,7},{7,1},{8,10},{10,12},{12... | collective-permute-start | bytes 147464 | tf_op jit(solution)/shard_map/ppermute | solution.py:32
  63.4 3.2 %collective-permute-start.2 = (bf16[16,1536]{1,0:T(8,128)(2,1)S(1)}, bf16[16,1536]{1,0:T(8,128)(2,1)S(1)}, u32[]{:S(2)}, u32[]{:S(2)}) collective-permute-start(bf16[16,1536]{1,0:T(8,128)(2,1)S(1)} %get-tuple-element.21), channel_id=1, source_target_pairs={{0,4},{2,6},{4,0},{6,2},{1,5},{3,7},{5,1},{7,3},{8,12},{10,14},{12... | collective-permute-start | bytes 147464 | tf_op jit(solution)/shard_map/ppermute | solution.py:32
  67.5 2.9 %collective-permute-start.3 = (bf16[16,1536]{1,0:T(8,128)(2,1)S(1)}, bf16[16,1536]{1,0:T(8,128)(2,1)S(1)}, u32[]{:S(2)}, u32[]{:S(2)}) collective-permute-start(bf16[16,1536]{1,0:T(8,128)(2,1)S(1)} %get-tuple-element.22), channel_id=1, source_target_pairs={{0,6},{2,0},{4,2},{6,4},{1,7},{3,1},{5,3},{7,5},{8,14},{10,8},{12,... | collective-permute-start | bytes 147464 | tf_op jit(solution)/shard_map/ppermute | solution.py:32
  70.4 2.2 %collective-permute-done.3.refs_10_.refs_3_ = bf16[16,1536]{1,0:T(8,128)(2,1)S(1)} collective-permute-done((bf16[16,1536]{1,0:T(8,128)(2,1)S(1)}, bf16[16,1536]{1,0:T(8,128)(2,1)S(1)}, u32[]{:S(2)}, u32[]{:S(2)}) %collective-permute-start.3) | collective-permute-done | bytes 49184 | tf_op jit(solution)/shard_map/ppermute | solution.py:32
  72.6 1.5 shard_map.87
  74.2 7.5 %collective-permute-start.7 = (f32[192,1536]{1,0:T(8,128)S(1)}, f32[192,1536]{1,0:T(8,128)S(1)}, u32[]{:S(2)}, u32[]{:S(2)}) collective-permute-start(f32[192,1536]{1,0:T(8,128)S(1)} %get-tuple-element.24), channel_id=1, source_target_pairs={{0,1},{1,0},{2,3},{3,2},{4,5},{5,4},{6,7},{7,6},{8,9},{9,8},{10,11... | collective-permute-start | bytes 3538952 | tf_op jit(solution)/shard_map/ppermute | solution.py:32
  81.7 2.5 %collective-permute-done.7.refs_2_ = f32[192,1536]{1,0:T(8,128)S(1)} collective-permute-done((f32[192,1536]{1,0:T(8,128)S(1)}, f32[192,1536]{1,0:T(8,128)S(1)}, u32[]{:S(2)}, u32[]{:S(2)}) %collective-permute-start.7) | collective-permute-done | bytes 1179680 | tf_op jit(solution)/shard_map/ppermute | solution.py:32
  84.8 3.5 %collective-permute-start.10 = (bf16[48,1536]{1,0:T(8,128)(2,1)S(1)}, bf16[48,1536]{1,0:T(8,128)(2,1)S(1)}, u32[]{:S(2)}, u32[]{:S(2)}) collective-permute-start(bf16[48,1536]{1,0:T(8,128)(2,1)S(1)} %get-tuple-element.28), channel_id=1, source_target_pairs={{0,6},{2,0},{4,2},{6,4},{1,7},{3,1},{5,3},{7,5},{8,14},{10,8},{12,... | collective-permute-start | bytes 442376 | tf_op jit(solution)/shard_map/ppermute | solution.py:32
  88.4 1.9 %collective-permute-start.8 = (bf16[48,1536]{1,0:T(8,128)(2,1)S(1)}, bf16[48,1536]{1,0:T(8,128)(2,1)S(1)}, u32[]{:S(2)}, u32[]{:S(2)}) collective-permute-start(bf16[48,1536]{1,0:T(8,128)(2,1)S(1)} %get-tuple-element.26), channel_id=1, source_target_pairs={{0,2},{2,4},{4,6},{6,0},{1,3},{3,5},{5,7},{7,1},{8,10},{10,12},{12... | collective-permute-start | bytes 442376 | tf_op jit(solution)/shard_map/ppermute | solution.py:32
  90.3 2.8 %collective-permute-start.9 = (bf16[48,1536]{1,0:T(8,128)(2,1)S(1)}, bf16[48,1536]{1,0:T(8,128)(2,1)S(1)}, u32[]{:S(2)}, u32[]{:S(2)}) collective-permute-start(bf16[48,1536]{1,0:T(8,128)(2,1)S(1)} %get-tuple-element.27), channel_id=1, source_target_pairs={{0,4},{2,6},{4,0},{6,2},{1,5},{3,7},{5,1},{7,3},{8,12},{10,14},{12... | collective-permute-start | bytes 442376 | tf_op jit(solution)/shard_map/ppermute | solution.py:32
  93.1 3.7 %collective-permute-done.8.refs_5_ = bf16[48,1536]{1,0:T(8,128)(2,1)S(1)} collective-permute-done((bf16[48,1536]{1,0:T(8,128)(2,1)S(1)}, bf16[48,1536]{1,0:T(8,128)(2,1)S(1)}, u32[]{:S(2)}, u32[]{:S(2)}) %collective-permute-start.8) | collective-permute-done | bytes 147488 | tf_op jit(solution)/shard_map/ppermute | solution.py:32
  96.8 7.4 %collective-permute-done.9.refs_6_ = bf16[48,1536]{1,0:T(8,128)(2,1)S(1)} collective-permute-done((bf16[48,1536]{1,0:T(8,128)(2,1)S(1)}, bf16[48,1536]{1,0:T(8,128)(2,1)S(1)}, u32[]{:S(2)}, u32[]{:S(2)}) %collective-permute-start.9) | collective-permute-done | bytes 147488 | tf_op jit(solution)/shard_map/ppermute | solution.py:32
  104.4 16.0 %all_gather.18 = bf16[512,768]{1,0:T(8,128)(2,1)S(1)} all-gather(bf16[64,768]{1,0:T(8,128)(2,1)S(1)} %get-tuple-element.29), channel_id=1, replica_groups=mesh['x'=4,'zh'=4,'y'=4,'zl'=4,'core'=2] {'zl','core'}, dimensions={0}, use_global_device_ids=true | all-gather | bytes 884736 | tf_op jit(solution)/shard_map/all_gather | solution.py:234
  120.4 1.4 shard_map.90
  121.8 1.2 copy-done
  123.0 6.9 %all-to-all-start = ((bf16[16,32,1536]{2,1,0:T(8,128)(2,1)}), bf16[16,32,1536]{2,1,0:T(8,128)(2,1)S(1)}, u32[]{:S(2)}, u32[]{:S(2)}) async-start(bf16[16,32,1536]{2,1,0:T(8,128)(2,1)} %copy-done), calls=%async_computation | async-start | bytes 3145728 | tf_op jit(solution)/shard_map/all_to_all | solution.py:207
  129.9 16.1 %all_gather.19 = bf16[512,768]{1,0:T(8,128)(2,1)S(1)} all-gather(bf16[64,768]{1,0:T(8,128)(2,1)S(1)} %get-tuple-element.30), channel_id=1, replica_groups=mesh['x'=4,'zh'=4,'y'=4,'zl'=4,'core'=2] {'zl','core'}, dimensions={0}, use_global_device_ids=true | all-gather | bytes 884736 | tf_op jit(solution)/shard_map/all_gather | solution.py:235
  146.9 7.8 %all-to-all-done.refs_0_ = bf16[16,32,1536]{2,1,0:T(8,128)(2,1)S(1)} async-done(((bf16[16,32,1536]{2,1,0:T(8,128)(2,1)}), bf16[16,32,1536]{2,1,0:T(8,128)(2,1)S(1)}, u32[]{:S(2)}, u32[]{:S(2)}) %all-to-all-start) | async-done | bytes 1572896 | tf_op jit(solution)/shard_map/all_to_all | solution.py:207
  155.6 6.3 %all-to-all-start.1 = ((bf16[4,8,1536]{2,1,0:T(8,128)(2,1)}), bf16[4,8,1536]{2,1,0:T(8,128)(2,1)S(1)}, u32[]{:S(2)}, u32[]{:S(2)}) async-start(bf16[4,8,1536]{2,1,0:T(8,128)(2,1)} %bitcast.9), calls=%async_computation.1 | async-start | bytes 196608 | tf_op jit(solution)/shard_map/all_to_all | solution.py:216
  161.9 1.1 copy-done.2
  164.1 1.1 copy-done.6
  165.3 1.1 copy-done.8
  166.4 2.0 %shard_map.93 = f32[9,128,128]{2,1,0:T(8,128)} custom-call(s32[9]{0:T(128)S(1)} %copy-done.13, bf16[8,64,768]{2,1,0:T(8,128)(2,1)S(1)} %bitcast.15, bf16[4,64,1536]{2,1,0:T(8,128)(2,1)S(1)} %all_gather.17.refs_3_.refs_2_, bf16[4,64,1536]{2,1,0:T(8,128)(2,1)S(1)} %copy-done.4, bf16[4,64,1536]{2,1,0:T(8,128)(2,1)S(1)} %copy-done.6, ...), custom_call_target="tpu_custom_call" | custom-call | flops 603979776 | bytes 4194304 | tf_op jit(solution)/shard_map/pallas_call | solution.py:37
  168.4 2.0 %shard_map.92 = f32[9,128,128]{2,1,0:T(8,128)} custom-call(s32[9]{0:T(128)S(1)} %copy-done.12, bf16[8,64,768]{2,1,0:T(8,128)(2,1)S(1)} %bitcast.13, bf16[4,64,1536]{2,1,0:T(8,128)(2,1)S(1)} %all_gather.17.refs_3_.refs_2_, bf16[4,64,1536]{2,1,0:T(8,128)(2,1)S(1)} %copy-done.4, bf16[4,64,1536]{2,1,0:T(8,128)(2,1)S(1)} %copy-done.6, ...), custom_call_target="tpu_custom_call" | custom-call | flops 603979776 | bytes 4194304 | tf_op jit(solution)/shard_map/pallas_call | solution.py:37
  170.3 4.2 %all-to-all-done.1 = bf16[4,8,1536]{2,1,0:T(8,128)(2,1)S(1)} async-done(((bf16[4,8,1536]{2,1,0:T(8,128)(2,1)}), bf16[4,8,1536]{2,1,0:T(8,128)(2,1)S(1)}, u32[]{:S(2)}, u32[]{:S(2)}) %all-to-all-start.1) | async-done | bytes 98336 | tf_op jit(solution)/shard_map/all_to_all | solution.py:216
  (40 shorter events, 8.8 us)
Async XLA Ops:
  0.6 46.7 %copy-start.13 = (s32[9]{0:T(128)S(1)}, s32[9]{0:T(128)}, u32[]{:S(2)}) copy-start(s32[9]{0:T(128)} %refs_0_.9) | copy-start | bytes 112
  0.6 46.7 %copy-start.9 = (bf16[9,128,128]{2,1,0:T(8,128)(2,1)S(1)}, bf16[9,128,128]{2,1,0:T(8,128)(2,1)}, u32[]{:S(2)}) copy-start(bf16[9,128,128]{2,1,0:T(8,128)(2,1)} %refs_3_.1) | copy-start | bytes 884740
  0.7 46.7 %copy-start.12 = (s32[9]{0:T(128)S(1)}, s32[9]{0:T(128)}, u32[]{:S(2)}) copy-start(s32[9]{0:T(128)} %refs_0_.8) | copy-start | bytes 112
  37.1 35.5 %collective-permute-start.4 = (bf16[4,64,1536]{2,1,0:T(8,128)(2,1)S(1)}, bf16[4,64,1536]{2,1,0:T(8,128)(2,1)S(1)}, u32[]{:S(2)}, u32[]{:S(2)}) collective-permute-start(bf16[4,64,1536]{2,1,0:T(8,128)(2,1)S(1)} %all_gather.17.refs_3_.refs_2_), channel_id=1, source_target_pairs={{0,8},{8,16},{16,24},{24,0},{1,9},{9,17},{17,25},{25,1},{2,10},{10... | collective-permute-start | bytes 2359304 | tf_op jit(solution)/shard_map/ppermute | solution.py:32
  40.3 32.3 %collective-permute-start.5 = (bf16[4,64,1536]{2,1,0:T(8,128)(2,1)S(1)}, bf16[4,64,1536]{2,1,0:T(8,128)(2,1)S(1)}, u32[]{:S(2)}, u32[]{:S(2)}) collective-permute-start(bf16[4,64,1536]{2,1,0:T(8,128)(2,1)S(1)} %all_gather.17.refs_3_.refs_2_), channel_id=1, source_target_pairs={{0,24},{8,0},{16,8},{24,16},{1,25},{9,1},{17,9},{25,17},{2,26},{10... | collective-permute-start | bytes 2359304 | tf_op jit(solution)/shard_map/ppermute | solution.py:32
  43.7 28.9 %collective-permute-start.6 = (bf16[4,64,1536]{2,1,0:T(8,128)(2,1)S(1)}, bf16[4,64,1536]{2,1,0:T(8,128)(2,1)S(1)}, u32[]{:S(2)}, u32[]{:S(2)}) collective-permute-start(bf16[4,64,1536]{2,1,0:T(8,128)(2,1)S(1)} %all_gather.17.refs_3_.refs_2_), channel_id=1, source_target_pairs={{0,16},{8,24},{16,0},{24,8},{1,17},{9,25},{17,1},{25,9},{2,18},{10... | collective-permute-start | bytes 2359304 | tf_op jit(solution)/shard_map/ppermute | solution.py:32
  47.3 1.0 copy-start.10
  48.3 24.3 %copy-start.11 = (bf16[9,128,128]{2,1,0:T(8,128)(2,1)S(1)}, bf16[9,128,128]{2,1,0:T(8,128)(2,1)}, u32[]{:S(2)}) copy-start(bf16[9,128,128]{2,1,0:T(8,128)(2,1)} %refs_7_.1) | copy-start | bytes 884740
  49.4 10.9 %collective-permute-start = (f32[64,1536]{1,0:T(8,128)S(1)}, f32[64,1536]{1,0:T(8,128)S(1)}, u32[]{:S(2)}, u32[]{:S(2)}) collective-permute-start(f32[64,1536]{1,0:T(8,128)S(1)} %get-tuple-element.18), channel_id=1, source_target_pairs={{0,1},{1,0},{2,3},{3,2},{4,5},{5,4},{6,7},{7,6},{8,9},{9,8},{10,11... | collective-permute-start | bytes 1179656 | tf_op jit(solution)/shard_map/ppermute | solution.py:32
  60.8 6.6 %collective-permute-start.1 = (bf16[16,1536]{1,0:T(8,128)(2,1)S(1)}, bf16[16,1536]{1,0:T(8,128)(2,1)S(1)}, u32[]{:S(2)}, u32[]{:S(2)}) collective-permute-start(bf16[16,1536]{1,0:T(8,128)(2,1)S(1)} %get-tuple-element.20), channel_id=1, source_target_pairs={{0,2},{2,4},{4,6},{6,0},{1,3},{3,5},{5,7},{7,1},{8,10},{10,12},{12... | collective-permute-start | bytes 147464 | tf_op jit(solution)/shard_map/ppermute | solution.py:32
  63.4 7.0 %collective-permute-start.2 = (bf16[16,1536]{1,0:T(8,128)(2,1)S(1)}, bf16[16,1536]{1,0:T(8,128)(2,1)S(1)}, u32[]{:S(2)}, u32[]{:S(2)}) collective-permute-start(bf16[16,1536]{1,0:T(8,128)(2,1)S(1)} %get-tuple-element.21), channel_id=1, source_target_pairs={{0,4},{2,6},{4,0},{6,2},{1,5},{3,7},{5,1},{7,3},{8,12},{10,14},{12... | collective-permute-start | bytes 147464 | tf_op jit(solution)/shard_map/ppermute | solution.py:32
  67.5 5.1 %collective-permute-start.3 = (bf16[16,1536]{1,0:T(8,128)(2,1)S(1)}, bf16[16,1536]{1,0:T(8,128)(2,1)S(1)}, u32[]{:S(2)}, u32[]{:S(2)}) collective-permute-start(bf16[16,1536]{1,0:T(8,128)(2,1)S(1)} %get-tuple-element.22), channel_id=1, source_target_pairs={{0,6},{2,0},{4,2},{6,4},{1,7},{3,1},{5,3},{7,5},{8,14},{10,8},{12,... | collective-permute-start | bytes 147464 | tf_op jit(solution)/shard_map/ppermute | solution.py:32
  72.6 1.6 copy-start.3
  72.6 1.6 copy-start.5
  72.6 1.6 copy-start.7
  74.2 10.0 %collective-permute-start.7 = (f32[192,1536]{1,0:T(8,128)S(1)}, f32[192,1536]{1,0:T(8,128)S(1)}, u32[]{:S(2)}, u32[]{:S(2)}) collective-permute-start(f32[192,1536]{1,0:T(8,128)S(1)} %get-tuple-element.24), channel_id=1, source_target_pairs={{0,1},{1,0},{2,3},{3,2},{4,5},{5,4},{6,7},{7,6},{8,9},{9,8},{10,11... | collective-permute-start | bytes 3538952 | tf_op jit(solution)/shard_map/ppermute | solution.py:32
  84.8 8.2 %collective-permute-start.10 = (bf16[48,1536]{1,0:T(8,128)(2,1)S(1)}, bf16[48,1536]{1,0:T(8,128)(2,1)S(1)}, u32[]{:S(2)}, u32[]{:S(2)}) collective-permute-start(bf16[48,1536]{1,0:T(8,128)(2,1)S(1)} %get-tuple-element.28), channel_id=1, source_target_pairs={{0,6},{2,0},{4,2},{6,4},{1,7},{3,1},{5,3},{7,5},{8,14},{10,8},{12,... | collective-permute-start | bytes 442376 | tf_op jit(solution)/shard_map/ppermute | solution.py:32
  88.4 8.4 %collective-permute-start.8 = (bf16[48,1536]{1,0:T(8,128)(2,1)S(1)}, bf16[48,1536]{1,0:T(8,128)(2,1)S(1)}, u32[]{:S(2)}, u32[]{:S(2)}) collective-permute-start(bf16[48,1536]{1,0:T(8,128)(2,1)S(1)} %get-tuple-element.26), channel_id=1, source_target_pairs={{0,2},{2,4},{4,6},{6,0},{1,3},{3,5},{5,7},{7,1},{8,10},{10,12},{12... | collective-permute-start | bytes 442376 | tf_op jit(solution)/shard_map/ppermute | solution.py:32
  90.3 13.9 %collective-permute-start.9 = (bf16[48,1536]{1,0:T(8,128)(2,1)S(1)}, bf16[48,1536]{1,0:T(8,128)(2,1)S(1)}, u32[]{:S(2)}, u32[]{:S(2)}) collective-permute-start(bf16[48,1536]{1,0:T(8,128)(2,1)S(1)} %get-tuple-element.27), channel_id=1, source_target_pairs={{0,4},{2,6},{4,0},{6,2},{1,5},{3,7},{5,1},{7,3},{8,12},{10,14},{12... | collective-permute-start | bytes 442376 | tf_op jit(solution)/shard_map/ppermute | solution.py:32
  121.8 1.2 copy-start
  123.0 31.7 %all-to-all-start = ((bf16[16,32,1536]{2,1,0:T(8,128)(2,1)}), bf16[16,32,1536]{2,1,0:T(8,128)(2,1)S(1)}, u32[]{:S(2)}, u32[]{:S(2)}) async-start(bf16[16,32,1536]{2,1,0:T(8,128)(2,1)} %copy-done), calls=%async_computation | async-start | bytes 3145728 | tf_op jit(solution)/shard_map/all_to_all | solution.py:207
  146.0 0.9 copy-start.1
  155.6 18.9 %all-to-all-start.1 = ((bf16[4,8,1536]{2,1,0:T(8,128)(2,1)}), bf16[4,8,1536]{2,1,0:T(8,128)(2,1)S(1)}, u32[]{:S(2)}, u32[]{:S(2)}) async-start(bf16[4,8,1536]{2,1,0:T(8,128)(2,1)} %bitcast.9), calls=%async_computation.1 | async-start | bytes 196608 | tf_op jit(solution)/shard_map/all_to_all | solution.py:216
  161.9 1.1 copy-start.2
  163.0 1.1 copy-start.4
  164.1 1.1 copy-start.6
  165.3 1.1 copy-start.8

commit v6 on v5

--- a/solution.py
+++ b/solution.py
@@ -32,14 +32,15 @@
     return lax.ppermute(value, axis, [(i, (i + step) % n) for i in range(n)])
 
 
-def call(body, ins, outs, scratch=(), flops=0, nbytes=0, vmem=16, after=()):
+def call(body, ins, outs, scratch=(), flops=0, nbytes=0, vmem=16, after=(), out_space=pltpu.VMEM):
     n, m = len(ins), len(ins) + len(after)
+    shape = pltpu.HBM if out_space == pltpu.HBM else jax.ShapeDtypeStruct
     return pl.pallas_call(
         lambda *refs: body(*refs[:n], *refs[m:]),
-        out_shape=[jax.ShapeDtypeStruct(s, d) for s, d in outs],
+        out_shape=[shape(s, d) for s, d in outs],
         in_specs=[SM if a.dtype == jnp.int32 else VM for a in ins]
         + [pl.BlockSpec(memory_space=pl.ANY)] * len(after),
-        out_specs=[VM] * len(outs),
+        out_specs=[pl.BlockSpec(memory_space=out_space)] * len(outs),
         scratch_shapes=list(scratch),
         compiler_params=pltpu.CompilerParams(vmem_limit_bytes=vmem << 20),
         cost_estimate=pl.CostEstimate(flops=flops, bytes_accessed=nbytes, transcendentals=0),
@@ -149,18 +150,25 @@
     )
 
 
-def input_grad_body(where, ids, hg, blocks, out, acc):
+def input_grad_body(where, ids, hg, blocks, out, acc, staged, sems):
     y = ids[2]
     acc[...] = jnp.zeros_like(acc)
     for b in range(NB):
         i, j = w1_pos(where[b])
         acc[i] += dot(tokens_of(hg, j), blocks[b], NT)
+    copies = []
     for q, step in enumerate(STEPS):
-        owner = lax.rem(y + 4 - step, 4) * 4
         for x in range(4):
             row = (4 * q + x) * 32
             for i in range(NI):
-                out[owner + x, :, i * BS : (i + 1) * BS] = acc[i, row : row + 32].astype(BF)
+                staged[4 * q + x, :, i * BS : (i + 1) * BS] = acc[i, row : row + 32].astype(BF)
+        owner = lax.rem(y + 4 - step, 4) * 4
+        copies.append(
+            pltpu.make_async_copy(staged.at[pl.ds(4 * q, 4)], out.at[pl.ds(owner, 4)], sems.at[q])
+        )
+        copies[-1].start()
+    for copy in copies:
+        copy.wait()
 
 
 def input_grad_partial(where, ids, hg, blocks):
@@ -168,7 +176,12 @@
         input_grad_body,
         (where, ids, hg, blocks),
         [((16, 32, WT), BF)],
-        [pltpu.VMEM((NI, TOK, BS), F32)],
+        [
+            pltpu.VMEM((NI, TOK, BS), F32),
+            pltpu.VMEM((16, 32, WT), BF),
+            pltpu.SemaphoreType.DMA((4,)),
+        ],
+        out_space=pltpu.HBM,
         flops=2 * NB * TOK * BS * BS * 4,
         nbytes=4 << 20,
     )
@@ -236,7 +249,7 @@
     partial = input_grad_partial(w1_where, ids, whole_hg, w1_blocks)
     w1_grad = block_grads(w1_pos, 0, w1_where, whole_hg, parts)
     w2_grad = block_grads(w2_pos, 32, w2_where, whole_av, parts)
-    input_grad = row_reduce(partial, (whole_av[0, :16, :BS],))
+    input_grad = row_reduce(partial, (whole_av[0, :16, :BS], w1_grad[0, :8]))
     return input_grad, w1_grad, w2_grad
 
 

time: 176 us -> 176 us (level)
  waiting for transfers between devices: 30 us -> 28 us
    all_to_all x1, waiting for transfers between devices: 7.83 us -> 2.91 us  [row_reduce(): parts = lax.all_to_all(partial, ('y', 'x'), 0, 0, tiled=True)]
    all_to_all x1, waiting for transfers between devices: 4.17 us -> 7.17 us  [row_reduce(): last = lax.all_to_all(mine, 'zh', 0, 0, tiled=True)]
    unnamed x28 -> x26, local copies, waits for them, and re-layouts: 7.6 us -> 7.77 us
where the time goes in v6:
time: 176 us; the launch traced here: 175 us
  blocking collectives  67.5 us (38%)
  starting transfers between devices  57.2 us (32%)
  waiting for transfers between devices  28 us (16%)
  Pallas kernels  11.3 us (6%)
  local copies, waits for them, and re-layouts  8.47 us (5%)
    ppermute x11, starting transfers between devices, shift(): return lax.ppermute(value, axis, [(i, (i + step) % n) for i in range(n)])  44 us
    all_gather x1, blocking collectives, shards(): lax.all_gather(jnp.concatenate([inputs, cotangent], axis=0), 'zh', axis=0)  24.5 us
    ppermute x11, waiting for transfers between devices, shift(): return lax.ppermute(value, axis, [(i, (i + step) % n) for i in range(n)])  18 us
    all_gather x1, blocking collectives, shards(): lax.all_gather(hidden_grad, ('zl', 'core'), axis=0, tiled=True)  16 us
    all_gather x1, blocking collectives, shards(): lax.all_gather(activated, ('zl', 'core'), axis=0, tiled=True)  15.9 us
    pallas_call x9, Pallas kernels, call(): pl.pallas_call(lambda *refs: body(*refs[:n], *refs[m:]), out_shape=[shape...  11.3 us
    all_gather x1, blocking collectives, shards(): along = lax.all_gather(near, 'x', axis=0)  11.1 us
    unnamed x26, local copies, waits for them, and re-layouts  7.77 us
  transfers between devices with their start and end apart: 13, of which 8 were waited for; matrix products, arithmetic and copies ran while one was open for 0% of the time, Pallas kernels for 3%

profile of v6, /device:TPU:1, one launch (start us, length us, event | category | flops | bytes accessed | tf_op | source)
XLA Modules:
  0.0 174.9 jit_solution(3946639395472000373)
XLA Ops:
  1.5 24.5 %all-gather = bf16[64,1536]{1,0:T(8,128)(2,1)S(1)} all-gather(bf16[16,1536]{1,0:T(8,128)(2,1)S(1)} %pad_maximum_fusion), channel_id=2, replica_groups=mesh['x'=4,'zh'=4,'y'=4,'zl'=4,'core'=2] {'zh'}, dimensions={0}, use_global_device_ids=true | all-gather | bytes 245760 | tf_op jit(solution)/shard_map/all_gather | solution.py:235
  26.0 11.1 %all_gather.17.refs_3_.refs_2_ = bf16[4,64,1536]{2,1,0:T(8,128)(2,1)S(1)} all-gather(bf16[1,64,1536]{2,1,0:T(8,128)(2,1)S(1)} %bitcast.19), channel_id=1, replica_groups=mesh['x'=4,'zh'=4,'y'=4,'zl'=4,'core'=2] {'x'}, dimensions={0}, use_global_device_ids=true | all-gather | bytes 983040 | tf_op jit(solution)/shard_map/all_gather | solution.py:237
  37.1 3.2 %collective-permute-start.4 = (bf16[4,64,1536]{2,1,0:T(8,128)(2,1)S(1)}, bf16[4,64,1536]{2,1,0:T(8,128)(2,1)S(1)}, u32[]{:S(2)}, u32[]{:S(2)}) collective-permute-start(bf16[4,64,1536]{2,1,0:T(8,128)(2,1)S(1)} %all_gather.17.refs_3_.refs_2_), channel_id=1, source_target_pairs={{0,8},{8,16},{16,24},{24,0},{1,9},{9,17},{17,25},{25,1},{2,10},{10... | collective-permute-start | bytes 2359304 | tf_op jit(solution)/shard_map/ppermute | solution.py:32
  40.3 3.4 %collective-permute-start.5 = (bf16[4,64,1536]{2,1,0:T(8,128)(2,1)S(1)}, bf16[4,64,1536]{2,1,0:T(8,128)(2,1)S(1)}, u32[]{:S(2)}, u32[]{:S(2)}) collective-permute-start(bf16[4,64,1536]{2,1,0:T(8,128)(2,1)S(1)} %all_gather.17.refs_3_.refs_2_), channel_id=1, source_target_pairs={{0,24},{8,0},{16,8},{24,16},{1,25},{9,1},{17,9},{25,17},{2,26},{10... | collective-permute-start | bytes 2359304 | tf_op jit(solution)/shard_map/ppermute | solution.py:32
  43.7 3.5 %collective-permute-start.6 = (bf16[4,64,1536]{2,1,0:T(8,128)(2,1)S(1)}, bf16[4,64,1536]{2,1,0:T(8,128)(2,1)S(1)}, u32[]{:S(2)}, u32[]{:S(2)}) collective-permute-start(bf16[4,64,1536]{2,1,0:T(8,128)(2,1)S(1)} %all_gather.17.refs_3_.refs_2_), channel_id=1, source_target_pairs={{0,16},{8,24},{16,0},{24,8},{1,17},{9,25},{17,1},{25,9},{2,18},{10... | collective-permute-start | bytes 2359304 | tf_op jit(solution)/shard_map/ppermute | solution.py:32
  49.4 9.6 %collective-permute-start = (f32[64,1536]{1,0:T(8,128)S(1)}, f32[64,1536]{1,0:T(8,128)S(1)}, u32[]{:S(2)}, u32[]{:S(2)}) collective-permute-start(f32[64,1536]{1,0:T(8,128)S(1)} %get-tuple-element.18), channel_id=1, source_target_pairs={{0,1},{1,0},{2,3},{3,2},{4,5},{5,4},{6,7},{7,6},{8,9},{9,8},{10,11... | collective-permute-start | bytes 1179656 | tf_op jit(solution)/shard_map/ppermute | solution.py:32
  58.9 1.3 collective-permute-done.refs_2_
  60.8 2.5 %collective-permute-start.1 = (bf16[16,1536]{1,0:T(8,128)(2,1)S(1)}, bf16[16,1536]{1,0:T(8,128)(2,1)S(1)}, u32[]{:S(2)}, u32[]{:S(2)}) collective-permute-start(bf16[16,1536]{1,0:T(8,128)(2,1)S(1)} %get-tuple-element.20), channel_id=1, source_target_pairs={{0,2},{2,4},{4,6},{6,0},{1,3},{3,5},{5,7},{7,1},{8,10},{10,12},{12... | collective-permute-start | bytes 147464 | tf_op jit(solution)/shard_map/ppermute | solution.py:32
  63.4 3.2 %collective-permute-start.2 = (bf16[16,1536]{1,0:T(8,128)(2,1)S(1)}, bf16[16,1536]{1,0:T(8,128)(2,1)S(1)}, u32[]{:S(2)}, u32[]{:S(2)}) collective-permute-start(bf16[16,1536]{1,0:T(8,128)(2,1)S(1)} %get-tuple-element.21), channel_id=1, source_target_pairs={{0,4},{2,6},{4,0},{6,2},{1,5},{3,7},{5,1},{7,3},{8,12},{10,14},{12... | collective-permute-start | bytes 147464 | tf_op jit(solution)/shard_map/ppermute | solution.py:32
  67.5 2.9 %collective-permute-start.3 = (bf16[16,1536]{1,0:T(8,128)(2,1)S(1)}, bf16[16,1536]{1,0:T(8,128)(2,1)S(1)}, u32[]{:S(2)}, u32[]{:S(2)}) collective-permute-start(bf16[16,1536]{1,0:T(8,128)(2,1)S(1)} %get-tuple-element.22), channel_id=1, source_target_pairs={{0,6},{2,0},{4,2},{6,4},{1,7},{3,1},{5,3},{7,5},{8,14},{10,8},{12,... | collective-permute-start | bytes 147464 | tf_op jit(solution)/shard_map/ppermute | solution.py:32
  70.4 2.2 %collective-permute-done.3.refs_10_.refs_3_ = bf16[16,1536]{1,0:T(8,128)(2,1)S(1)} collective-permute-done((bf16[16,1536]{1,0:T(8,128)(2,1)S(1)}, bf16[16,1536]{1,0:T(8,128)(2,1)S(1)}, u32[]{:S(2)}, u32[]{:S(2)}) %collective-permute-start.3) | collective-permute-done | bytes 49184 | tf_op jit(solution)/shard_map/ppermute | solution.py:32
  72.6 1.5 shard_map.87
  74.2 7.5 %collective-permute-start.7 = (f32[192,1536]{1,0:T(8,128)S(1)}, f32[192,1536]{1,0:T(8,128)S(1)}, u32[]{:S(2)}, u32[]{:S(2)}) collective-permute-start(f32[192,1536]{1,0:T(8,128)S(1)} %get-tuple-element.24), channel_id=1, source_target_pairs={{0,1},{1,0},{2,3},{3,2},{4,5},{5,4},{6,7},{7,6},{8,9},{9,8},{10,11... | collective-permute-start | bytes 3538952 | tf_op jit(solution)/shard_map/ppermute | solution.py:32
  81.8 2.5 %collective-permute-done.7.refs_2_ = f32[192,1536]{1,0:T(8,128)S(1)} collective-permute-done((f32[192,1536]{1,0:T(8,128)S(1)}, f32[192,1536]{1,0:T(8,128)S(1)}, u32[]{:S(2)}, u32[]{:S(2)}) %collective-permute-start.7) | collective-permute-done | bytes 1179680 | tf_op jit(solution)/shard_map/ppermute | solution.py:32
  84.9 3.5 %collective-permute-start.10 = (bf16[48,1536]{1,0:T(8,128)(2,1)S(1)}, bf16[48,1536]{1,0:T(8,128)(2,1)S(1)}, u32[]{:S(2)}, u32[]{:S(2)}) collective-permute-start(bf16[48,1536]{1,0:T(8,128)(2,1)S(1)} %get-tuple-element.28), channel_id=1, source_target_pairs={{0,6},{2,0},{4,2},{6,4},{1,7},{3,1},{5,3},{7,5},{8,14},{10,8},{12,... | collective-permute-start | bytes 442376 | tf_op jit(solution)/shard_map/ppermute | solution.py:32
  88.4 1.9 %collective-permute-start.8 = (bf16[48,1536]{1,0:T(8,128)(2,1)S(1)}, bf16[48,1536]{1,0:T(8,128)(2,1)S(1)}, u32[]{:S(2)}, u32[]{:S(2)}) collective-permute-start(bf16[48,1536]{1,0:T(8,128)(2,1)S(1)} %get-tuple-element.26), channel_id=1, source_target_pairs={{0,2},{2,4},{4,6},{6,0},{1,3},{3,5},{5,7},{7,1},{8,10},{10,12},{12... | collective-permute-start | bytes 442376 | tf_op jit(solution)/shard_map/ppermute | solution.py:32
  90.3 2.8 %collective-permute-start.9 = (bf16[48,1536]{1,0:T(8,128)(2,1)S(1)}, bf16[48,1536]{1,0:T(8,128)(2,1)S(1)}, u32[]{:S(2)}, u32[]{:S(2)}) collective-permute-start(bf16[48,1536]{1,0:T(8,128)(2,1)S(1)} %get-tuple-element.27), channel_id=1, source_target_pairs={{0,4},{2,6},{4,0},{6,2},{1,5},{3,7},{5,1},{7,3},{8,12},{10,14},{12... | collective-permute-start | bytes 442376 | tf_op jit(solution)/shard_map/ppermute | solution.py:32
  93.1 3.7 %collective-permute-done.8.refs_5_ = bf16[48,1536]{1,0:T(8,128)(2,1)S(1)} collective-permute-done((bf16[48,1536]{1,0:T(8,128)(2,1)S(1)}, bf16[48,1536]{1,0:T(8,128)(2,1)S(1)}, u32[]{:S(2)}, u32[]{:S(2)}) %collective-permute-start.8) | collective-permute-done | bytes 147488 | tf_op jit(solution)/shard_map/ppermute | solution.py:32
  96.8 7.4 %collective-permute-done.9.refs_6_ = bf16[48,1536]{1,0:T(8,128)(2,1)S(1)} collective-permute-done((bf16[48,1536]{1,0:T(8,128)(2,1)S(1)}, bf16[48,1536]{1,0:T(8,128)(2,1)S(1)}, u32[]{:S(2)}, u32[]{:S(2)}) %collective-permute-start.9) | collective-permute-done | bytes 147488 | tf_op jit(solution)/shard_map/ppermute | solution.py:32
  104.4 16.0 %all_gather.18 = bf16[512,768]{1,0:T(8,128)(2,1)S(1)} all-gather(bf16[64,768]{1,0:T(8,128)(2,1)S(1)} %get-tuple-element.29), channel_id=1, replica_groups=mesh['x'=4,'zh'=4,'y'=4,'zl'=4,'core'=2] {'zl','core'}, dimensions={0}, use_global_device_ids=true | all-gather | bytes 884736 | tf_op jit(solution)/shard_map/all_gather | solution.py:247
  120.4 2.5 %shard_map.90 = bf16[16,32,1536]{2,1,0:T(8,128)(2,1)} custom-call(s32[9]{0:T(128)S(1)} %copy-done.11, s32[3]{0:T(128)S(1)} %pad_add_fusion.refs_2_.refs_0_.refs_1_, bf16[8,64,768]{2,1,0:T(8,128)(2,1)S(1)} %bitcast.14, bf16[9,128,128]{2,1,0:T(8,128)(2,1)S(1)} %copy-done.9), custom_call_target="tpu_custom_call" | custom-call | flops 603979776 | bytes 4194304 | tf_op jit(solution)/shard_map/pallas_call | solution.py:38
  122.9 6.9 %all-to-all-start = ((bf16[16,32,1536]{2,1,0:T(8,128)(2,1)}), bf16[16,32,1536]{2,1,0:T(8,128)(2,1)S(1)}, u32[]{:S(2)}, u32[]{:S(2)}) async-start(bf16[16,32,1536]{2,1,0:T(8,128)(2,1)} %shard_map.90), calls=%async_computation | async-start | bytes 3145728 | tf_op jit(solution)/shard_map/all_to_all | solution.py:220
  132.0 1.1 copy-done.7
  133.1 2.0 %shard_map.91 = f32[9,128,128]{2,1,0:T(8,128)} custom-call(s32[9]{0:T(128)S(1)} %copy-done.11, bf16[8,64,768]{2,1,0:T(8,128)(2,1)S(1)} %bitcast.15, bf16[4,64,1536]{2,1,0:T(8,128)(2,1)S(1)} %all_gather.17.refs_3_.refs_2_, bf16[4,64,1536]{2,1,0:T(8,128)(2,1)S(1)} %copy-done.1, bf16[4,64,1536]{2,1,0:T(8,128)(2,1)S(1)} %copy-done.4, ...), custom_call_target="tpu_custom_call" | custom-call | flops 603979776 | bytes 4194304 | tf_op jit(solution)/shard_map/pallas_call | solution.py:38
  135.8 15.9 %all_gather.19 = bf16[512,768]{1,0:T(8,128)(2,1)S(1)} all-gather(bf16[64,768]{1,0:T(8,128)(2,1)S(1)} %get-tuple-element.30), channel_id=1, replica_groups=mesh['x'=4,'zh'=4,'y'=4,'zl'=4,'core'=2] {'zl','core'}, dimensions={0}, use_global_device_ids=true | all-gather | bytes 884736 | tf_op jit(solution)/shard_map/all_gather | solution.py:248
  151.7 2.9 %all-to-all-done.refs_0_ = bf16[16,32,1536]{2,1,0:T(8,128)(2,1)S(1)} async-done(((bf16[16,32,1536]{2,1,0:T(8,128)(2,1)}), bf16[16,32,1536]{2,1,0:T(8,128)(2,1)S(1)}, u32[]{:S(2)}, u32[]{:S(2)}) %all-to-all-start) | async-done | bytes 1572896 | tf_op jit(solution)/shard_map/all_to_all | solution.py:220
  155.4 6.3 %all-to-all-start.1 = ((bf16[4,8,1536]{2,1,0:T(8,128)(2,1)}), bf16[4,8,1536]{2,1,0:T(8,128)(2,1)S(1)}, u32[]{:S(2)}, u32[]{:S(2)}) async-start(bf16[4,8,1536]{2,1,0:T(8,128)(2,1)} %bitcast.10), calls=%async_computation.1 | async-start | bytes 196608 | tf_op jit(solution)/shard_map/all_to_all | solution.py:229
  161.8 1.1 copy-done.2
  162.9 1.1 copy-done.5
  164.0 1.1 copy-done.8
  165.2 2.0 %shard_map.93 = f32[9,128,128]{2,1,0:T(8,128)} custom-call(s32[9]{0:T(128)S(1)} %copy-done.12, bf16[8,64,768]{2,1,0:T(8,128)(2,1)S(1)} %bitcast.17, bf16[4,64,1536]{2,1,0:T(8,128)(2,1)S(1)} %all_gather.17.refs_3_.refs_2_, bf16[4,64,1536]{2,1,0:T(8,128)(2,1)S(1)} %copy-done.2, bf16[4,64,1536]{2,1,0:T(8,128)(2,1)S(1)} %copy-done.5, ...), custom_call_target="tpu_custom_call" | custom-call | flops 603979776 | bytes 4194304 | tf_op jit(solution)/shard_map/pallas_call | solution.py:38
  167.1 7.2 %all-to-all-done.1 = bf16[4,8,1536]{2,1,0:T(8,128)(2,1)S(1)} async-done(((bf16[4,8,1536]{2,1,0:T(8,128)(2,1)}), bf16[4,8,1536]{2,1,0:T(8,128)(2,1)S(1)}, u32[]{:S(2)}, u32[]{:S(2)}) %all-to-all-start.1) | async-done | bytes 98336 | tf_op jit(solution)/shard_map/all_to_all | solution.py:229
  (39 shorter events, 9.7 us)
Async XLA Ops:
  0.6 46.7 %copy-start.12 = (s32[9]{0:T(128)S(1)}, s32[9]{0:T(128)}, u32[]{:S(2)}) copy-start(s32[9]{0:T(128)} %refs_0_.9) | copy-start | bytes 112
  0.6 46.7 %copy-start.9 = (bf16[9,128,128]{2,1,0:T(8,128)(2,1)S(1)}, bf16[9,128,128]{2,1,0:T(8,128)(2,1)}, u32[]{:S(2)}) copy-start(bf16[9,128,128]{2,1,0:T(8,128)(2,1)} %refs_3_.1) | copy-start | bytes 884740
  0.7 46.7 %copy-start.11 = (s32[9]{0:T(128)S(1)}, s32[9]{0:T(128)}, u32[]{:S(2)}) copy-start(s32[9]{0:T(128)} %refs_0_.8) | copy-start | bytes 112
  37.1 35.5 %collective-permute-start.4 = (bf16[4,64,1536]{2,1,0:T(8,128)(2,1)S(1)}, bf16[4,64,1536]{2,1,0:T(8,128)(2,1)S(1)}, u32[]{:S(2)}, u32[]{:S(2)}) collective-permute-start(bf16[4,64,1536]{2,1,0:T(8,128)(2,1)S(1)} %all_gather.17.refs_3_.refs_2_), channel_id=1, source_target_pairs={{0,8},{8,16},{16,24},{24,0},{1,9},{9,17},{17,25},{25,1},{2,10},{10... | collective-permute-start | bytes 2359304 | tf_op jit(solution)/shard_map/ppermute | solution.py:32
  40.3 32.3 %collective-permute-start.5 = (bf16[4,64,1536]{2,1,0:T(8,128)(2,1)S(1)}, bf16[4,64,1536]{2,1,0:T(8,128)(2,1)S(1)}, u32[]{:S(2)}, u32[]{:S(2)}) collective-permute-start(bf16[4,64,1536]{2,1,0:T(8,128)(2,1)S(1)} %all_gather.17.refs_3_.refs_2_), channel_id=1, source_target_pairs={{0,24},{8,0},{16,8},{24,16},{1,25},{9,1},{17,9},{25,17},{2,26},{10... | collective-permute-start | bytes 2359304 | tf_op jit(solution)/shard_map/ppermute | solution.py:32
  43.7 28.9 %collective-permute-start.6 = (bf16[4,64,1536]{2,1,0:T(8,128)(2,1)S(1)}, bf16[4,64,1536]{2,1,0:T(8,128)(2,1)S(1)}, u32[]{:S(2)}, u32[]{:S(2)}) collective-permute-start(bf16[4,64,1536]{2,1,0:T(8,128)(2,1)S(1)} %all_gather.17.refs_3_.refs_2_), channel_id=1, source_target_pairs={{0,16},{8,24},{16,0},{24,8},{1,17},{9,25},{17,1},{25,9},{2,18},{10... | collective-permute-start | bytes 2359304 | tf_op jit(solution)/shard_map/ppermute | solution.py:32
  47.3 1.0 copy-start.10
  49.4 10.9 %collective-permute-start = (f32[64,1536]{1,0:T(8,128)S(1)}, f32[64,1536]{1,0:T(8,128)S(1)}, u32[]{:S(2)}, u32[]{:S(2)}) collective-permute-start(f32[64,1536]{1,0:T(8,128)S(1)} %get-tuple-element.18), channel_id=1, source_target_pairs={{0,1},{1,0},{2,3},{3,2},{4,5},{5,4},{6,7},{7,6},{8,9},{9,8},{10,11... | collective-permute-start | bytes 1179656 | tf_op jit(solution)/shard_map/ppermute | solution.py:32
  60.8 6.6 %collective-permute-start.1 = (bf16[16,1536]{1,0:T(8,128)(2,1)S(1)}, bf16[16,1536]{1,0:T(8,128)(2,1)S(1)}, u32[]{:S(2)}, u32[]{:S(2)}) collective-permute-start(bf16[16,1536]{1,0:T(8,128)(2,1)S(1)} %get-tuple-element.20), channel_id=1, source_target_pairs={{0,2},{2,4},{4,6},{6,0},{1,3},{3,5},{5,7},{7,1},{8,10},{10,12},{12... | collective-permute-start | bytes 147464 | tf_op jit(solution)/shard_map/ppermute | solution.py:32
  63.4 7.0 %collective-permute-start.2 = (bf16[16,1536]{1,0:T(8,128)(2,1)S(1)}, bf16[16,1536]{1,0:T(8,128)(2,1)S(1)}, u32[]{:S(2)}, u32[]{:S(2)}) collective-permute-start(bf16[16,1536]{1,0:T(8,128)(2,1)S(1)} %get-tuple-element.21), channel_id=1, source_target_pairs={{0,4},{2,6},{4,0},{6,2},{1,5},{3,7},{5,1},{7,3},{8,12},{10,14},{12... | collective-permute-start | bytes 147464 | tf_op jit(solution)/shard_map/ppermute | solution.py:32
  67.5 5.1 %collective-permute-start.3 = (bf16[16,1536]{1,0:T(8,128)(2,1)S(1)}, bf16[16,1536]{1,0:T(8,128)(2,1)S(1)}, u32[]{:S(2)}, u32[]{:S(2)}) collective-permute-start(bf16[16,1536]{1,0:T(8,128)(2,1)S(1)} %get-tuple-element.22), channel_id=1, source_target_pairs={{0,6},{2,0},{4,2},{6,4},{1,7},{3,1},{5,3},{7,5},{8,14},{10,8},{12,... | collective-permute-start | bytes 147464 | tf_op jit(solution)/shard_map/ppermute | solution.py:32
  72.6 1.6 copy-start
  72.6 1.6 copy-start.3
  72.6 1.6 copy-start.6
  74.2 10.0 %collective-permute-start.7 = (f32[192,1536]{1,0:T(8,128)S(1)}, f32[192,1536]{1,0:T(8,128)S(1)}, u32[]{:S(2)}, u32[]{:S(2)}) collective-permute-start(f32[192,1536]{1,0:T(8,128)S(1)} %get-tuple-element.24), channel_id=1, source_target_pairs={{0,1},{1,0},{2,3},{3,2},{4,5},{5,4},{6,7},{7,6},{8,9},{9,8},{10,11... | collective-permute-start | bytes 3538952 | tf_op jit(solution)/shard_map/ppermute | solution.py:32
  84.9 8.2 %collective-permute-start.10 = (bf16[48,1536]{1,0:T(8,128)(2,1)S(1)}, bf16[48,1536]{1,0:T(8,128)(2,1)S(1)}, u32[]{:S(2)}, u32[]{:S(2)}) collective-permute-start(bf16[48,1536]{1,0:T(8,128)(2,1)S(1)} %get-tuple-element.28), channel_id=1, source_target_pairs={{0,6},{2,0},{4,2},{6,4},{1,7},{3,1},{5,3},{7,5},{8,14},{10,8},{12,... | collective-permute-start | bytes 442376 | tf_op jit(solution)/shard_map/ppermute | solution.py:32
  88.4 8.4 %collective-permute-start.8 = (bf16[48,1536]{1,0:T(8,128)(2,1)S(1)}, bf16[48,1536]{1,0:T(8,128)(2,1)S(1)}, u32[]{:S(2)}, u32[]{:S(2)}) collective-permute-start(bf16[48,1536]{1,0:T(8,128)(2,1)S(1)} %get-tuple-element.26), channel_id=1, source_target_pairs={{0,2},{2,4},{4,6},{6,0},{1,3},{3,5},{5,7},{7,1},{8,10},{10,12},{12... | collective-permute-start | bytes 442376 | tf_op jit(solution)/shard_map/ppermute | solution.py:32
  90.3 13.9 %collective-permute-start.9 = (bf16[48,1536]{1,0:T(8,128)(2,1)S(1)}, bf16[48,1536]{1,0:T(8,128)(2,1)S(1)}, u32[]{:S(2)}, u32[]{:S(2)}) collective-permute-start(bf16[48,1536]{1,0:T(8,128)(2,1)S(1)} %get-tuple-element.27), channel_id=1, source_target_pairs={{0,4},{2,6},{4,0},{6,2},{1,5},{3,7},{5,1},{7,3},{8,12},{10,14},{12... | collective-permute-start | bytes 442376 | tf_op jit(solution)/shard_map/ppermute | solution.py:32
  122.9 31.7 %all-to-all-start = ((bf16[16,32,1536]{2,1,0:T(8,128)(2,1)}), bf16[16,32,1536]{2,1,0:T(8,128)(2,1)S(1)}, u32[]{:S(2)}, u32[]{:S(2)}) async-start(bf16[16,32,1536]{2,1,0:T(8,128)(2,1)} %shard_map.90), calls=%async_computation | async-start | bytes 3145728 | tf_op jit(solution)/shard_map/all_to_all | solution.py:220
  129.7 1.1 copy-start.1
  130.9 1.1 copy-start.4
  132.0 1.1 copy-start.7
  155.4 18.9 %all-to-all-start.1 = ((bf16[4,8,1536]{2,1,0:T(8,128)(2,1)}), bf16[4,8,1536]{2,1,0:T(8,128)(2,1)S(1)}, u32[]{:S(2)}, u32[]{:S(2)}) async-start(bf16[4,8,1536]{2,1,0:T(8,128)(2,1)} %bitcast.10), calls=%async_computation.1 | async-start | bytes 196608 | tf_op jit(solution)/shard_map/all_to_all | solution.py:229
  161.8 1.1 copy-start.2
  162.9 1.1 copy-start.5
  164.0 1.1 copy-start.8

commit v7 on v6

--- a/solution.py
+++ b/solution.py
@@ -69,8 +69,8 @@
 
 
 def rows_of(parts, first, index):
-    at = lanes(index)
-    return jnp.concatenate([p[:, first : first + 32, at].reshape(4 * 32, BS) for p in parts], axis=0)
+    at = lanes(index + first)
+    return jnp.concatenate([p[:, :, at].reshape(4 * 32, BS) for p in parts], axis=0)
 
 
 def partial_body(where1, where2, ids, *refs):
@@ -82,7 +82,7 @@
         i, j = w1_pos(where1[b])
         acc[j] += dot(rows_of(parts, 0, i), blocks1[b], NN)
         i, j = w2_pos(where2[b])
-        acc[NJ + j] += dot(rows_of(parts, 32, i), blocks2[b], NT)
+        acc[NJ + j] += dot(rows_of(parts, NI, i), blocks2[b], NT)
     for z in range(4):
         mine = pl.ds(pl.multiple_of((2 * z + core) * n, n), n)
         other = pl.ds(pl.multiple_of((2 * z + 1 - core) * n, n), n)
@@ -127,20 +127,41 @@
     return mine, shift(s1, "zl", 1), shift(s2, "zl", 2), shift(s3, "zl", 3)
 
 
-def gelu_body(*refs):
-    activated, hidden_grad = refs[8:]
-    for h in range(2):
-        own, r1, r2, r3 = refs[4 * h : 4 * h + 4]
-        v, g = own[:, :HT], own[:, HT:]
-        for ref in (r1, r2, r3):
-            v = v + ref[:, :HT].astype(F32)
-            g = g + ref[:, HT:].astype(F32)
-        t = jnp.tanh(C0 * (v + 0.044715 * v * v * v))
-        derive = C0 * (1.0 + 3.0 * 0.044715 * v * v)
-        slope = 0.5 * (1.0 + t) + 0.5 * v * (1.0 - t * t) * derive
-        at = slice(0, FIRST) if h == 0 else slice(FIRST, Q)
-        activated[at] = (0.5 * v * (1.0 + t)).astype(BF)
-        hidden_grad[at] = (g * slope).astype(BF)
+def whole_split_body(ids, keep, got, mine, sums):
+    n = mine.shape[0]
+    own = pl.ds(pl.multiple_of(ids[1] * n, n), n)
+    mine[...] = keep[own] + got[own]
+    sums[...] = (keep[...] + got[...]).astype(BF)
+
+
+def column_sums_at_once(ids, keep, got):
+    n = keep.shape[0] // 4
+    mine, sums = call(
+        whole_split_body,
+        (ids, keep, got),
+        [((n, WT), F32), ((4 * n, WT), BF)],
+        flops=1 << 20,
+        nbytes=1 << 20,
+    )
+    return mine, lax.all_to_all(sums, "zl", 0, 0, tiled=True)
+
+
+def gelu_of(v, g):
+    t = jnp.tanh(C0 * (v + 0.044715 * v * v * v))
+    derive = C0 * (1.0 + 3.0 * 0.044715 * v * v)
+    slope = 0.5 * (1.0 + t) + 0.5 * v * (1.0 - t * t) * derive
+    return (0.5 * v * (1.0 + t)).astype(BF), (g * slope).astype(BF)
+
+
+def gelu_body(ids, own, r1, r2, r3, mine, others, activated, hidden_grad):
+    total = own[...] + r1[...].astype(F32) + r2[...].astype(F32) + r3[...].astype(F32)
+    activated[:FIRST], hidden_grad[:FIRST] = gelu_of(total[:, :HT], total[:, HT:])
+    n = Q - FIRST
+    total = mine[...]
+    for z in range(4):
+        term = others[z * n : (z + 1) * n].astype(F32)
+        total = total + jnp.where(ids[1] == z, 0.0, term)
+    activated[FIRST:], hidden_grad[FIRST:] = gelu_of(total[:, :HT], total[:, HT:])
 
 
 def tokens_of(hid, index):
@@ -232,23 +253,23 @@
 
 def shards(inputs, cotangent, w1_blocks, w1_where, w2_blocks, w2_where):
     ids = jnp.stack([lax.axis_index(a) for a in ("core", "zl", "y")]).astype(jnp.int32)
-    near = lax.all_gather(jnp.concatenate([inputs, cotangent], axis=0), "zh", axis=0)
-    near = near.reshape(4, 2, 8, WT).swapaxes(0, 1).reshape(64, WT)
+    both = jnp.concatenate([inputs, cotangent], axis=1)
+    near = lax.all_gather(both, "zh", axis=0, tiled=True)
     along = lax.all_gather(near, "x", axis=0)
     parts = [along] + [shift(along, "y", step) for step in STEPS[1:]]
     weights = (w1_blocks, w2_blocks)
     keep, send = product_terms(ids, w1_where, w2_where, parts[:1], *weights)
     first = column_sums(ids, keep, shift(send, "core", 1))
     keep, send = product_terms(ids, w1_where, w2_where, parts[1:], *weights, after=first[1:])
-    second = column_sums(ids, keep, shift(send, "core", 1))
+    second = column_sums_at_once(ids, keep, shift(send, "core", 1))
     activated, hidden_grad = call(
-        gelu_body, (*first, *second), [((Q, HT), BF)] * 2, flops=1 << 22, nbytes=1 << 20
+        gelu_body, (ids, *first, *second), [((Q, HT), BF)] * 2, flops=1 << 22, nbytes=1 << 20
     )
     whole_hg = lax.all_gather(hidden_grad, ("zl", "core"), axis=0, tiled=True).reshape(8, Q, HT)
     whole_av = lax.all_gather(activated, ("zl", "core"), axis=0, tiled=True).reshape(8, Q, HT)
     partial = input_grad_partial(w1_where, ids, whole_hg, w1_blocks)
     w1_grad = block_grads(w1_pos, 0, w1_where, whole_hg, parts)
-    w2_grad = block_grads(w2_pos, 32, w2_where, whole_av, parts)
+    w2_grad = block_grads(w2_pos, NI, w2_where, whole_av, parts)
     input_grad = row_reduce(partial, (whole_av[0, :16, :BS], w1_grad[0, :8]))
     return input_grad, w1_grad, w2_grad
 

time: 176 us -> 177 us (level)
  blocking collectives: 67.5 us -> 86.4 us
  waiting for transfers between devices: 28 us -> 17.2 us
  starting transfers between devices: 57.2 us -> 49 us
    all_to_all x0 -> x1, blocking collectives: none -> 18 us  [column_sums_at_once(): return (mine, lax.all_to_all(sums, 'zl', 0, 0, tiled=True))]
    ppermute x11 -> x8, waiting for transfers between devices: 18 us -> 6.93 us  [shift(): return lax.ppermute(value, axis, [(i, (i + step) % n) for i in range(n)])]
    ppermute x11 -> x8, starting transfers between devices: 44 us -> 35.8 us  [shift(): return lax.ppermute(value, axis, [(i, (i + step) % n) for i in range(n)])]
  transfers between devices with their start and end apart: 13 -> 10, of which waited for: 8 -> 6; matrix products, arithmetic and copies ran while one was open for 0% -> 0% of each run, Pallas kernels for 3% -> 3%
where the time goes in v7:
time: 177 us; the launch traced here: 176 us
  blocking collectives  86.4 us (49%)
  starting transfers between devices  49 us (28%)
  waiting for transfers between devices  17.2 us (10%)
  Pallas kernels  12.2 us (7%)
  local copies, waits for them, and re-layouts  8.46 us (5%)
    ppermute x8, starting transfers between devices, shift(): return lax.ppermute(value, axis, [(i, (i + step) % n) for i in range(n)])  35.8 us
    all_gather x1, blocking collectives, shards(): near = lax.all_gather(both, 'zh', axis=0, tiled=True)  24.5 us
    all_to_all x1, blocking collectives, column_sums_at_once(): return (mine, lax.all_to_all(sums, 'zl', 0, 0, tiled=True))  18 us
    all_gather x1, blocking collectives, shards(): lax.all_gather(hidden_grad, ('zl', 'core'), axis=0, tiled=True)  17 us
    all_gather x1, blocking collectives, shards(): lax.all_gather(activated, ('zl', 'core'), axis=0, tiled=True)  15.7 us
    pallas_call x9, Pallas kernels, call(): pl.pallas_call(lambda *refs: body(*refs[:n], *refs[m:]), out_shape=[shape...  12.2 us
    all_gather x1, blocking collectives, shards(): along = lax.all_gather(near, 'x', axis=0)  11.1 us
    unnamed x26, local copies, waits for them, and re-layouts  7.77 us
  transfers between devices with their start and end apart: 10, of which 6 were waited for; matrix products, arithmetic and copies ran while one was open for 0% of the time, Pallas kernels for 3%

profile of v7, /device:TPU:1, one launch (start us, length us, event | category | flops | bytes accessed | tf_op | source)
XLA Modules:
  0.0 175.6 jit_solution(16174892878293935533)
XLA Ops:
  1.5 24.5 %all_gather.15 = bf16[32,3072]{1,0:T(8,128)(2,1)S(1)} all-gather(bf16[8,3072]{1,0:T(8,128)(2,1)S(1)} %pad_maximum_fusion), channel_id=1, replica_groups=mesh['x'=4,'zh'=4,'y'=4,'zl'=4,'core'=2] {'zh'}, dimensions={0}, use_global_device_ids=true | all-gather | bytes 245760 | tf_op jit(solution)/shard_map/all_gather | solution.py:257
  26.0 11.1 %all-gather = bf16[128,3072]{1,0:T(8,128)(2,1)S(1)} all-gather(bf16[32,3072]{1,0:T(8,128)(2,1)S(1)} %all_gather.15), channel_id=2, replica_groups=mesh['x'=4,'zh'=4,'y'=4,'zl'=4,'core'=2] {'x'}, dimensions={0}, use_global_device_ids=true | all-gather | bytes 983040 | tf_op jit(solution)/shard_map/all_gather | solution.py:258
  37.1 3.2 %collective-permute-start.4 = (bf16[4,32,3072]{2,1,0:T(8,128)(2,1)S(1)}, bf16[4,32,3072]{2,1,0:T(8,128)(2,1)S(1)}, u32[]{:S(2)}, u32[]{:S(2)}) collective-permute-start(bf16[4,32,3072]{2,1,0:T(8,128)(2,1)S(1)} %bitcast.13), channel_id=1, source_target_pairs={{0,8},{8,16},{16,24},{24,0},{1,9},{9,17},{17,25},{25,1},{2,10},{10... | collective-permute-start | bytes 2359304 | tf_op jit(solution)/shard_map/ppermute | solution.py:32
  40.3 3.4 %collective-permute-start.5 = (bf16[4,32,3072]{2,1,0:T(8,128)(2,1)S(1)}, bf16[4,32,3072]{2,1,0:T(8,128)(2,1)S(1)}, u32[]{:S(2)}, u32[]{:S(2)}) collective-permute-start(bf16[4,32,3072]{2,1,0:T(8,128)(2,1)S(1)} %bitcast.14), channel_id=1, source_target_pairs={{0,24},{8,0},{16,8},{24,16},{1,25},{9,1},{17,9},{25,17},{2,26},{10... | collective-permute-start | bytes 2359304 | tf_op jit(solution)/shard_map/ppermute | solution.py:32
  43.7 3.5 %collective-permute-start.6 = (bf16[4,32,3072]{2,1,0:T(8,128)(2,1)S(1)}, bf16[4,32,3072]{2,1,0:T(8,128)(2,1)S(1)}, u32[]{:S(2)}, u32[]{:S(2)}) collective-permute-start(bf16[4,32,3072]{2,1,0:T(8,128)(2,1)S(1)} %bitcast.15), channel_id=1, source_target_pairs={{0,16},{8,24},{16,0},{24,8},{1,17},{9,25},{17,1},{25,9},{2,18},{10... | collective-permute-start | bytes 2359304 | tf_op jit(solution)/shard_map/ppermute | solution.py:32
  47.3 1.0 copy-done.10
  48.3 1.0 shard_map.85
  49.3 9.6 %collective-permute-start = (f32[64,1536]{1,0:T(8,128)S(1)}, f32[64,1536]{1,0:T(8,128)S(1)}, u32[]{:S(2)}, u32[]{:S(2)}) collective-permute-start(f32[64,1536]{1,0:T(8,128)S(1)} %get-tuple-element.16), channel_id=1, source_target_pairs={{0,1},{1,0},{2,3},{3,2},{4,5},{5,4},{6,7},{7,6},{8,9},{9,8},{10,11... | collective-permute-start | bytes 1179656 | tf_op jit(solution)/shard_map/ppermute | solution.py:32
  58.9 1.3 collective-permute-done.refs_2_
  60.8 2.5 %collective-permute-start.1 = (bf16[16,1536]{1,0:T(8,128)(2,1)S(1)}, bf16[16,1536]{1,0:T(8,128)(2,1)S(1)}, u32[]{:S(2)}, u32[]{:S(2)}) collective-permute-start(bf16[16,1536]{1,0:T(8,128)(2,1)S(1)} %get-tuple-element.18), channel_id=1, source_target_pairs={{0,2},{2,4},{4,6},{6,0},{1,3},{3,5},{5,7},{7,1},{8,10},{10,12},{12... | collective-permute-start | bytes 147464 | tf_op jit(solution)/shard_map/ppermute | solution.py:32
  63.3 3.2 %collective-permute-start.2 = (bf16[16,1536]{1,0:T(8,128)(2,1)S(1)}, bf16[16,1536]{1,0:T(8,128)(2,1)S(1)}, u32[]{:S(2)}, u32[]{:S(2)}) collective-permute-start(bf16[16,1536]{1,0:T(8,128)(2,1)S(1)} %get-tuple-element.19), channel_id=1, source_target_pairs={{0,4},{2,6},{4,0},{6,2},{1,5},{3,7},{5,1},{7,3},{8,12},{10,14},{12... | collective-permute-start | bytes 147464 | tf_op jit(solution)/shard_map/ppermute | solution.py:32
  67.5 2.9 %collective-permute-start.3 = (bf16[16,1536]{1,0:T(8,128)(2,1)S(1)}, bf16[16,1536]{1,0:T(8,128)(2,1)S(1)}, u32[]{:S(2)}, u32[]{:S(2)}) collective-permute-start(bf16[16,1536]{1,0:T(8,128)(2,1)S(1)} %get-tuple-element.20), channel_id=1, source_target_pairs={{0,6},{2,0},{4,2},{6,4},{1,7},{3,1},{5,3},{7,5},{8,14},{10,8},{12,... | collective-permute-start | bytes 147464 | tf_op jit(solution)/shard_map/ppermute | solution.py:32
  70.3 2.2 %collective-permute-done.3.refs_10_.refs_4_ = bf16[16,1536]{1,0:T(8,128)(2,1)S(1)} collective-permute-done((bf16[16,1536]{1,0:T(8,128)(2,1)S(1)}, bf16[16,1536]{1,0:T(8,128)(2,1)S(1)}, u32[]{:S(2)}, u32[]{:S(2)}) %collective-permute-start.3) | collective-permute-done | bytes 49184 | tf_op jit(solution)/shard_map/ppermute | solution.py:32
  72.6 1.7 shard_map.87
  74.3 7.5 %collective-permute-start.7 = (f32[192,1536]{1,0:T(8,128)S(1)}, f32[192,1536]{1,0:T(8,128)S(1)}, u32[]{:S(2)}, u32[]{:S(2)}) collective-permute-start(f32[192,1536]{1,0:T(8,128)S(1)} %get-tuple-element.22), channel_id=1, source_target_pairs={{0,1},{1,0},{2,3},{3,2},{4,5},{5,4},{6,7},{7,6},{8,9},{9,8},{10,11... | collective-permute-start | bytes 3538952 | tf_op jit(solution)/shard_map/ppermute | solution.py:32
  81.9 2.5 %collective-permute-done.7.refs_2_ = f32[192,1536]{1,0:T(8,128)S(1)} collective-permute-done((f32[192,1536]{1,0:T(8,128)S(1)}, f32[192,1536]{1,0:T(8,128)S(1)}, u32[]{:S(2)}, u32[]{:S(2)}) %collective-permute-start.7) | collective-permute-done | bytes 1179680 | tf_op jit(solution)/shard_map/ppermute | solution.py:32
  85.0 18.0 %all_to_all.25 = bf16[4,48,1536]{2,1,0:T(8,128)(2,1)S(1)} all-to-all(bf16[4,48,1536]{2,1,0:T(8,128)(2,1)S(1)} %bitcast.24), channel_id=1, replica_groups=mesh['x'=4,'zh'=4,'y'=4,'zl'=4,'core'=2] {'zl'}, dimensions={0} | all-to-all | bytes 1179648 | tf_op jit(solution)/shard_map/all_to_all | solution.py:146
  103.8 17.0 %all_gather.18 = bf16[512,768]{1,0:T(8,128)(2,1)S(1)} all-gather(bf16[64,768]{1,0:T(8,128)(2,1)S(1)} %get-tuple-element.25), channel_id=1, replica_groups=mesh['x'=4,'zh'=4,'y'=4,'zl'=4,'core'=2] {'zl','core'}, dimensions={0}, use_global_device_ids=true | all-gather | bytes 884736 | tf_op jit(solution)/shard_map/all_gather | solution.py:268
  120.9 2.5 %shard_map.90 = bf16[16,32,1536]{2,1,0:T(8,128)(2,1)} custom-call(s32[9]{0:T(128)S(1)} %copy-done.11, s32[3]{0:T(128)S(1)} %pad_add_fusion.refs_2_.refs_0_.refs_1_, bf16[8,64,768]{2,1,0:T(8,128)(2,1)S(1)} %bitcast.19, bf16[9,128,128]{2,1,0:T(8,128)(2,1)S(1)} %copy-done.9), custom_call_target="tpu_custom_call" | custom-call | flops 603979776 | bytes 4194304 | tf_op jit(solution)/shard_map/pallas_call | solution.py:38
  123.4 6.9 %all-to-all-start.1 = ((bf16[16,32,1536]{2,1,0:T(8,128)(2,1)}), bf16[16,32,1536]{2,1,0:T(8,128)(2,1)S(1)}, u32[]{:S(2)}, u32[]{:S(2)}) async-start(bf16[16,32,1536]{2,1,0:T(8,128)(2,1)} %shard_map.90), calls=%async_computation.1 | async-start | bytes 3145728 | tf_op jit(solution)/shard_map/all_to_all | solution.py:241
  130.3 1.1 copy-done.1
  131.4 1.1 copy-done.4
  132.5 1.1 copy-done.7
  133.6 2.0 %shard_map.91 = f32[9,128,128]{2,1,0:T(8,128)} custom-call(s32[9]{0:T(128)S(1)} %copy-done.11, bf16[8,64,768]{2,1,0:T(8,128)(2,1)S(1)} %bitcast.20, bf16[4,32,3072]{2,1,0:T(8,128)(2,1)S(1)} %bitcast.17, bf16[4,32,3072]{2,1,0:T(8,128)(2,1)S(1)} %copy-done.1, bf16[4,32,3072]{2,1,0:T(8,128)(2,1)S(1)} %copy-done.4, bf16[4,32,3072]{2,1,0:T(8,128)(2,1)S(1)} %copy-done.7), custom_call_target="tpu_custom_call" | custom-call | flops 603979776 | bytes 4194304 | tf_op jit(solution)/shard_map/pallas_call | solution.py:38
  136.3 15.7 %all_gather.19 = bf16[512,768]{1,0:T(8,128)(2,1)S(1)} all-gather(bf16[64,768]{1,0:T(8,128)(2,1)S(1)} %get-tuple-element.26), channel_id=1, replica_groups=mesh['x'=4,'zh'=4,'y'=4,'zl'=4,'core'=2] {'zl','core'}, dimensions={0}, use_global_device_ids=true | all-gather | bytes 884736 | tf_op jit(solution)/shard_map/all_gather | solution.py:269
  152.1 3.0 %all-to-all-done.1.refs_0_ = bf16[16,32,1536]{2,1,0:T(8,128)(2,1)S(1)} async-done(((bf16[16,32,1536]{2,1,0:T(8,128)(2,1)}), bf16[16,32,1536]{2,1,0:T(8,128)(2,1)S(1)}, u32[]{:S(2)}, u32[]{:S(2)}) %all-to-all-start.1) | async-done | bytes 1572896 | tf_op jit(solution)/shard_map/all_to_all | solution.py:241
  155.9 6.3 %all-to-all-start.2 = ((bf16[4,8,1536]{2,1,0:T(8,128)(2,1)}), bf16[4,8,1536]{2,1,0:T(8,128)(2,1)S(1)}, u32[]{:S(2)}, u32[]{:S(2)}) async-start(bf16[4,8,1536]{2,1,0:T(8,128)(2,1)} %bitcast.10), calls=%async_computation.2 | async-start | bytes 196608 | tf_op jit(solution)/shard_map/all_to_all | solution.py:250
  162.3 1.1 copy-done.2
  163.4 1.1 copy-done.5
  164.6 1.1 copy-done.8
  165.7 2.0 %shard_map.93 = f32[9,128,128]{2,1,0:T(8,128)} custom-call(s32[9]{0:T(128)S(1)} %copy-done.12, bf16[8,64,768]{2,1,0:T(8,128)(2,1)S(1)} %bitcast.22, bf16[4,32,3072]{2,1,0:T(8,128)(2,1)S(1)} %bitcast.18, bf16[4,32,3072]{2,1,0:T(8,128)(2,1)S(1)} %copy-done.2, bf16[4,32,3072]{2,1,0:T(8,128)(2,1)S(1)} %copy-done.5, bf16[4,32,3072]{2,1,0:T(8,128)(2,1)S(1)} %copy-done.8), custom_call_target="tpu_custom_call" | custom-call | flops 603979776 | bytes 4194304 | tf_op jit(solution)/shard_map/pallas_call | solution.py:38
  167.7 7.3 %all-to-all-done.2 = bf16[4,8,1536]{2,1,0:T(8,128)(2,1)S(1)} async-done(((bf16[4,8,1536]{2,1,0:T(8,128)(2,1)}), bf16[4,8,1536]{2,1,0:T(8,128)(2,1)S(1)}, u32[]{:S(2)}, u32[]{:S(2)}) %all-to-all-start.2) | async-done | bytes 98336 | tf_op jit(solution)/shard_map/all_to_all | solution.py:250
  (33 shorter events, 6.1 us)
Async XLA Ops:
  0.6 46.7 %copy-start.12 = (s32[9]{0:T(128)S(1)}, s32[9]{0:T(128)}, u32[]{:S(2)}) copy-start(s32[9]{0:T(128)} %refs_0_.9) | copy-start | bytes 112
  0.6 46.7 %copy-start.9 = (bf16[9,128,128]{2,1,0:T(8,128)(2,1)S(1)}, bf16[9,128,128]{2,1,0:T(8,128)(2,1)}, u32[]{:S(2)}) copy-start(bf16[9,128,128]{2,1,0:T(8,128)(2,1)} %refs_3_.1) | copy-start | bytes 884740
  0.7 46.7 %copy-start.11 = (s32[9]{0:T(128)S(1)}, s32[9]{0:T(128)}, u32[]{:S(2)}) copy-start(s32[9]{0:T(128)} %refs_0_.8) | copy-start | bytes 112
  37.1 35.5 %collective-permute-start.4 = (bf16[4,32,3072]{2,1,0:T(8,128)(2,1)S(1)}, bf16[4,32,3072]{2,1,0:T(8,128)(2,1)S(1)}, u32[]{:S(2)}, u32[]{:S(2)}) collective-permute-start(bf16[4,32,3072]{2,1,0:T(8,128)(2,1)S(1)} %bitcast.13), channel_id=1, source_target_pairs={{0,8},{8,16},{16,24},{24,0},{1,9},{9,17},{17,25},{25,1},{2,10},{10... | collective-permute-start | bytes 2359304 | tf_op jit(solution)/shard_map/ppermute | solution.py:32
  40.3 32.3 %collective-permute-start.5 = (bf16[4,32,3072]{2,1,0:T(8,128)(2,1)S(1)}, bf16[4,32,3072]{2,1,0:T(8,128)(2,1)S(1)}, u32[]{:S(2)}, u32[]{:S(2)}) collective-permute-start(bf16[4,32,3072]{2,1,0:T(8,128)(2,1)S(1)} %bitcast.14), channel_id=1, source_target_pairs={{0,24},{8,0},{16,8},{24,16},{1,25},{9,1},{17,9},{25,17},{2,26},{10... | collective-permute-start | bytes 2359304 | tf_op jit(solution)/shard_map/ppermute | solution.py:32
  43.7 28.9 %collective-permute-start.6 = (bf16[4,32,3072]{2,1,0:T(8,128)(2,1)S(1)}, bf16[4,32,3072]{2,1,0:T(8,128)(2,1)S(1)}, u32[]{:S(2)}, u32[]{:S(2)}) collective-permute-start(bf16[4,32,3072]{2,1,0:T(8,128)(2,1)S(1)} %bitcast.15), channel_id=1, source_target_pairs={{0,16},{8,24},{16,0},{24,8},{1,17},{9,25},{17,1},{25,9},{2,18},{10... | collective-permute-start | bytes 2359304 | tf_op jit(solution)/shard_map/ppermute | solution.py:32
  47.3 1.0 copy-start.10
  49.3 10.9 %collective-permute-start = (f32[64,1536]{1,0:T(8,128)S(1)}, f32[64,1536]{1,0:T(8,128)S(1)}, u32[]{:S(2)}, u32[]{:S(2)}) collective-permute-start(f32[64,1536]{1,0:T(8,128)S(1)} %get-tuple-element.16), channel_id=1, source_target_pairs={{0,1},{1,0},{2,3},{3,2},{4,5},{5,4},{6,7},{7,6},{8,9},{9,8},{10,11... | collective-permute-start | bytes 1179656 | tf_op jit(solution)/shard_map/ppermute | solution.py:32
  60.8 6.6 %collective-permute-start.1 = (bf16[16,1536]{1,0:T(8,128)(2,1)S(1)}, bf16[16,1536]{1,0:T(8,128)(2,1)S(1)}, u32[]{:S(2)}, u32[]{:S(2)}) collective-permute-start(bf16[16,1536]{1,0:T(8,128)(2,1)S(1)} %get-tuple-element.18), channel_id=1, source_target_pairs={{0,2},{2,4},{4,6},{6,0},{1,3},{3,5},{5,7},{7,1},{8,10},{10,12},{12... | collective-permute-start | bytes 147464 | tf_op jit(solution)/shard_map/ppermute | solution.py:32
  63.3 7.0 %collective-permute-start.2 = (bf16[16,1536]{1,0:T(8,128)(2,1)S(1)}, bf16[16,1536]{1,0:T(8,128)(2,1)S(1)}, u32[]{:S(2)}, u32[]{:S(2)}) collective-permute-start(bf16[16,1536]{1,0:T(8,128)(2,1)S(1)} %get-tuple-element.19), channel_id=1, source_target_pairs={{0,4},{2,6},{4,0},{6,2},{1,5},{3,7},{5,1},{7,3},{8,12},{10,14},{12... | collective-permute-start | bytes 147464 | tf_op jit(solution)/shard_map/ppermute | solution.py:32
  67.5 5.1 %collective-permute-start.3 = (bf16[16,1536]{1,0:T(8,128)(2,1)S(1)}, bf16[16,1536]{1,0:T(8,128)(2,1)S(1)}, u32[]{:S(2)}, u32[]{:S(2)}) collective-permute-start(bf16[16,1536]{1,0:T(8,128)(2,1)S(1)} %get-tuple-element.20), channel_id=1, source_target_pairs={{0,6},{2,0},{4,2},{6,4},{1,7},{3,1},{5,3},{7,5},{8,14},{10,8},{12,... | collective-permute-start | bytes 147464 | tf_op jit(solution)/shard_map/ppermute | solution.py:32
  72.6 1.7 copy-start
  72.6 1.7 copy-start.3
  72.6 1.7 copy-start.6
  74.3 10.0 %collective-permute-start.7 = (f32[192,1536]{1,0:T(8,128)S(1)}, f32[192,1536]{1,0:T(8,128)S(1)}, u32[]{:S(2)}, u32[]{:S(2)}) collective-permute-start(f32[192,1536]{1,0:T(8,128)S(1)} %get-tuple-element.22), channel_id=1, source_target_pairs={{0,1},{1,0},{2,3},{3,2},{4,5},{5,4},{6,7},{7,6},{8,9},{9,8},{10,11... | collective-permute-start | bytes 3538952 | tf_op jit(solution)/shard_map/ppermute | solution.py:32
  123.4 31.8 %all-to-all-start.1 = ((bf16[16,32,1536]{2,1,0:T(8,128)(2,1)}), bf16[16,32,1536]{2,1,0:T(8,128)(2,1)S(1)}, u32[]{:S(2)}, u32[]{:S(2)}) async-start(bf16[16,32,1536]{2,1,0:T(8,128)(2,1)} %shard_map.90), calls=%async_computation.1 | async-start | bytes 3145728 | tf_op jit(solution)/shard_map/all_to_all | solution.py:241
  130.2 1.1 copy-start.1
  131.4 1.1 copy-start.4
  132.5 1.1 copy-start.7
  155.9 19.1 %all-to-all-start.2 = ((bf16[4,8,1536]{2,1,0:T(8,128)(2,1)}), bf16[4,8,1536]{2,1,0:T(8,128)(2,1)S(1)}, u32[]{:S(2)}, u32[]{:S(2)}) async-start(bf16[4,8,1536]{2,1,0:T(8,128)(2,1)} %bitcast.10), calls=%async_computation.2 | async-start | bytes 196608 | tf_op jit(solution)/shard_map/all_to_all | solution.py:250
  162.3 1.1 copy-start.2
  163.4 1.1 copy-start.5
  164.6 1.1 copy-start.8

commit v8 on v7

--- a/solution.py
+++ b/solution.py
@@ -213,7 +213,7 @@
     parts, out = refs[:4], refs[4]
     for b in range(NB):
         i, j = pos(where[b])
-        left, right = rows_of(parts, first, i), tokens_of(hid, j)
+        left, right = rows_of(parts, first, i), tokens_of(hid, j).astype(BF)
         if first:
             left, right = right, left
         out[b] = dot(left, right, TN)
@@ -237,7 +237,15 @@
     out[...] = total.astype(BF)
 
 
-def row_reduce(partial, after):
+def last_sum_body(parts, out):
+    out[...] = jnp.sum(parts[...].astype(F32).reshape(4, 8, WT), axis=0).astype(BF)
+
+
+def widen_body(narrow, wide):
+    wide[...] = narrow[...].astype(F32)
+
+
+def row_reduce(partial, after, after_last):
     parts = lax.all_to_all(partial, ("y", "x"), 0, 0, tiled=True)
     (mine,) = call(
         sum_body,
@@ -248,7 +256,8 @@
         after=after,
     )
     last = lax.all_to_all(mine, "zh", 0, 0, tiled=True)
-    return jnp.sum(last.reshape(4, 8, WT).astype(F32), axis=0).astype(BF)
+    (out,) = call(last_sum_body, (last,), [((8, WT), BF)], flops=1 << 16, nbytes=1 << 17, after=after_last)
+    return out
 
 
 def shards(inputs, cotangent, w1_blocks, w1_where, w2_blocks, w2_where):
@@ -266,11 +275,12 @@
         gelu_body, (ids, *first, *second), [((Q, HT), BF)] * 2, flops=1 << 22, nbytes=1 << 20
     )
     whole_hg = lax.all_gather(hidden_grad, ("zl", "core"), axis=0, tiled=True).reshape(8, Q, HT)
-    whole_av = lax.all_gather(activated, ("zl", "core"), axis=0, tiled=True).reshape(8, Q, HT)
     partial = input_grad_partial(w1_where, ids, whole_hg, w1_blocks)
+    (wide,) = call(widen_body, (activated,), [((Q, HT), F32)], flops=1 << 16, nbytes=1 << 18, after=(partial,))
+    whole_av = lax.all_gather(wide, ("zl", "core"), axis=0)
     w1_grad = block_grads(w1_pos, 0, w1_where, whole_hg, parts)
     w2_grad = block_grads(w2_pos, NI, w2_where, whole_av, parts)
-    input_grad = row_reduce(partial, (whole_av[0, :16, :BS], w1_grad[0, :8]))
+    input_grad = row_reduce(partial, (w1_grad[0, :8],), (w2_grad[0, :8],))
     return input_grad, w1_grad, w2_grad
 
 

time: 177 us -> 189 us (1.068)
  waiting for transfers between devices: 17.2 us -> 32.8 us
  blocking collectives: 86.4 us -> 70.9 us
  between operations: 0.87 us -> 14.2 us
  starting transfers between devices: 49 us -> 44 us
  local copies, waits for them, and re-layouts: 8.46 us -> 11.8 us
    all_gather x1 -> x0, blocking collectives: 15.7 us -> none  [shards(): lax.all_gather(activated, ('zl', 'core'), axis=0, tiled=True)]
    all_to_all x1, waiting for transfers between devices: 3.03 us -> 18.6 us  [row_reduce(): parts = lax.all_to_all(partial, ('y', 'x'), 0, 0, tiled=True)]
    ppermute x8, starting transfers between devices: 35.8 us -> 31.9 us  [shift(): return lax.ppermute(value, axis, [(i, (i + step) % n) for i in range(n)])]
    unnamed x26 -> x32, local copies, waits for them, and re-layouts: 7.77 us -> 10.3 us
    pallas_call x9 -> x11, Pallas kernels: 12.2 us -> 13.7 us  [call(): pl.pallas_call(lambda *refs: body(*refs[:n], *refs[m:]), out_shape=[shape...]
  transfers between devices with their start and end apart: 10 -> 11, of which waited for: 6 -> 7; matrix products, arithmetic and copies ran while one was open for 0% -> 1% of each run, Pallas kernels for 3% -> 4%
where the time goes in v8:
time: 189 us; the launch traced here: 188 us
  blocking collectives  70.9 us (38%)
  starting transfers between devices  44 us (23%)
  waiting for transfers between devices  32.8 us (17%)
  between operations  14.2 us (8%)
  Pallas kernels  13.7 us (7%)
  local copies, waits for them, and re-layouts  11.8 us (6%)
    ppermute x8, starting transfers between devices, shift(): return lax.ppermute(value, axis, [(i, (i + step) % n) for i in range(n)])  31.9 us
    all_gather x1, blocking collectives, shards(): near = lax.all_gather(both, 'zh', axis=0, tiled=True)  24.5 us
    all_to_all x1, waiting for transfers between devices, row_reduce(): parts = lax.all_to_all(partial, ('y', 'x'), 0, 0, tiled=True)  18.6 us
    all_to_all x1, blocking collectives, column_sums_at_once(): return (mine, lax.all_to_all(sums, 'zl', 0, 0, tiled=True))  18.2 us
    all_gather x1, blocking collectives, shards(): lax.all_gather(hidden_grad, ('zl', 'core'), axis=0, tiled=True)  17 us
    pallas_call x11, Pallas kernels, call(): pl.pallas_call(lambda *refs: body(*refs[:n], *refs[m:]), out_shape=[shape...  13.7 us
    all_gather x1, blocking collectives, shards(): along = lax.all_gather(near, 'x', axis=0)  11.1 us
    unnamed x32, local copies, waits for them, and re-layouts  10.3 us
  transfers between devices with their start and end apart: 11, of which 7 were waited for; matrix products, arithmetic and copies ran while one was open for 1% of the time, Pallas kernels for 4%

profile of v8, /device:TPU:1, one launch (start us, length us, event | category | flops | bytes accessed | tf_op | source)
XLA Modules:
  0.0 188.2 jit_solution(10471983078609288249)
XLA Ops:
  8.0 24.5 %all_gather.18 = bf16[32,3072]{1,0:T(8,128)(2,1)S(1)} all-gather(bf16[8,3072]{1,0:T(8,128)(2,1)S(1)} %pad_maximum_fusion), channel_id=1, replica_groups=mesh['x'=4,'zh'=4,'y'=4,'zl'=4,'core'=2] {'zh'}, dimensions={0}, use_global_device_ids=true | all-gather | bytes 245760 | tf_op jit(solution)/shard_map/all_gather | solution.py:266
  32.5 11.1 %all-gather = bf16[128,3072]{1,0:T(8,128)(2,1)S(1)} all-gather(bf16[32,3072]{1,0:T(8,128)(2,1)S(1)} %all_gather.18), channel_id=2, replica_groups=mesh['x'=4,'zh'=4,'y'=4,'zl'=4,'core'=2] {'x'}, dimensions={0}, use_global_device_ids=true | all-gather | bytes 983040 | tf_op jit(solution)/shard_map/all_gather | solution.py:267
  43.6 4.8 %collective-permute-start.6 = (bf16[4,32,3072]{2,1,0:T(8,128)(2,1)S(1)}, bf16[4,32,3072]{2,1,0:T(8,128)(2,1)S(1)}, u32[]{:S(2)}, u32[]{:S(2)}) collective-permute-start(bf16[4,32,3072]{2,1,0:T(8,128)(2,1)S(1)} %bitcast.14), channel_id=1, source_target_pairs={{0,16},{8,24},{16,0},{24,8},{1,17},{9,25},{17,1},{25,9},{2,18},{10... | collective-permute-start | bytes 2359304 | tf_op jit(solution)/shard_map/ppermute | solution.py:32
  48.4 2.7 %collective-permute-start.5 = (bf16[4,32,3072]{2,1,0:T(8,128)(2,1)S(1)}, bf16[4,32,3072]{2,1,0:T(8,128)(2,1)S(1)}, u32[]{:S(2)}, u32[]{:S(2)}) collective-permute-start(bf16[4,32,3072]{2,1,0:T(8,128)(2,1)S(1)} %bitcast.15), channel_id=1, source_target_pairs={{0,24},{8,0},{16,8},{24,16},{1,25},{9,1},{17,9},{25,17},{2,26},{10... | collective-permute-start | bytes 2359304 | tf_op jit(solution)/shard_map/ppermute | solution.py:32
  51.1 2.6 %collective-permute-start.4 = (bf16[4,32,3072]{2,1,0:T(8,128)(2,1)S(1)}, bf16[4,32,3072]{2,1,0:T(8,128)(2,1)S(1)}, u32[]{:S(2)}, u32[]{:S(2)}) collective-permute-start(bf16[4,32,3072]{2,1,0:T(8,128)(2,1)S(1)} %bitcast.16), channel_id=1, source_target_pairs={{0,8},{8,16},{16,24},{24,0},{1,9},{9,17},{17,25},{25,1},{2,10},{10... | collective-permute-start | bytes 2359304 | tf_op jit(solution)/shard_map/ppermute | solution.py:32
  53.8 1.0 copy-done.10
  57.0 1.0 shard_map.85
  58.1 9.6 %collective-permute-start = (f32[64,1536]{1,0:T(8,128)S(1)}, f32[64,1536]{1,0:T(8,128)S(1)}, u32[]{:S(2)}, u32[]{:S(2)}) collective-permute-start(f32[64,1536]{1,0:T(8,128)S(1)} %get-tuple-element.16), channel_id=1, source_target_pairs={{0,1},{1,0},{2,3},{3,2},{4,5},{5,4},{6,7},{7,6},{8,9},{9,8},{10,11... | collective-permute-start | bytes 1179656 | tf_op jit(solution)/shard_map/ppermute | solution.py:32
  67.7 1.3 collective-permute-done.refs_2_
  69.6 2.5 %collective-permute-start.1 = (bf16[16,1536]{1,0:T(8,128)(2,1)S(1)}, bf16[16,1536]{1,0:T(8,128)(2,1)S(1)}, u32[]{:S(2)}, u32[]{:S(2)}) collective-permute-start(bf16[16,1536]{1,0:T(8,128)(2,1)S(1)} %get-tuple-element.18), channel_id=1, source_target_pairs={{0,2},{2,4},{4,6},{6,0},{1,3},{3,5},{5,7},{7,1},{8,10},{10,12},{12... | collective-permute-start | bytes 147464 | tf_op jit(solution)/shard_map/ppermute | solution.py:32
  72.1 3.2 %collective-permute-start.2 = (bf16[16,1536]{1,0:T(8,128)(2,1)S(1)}, bf16[16,1536]{1,0:T(8,128)(2,1)S(1)}, u32[]{:S(2)}, u32[]{:S(2)}) collective-permute-start(bf16[16,1536]{1,0:T(8,128)(2,1)S(1)} %get-tuple-element.19), channel_id=1, source_target_pairs={{0,4},{2,6},{4,0},{6,2},{1,5},{3,7},{5,1},{7,3},{8,12},{10,14},{12... | collective-permute-start | bytes 147464 | tf_op jit(solution)/shard_map/ppermute | solution.py:32
  76.2 2.9 %collective-permute-start.3 = (bf16[16,1536]{1,0:T(8,128)(2,1)S(1)}, bf16[16,1536]{1,0:T(8,128)(2,1)S(1)}, u32[]{:S(2)}, u32[]{:S(2)}) collective-permute-start(bf16[16,1536]{1,0:T(8,128)(2,1)S(1)} %get-tuple-element.20), channel_id=1, source_target_pairs={{0,6},{2,0},{4,2},{6,4},{1,7},{3,1},{5,3},{7,5},{8,14},{10,8},{12,... | collective-permute-start | bytes 147464 | tf_op jit(solution)/shard_map/ppermute | solution.py:32
  79.1 2.2 %collective-permute-done.3.refs_10_.refs_4_ = bf16[16,1536]{1,0:T(8,128)(2,1)S(1)} collective-permute-done((bf16[16,1536]{1,0:T(8,128)(2,1)S(1)}, bf16[16,1536]{1,0:T(8,128)(2,1)S(1)}, u32[]{:S(2)}, u32[]{:S(2)}) %collective-permute-start.3) | collective-permute-done | bytes 49184 | tf_op jit(solution)/shard_map/ppermute | solution.py:32
  81.4 1.0 collective-permute-done.5.refs_4_
  82.4 1.7 shard_map.87
  84.1 3.7 %collective-permute-start.7 = (f32[192,1536]{1,0:T(8,128)S(1)}, f32[192,1536]{1,0:T(8,128)S(1)}, u32[]{:S(2)}, u32[]{:S(2)}) collective-permute-start(f32[192,1536]{1,0:T(8,128)S(1)} %get-tuple-element.22), channel_id=1, source_target_pairs={{0,1},{1,0},{2,3},{3,2},{4,5},{5,4},{6,7},{7,6},{8,9},{9,8},{10,11... | collective-permute-start | bytes 3538952 | tf_op jit(solution)/shard_map/ppermute | solution.py:32
  87.8 2.5 %collective-permute-done.7.refs_2_ = f32[192,1536]{1,0:T(8,128)S(1)} collective-permute-done((f32[192,1536]{1,0:T(8,128)S(1)}, f32[192,1536]{1,0:T(8,128)S(1)}, u32[]{:S(2)}, u32[]{:S(2)}) %collective-permute-start.7) | collective-permute-done | bytes 1179680 | tf_op jit(solution)/shard_map/ppermute | solution.py:32
  91.1 18.2 %all_to_all.27 = bf16[4,48,1536]{2,1,0:T(8,128)(2,1)S(1)} all-to-all(bf16[4,48,1536]{2,1,0:T(8,128)(2,1)S(1)} %bitcast.24), channel_id=1, replica_groups=mesh['x'=4,'zh'=4,'y'=4,'zl'=4,'core'=2] {'zl'}, dimensions={0} | all-to-all | bytes 1179648 | tf_op jit(solution)/shard_map/all_to_all | solution.py:146
  110.1 17.0 %all_gather.21 = bf16[512,768]{1,0:T(8,128)(2,1)S(1)} all-gather(bf16[64,768]{1,0:T(8,128)(2,1)S(1)} %get-tuple-element.25), channel_id=1, replica_groups=mesh['x'=4,'zh'=4,'y'=4,'zl'=4,'core'=2] {'zl','core'}, dimensions={0}, use_global_device_ids=true | all-gather | bytes 884736 | tf_op jit(solution)/shard_map/all_gather | solution.py:277
  127.1 2.4 %shard_map.90.refs_1_ = bf16[16,32,1536]{2,1,0:T(8,128)(2,1)} custom-call(s32[9]{0:T(128)S(1)} %copy-done.12, s32[3]{0:T(128)S(1)} %pad_add_fusion.refs_2_.refs_0_.refs_1_, bf16[8,64,768]{2,1,0:T(8,128)(2,1)S(1)} %bitcast.20, bf16[9,128,128]{2,1,0:T(8,128)(2,1)S(1)} %copy-done.10), custom_call_target="tpu_custom_call" | custom-call | flops 603979776 | bytes 4194304 | tf_op jit(solution)/shard_map/pallas_call | solution.py:38
  130.3 5.8 %all-to-all-start.1 = ((bf16[16,32,1536]{2,1,0:T(8,128)(2,1)}), bf16[16,32,1536]{2,1,0:T(8,128)(2,1)S(1)}, u32[]{:S(2)}, u32[]{:S(2)}) async-start(bf16[16,32,1536]{2,1,0:T(8,128)(2,1)} %shard_map.90.refs_1_), calls=%async_computation.1 | async-start | bytes 3145728 | tf_op jit(solution)/shard_map/all_to_all | solution.py:249
  136.1 1.1 copy-done.1
  137.2 1.1 copy-done.4
  138.4 1.1 copy-done.7
  139.5 2.0 %shard_map.91 = f32[9,128,128]{2,1,0:T(8,128)} custom-call(s32[9]{0:T(128)S(1)} %copy-done.13, bf16[8,64,768]{2,1,0:T(8,128)(2,1)S(1)} %bitcast.21, bf16[4,32,3072]{2,1,0:T(8,128)(2,1)S(1)} %bitcast.18, bf16[4,32,3072]{2,1,0:T(8,128)(2,1)S(1)} %copy-done.7, bf16[4,32,3072]{2,1,0:T(8,128)(2,1)S(1)} %copy-done.4, bf16[4,32,3072]{2,1,0:T(8,128)(2,1)S(1)} %copy-done.1), custom_call_target="tpu_custom_call" | custom-call | flops 603979776 | bytes 4194304 | tf_op jit(solution)/shard_map/pallas_call | solution.py:38
  142.3 18.6 %all-to-all-done.1.refs_0_ = bf16[16,32,1536]{2,1,0:T(8,128)(2,1)S(1)} async-done(((bf16[16,32,1536]{2,1,0:T(8,128)(2,1)}), bf16[16,32,1536]{2,1,0:T(8,128)(2,1)S(1)}, u32[]{:S(2)}, u32[]{:S(2)}) %all-to-all-start.1) | async-done | bytes 1572896 | tf_op jit(solution)/shard_map/all_to_all | solution.py:249
  161.7 6.3 %all-to-all-start.2 = ((bf16[4,8,1536]{2,1,0:T(8,128)(2,1)}), bf16[4,8,1536]{2,1,0:T(8,128)(2,1)S(1)}, u32[]{:S(2)}, u32[]{:S(2)}) async-start(bf16[4,8,1536]{2,1,0:T(8,128)(2,1)} %bitcast.8), calls=%async_computation.2 | async-start | bytes 196608 | tf_op jit(solution)/shard_map/all_to_all | solution.py:258
  168.1 1.1 copy-done.5
  169.2 1.1 copy-done.8
  170.3 1.4 copy-done.9
  171.7 2.2 %shard_map.94 = f32[9,128,128]{2,1,0:T(8,128)} custom-call(s32[9]{0:T(128)S(1)} %copy-done.15, f32[8,64,768]{2,1,0:T(8,128)S(1)} %bitcast.23, bf16[4,32,3072]{2,1,0:T(8,128)(2,1)S(1)} %bitcast.19, bf16[4,32,3072]{2,1,0:T(8,128)(2,1)S(1)} %copy-done.8, bf16[4,32,3072]{2,1,0:T(8,128)(2,1)S(1)} %copy-done.5, bf16[4,32,3072]{2,1,0:T(8,128)(2,1)S(1)} %copy-done.2), custom_call_target="tpu_custom_call" | custom-call | flops 603979776 | bytes 4194304 | tf_op jit(solution)/shard_map/pallas_call | solution.py:38
  174.6 6.2 %all-to-all-done.2 = bf16[4,8,1536]{2,1,0:T(8,128)(2,1)S(1)} async-done(((bf16[4,8,1536]{2,1,0:T(8,128)(2,1)}), bf16[4,8,1536]{2,1,0:T(8,128)(2,1)S(1)}, u32[]{:S(2)}, u32[]{:S(2)}) %all-to-all-start.2) | async-done | bytes 98336 | tf_op jit(solution)/shard_map/all_to_all | solution.py:258
  (42 shorter events, 9.9 us)
Async XLA Ops:
  7.2 160.9 %all-gather.4.cloned.1.call-start = ((), (), s32[]{:S(2)}) async-start(), calls=%async_computation.3 | async-start | bytes 1769472 | tf_op jit(solution)/shard_map/all_gather | solution.py:280
  43.6 37.8 %collective-permute-start.6 = (bf16[4,32,3072]{2,1,0:T(8,128)(2,1)S(1)}, bf16[4,32,3072]{2,1,0:T(8,128)(2,1)S(1)}, u32[]{:S(2)}, u32[]{:S(2)}) collective-permute-start(bf16[4,32,3072]{2,1,0:T(8,128)(2,1)S(1)} %bitcast.14), channel_id=1, source_target_pairs={{0,16},{8,24},{16,0},{24,8},{1,17},{9,25},{17,1},{25,9},{2,18},{10... | collective-permute-start | bytes 2359304 | tf_op jit(solution)/shard_map/ppermute | solution.py:32
  48.4 34.0 %collective-permute-start.5 = (bf16[4,32,3072]{2,1,0:T(8,128)(2,1)S(1)}, bf16[4,32,3072]{2,1,0:T(8,128)(2,1)S(1)}, u32[]{:S(2)}, u32[]{:S(2)}) collective-permute-start(bf16[4,32,3072]{2,1,0:T(8,128)(2,1)S(1)} %bitcast.15), channel_id=1, source_target_pairs={{0,24},{8,0},{16,8},{24,16},{1,25},{9,1},{17,9},{25,17},{2,26},{10... | collective-permute-start | bytes 2359304 | tf_op jit(solution)/shard_map/ppermute | solution.py:32
  51.1 31.3 %collective-permute-start.4 = (bf16[4,32,3072]{2,1,0:T(8,128)(2,1)S(1)}, bf16[4,32,3072]{2,1,0:T(8,128)(2,1)S(1)}, u32[]{:S(2)}, u32[]{:S(2)}) collective-permute-start(bf16[4,32,3072]{2,1,0:T(8,128)(2,1)S(1)} %bitcast.16), channel_id=1, source_target_pairs={{0,8},{8,16},{16,24},{24,0},{1,9},{9,17},{17,25},{25,1},{2,10},{10... | collective-permute-start | bytes 2359304 | tf_op jit(solution)/shard_map/ppermute | solution.py:32
  53.8 1.0 copy-start.10
  54.8 1.0 copy-start.11
  55.7 0.7 copy-start.12
  56.4 0.7 copy-start.14
  58.1 10.9 %collective-permute-start = (f32[64,1536]{1,0:T(8,128)S(1)}, f32[64,1536]{1,0:T(8,128)S(1)}, u32[]{:S(2)}, u32[]{:S(2)}) collective-permute-start(f32[64,1536]{1,0:T(8,128)S(1)} %get-tuple-element.16), channel_id=1, source_target_pairs={{0,1},{1,0},{2,3},{3,2},{4,5},{5,4},{6,7},{7,6},{8,9},{9,8},{10,11... | collective-permute-start | bytes 1179656 | tf_op jit(solution)/shard_map/ppermute | solution.py:32
  69.6 6.6 %collective-permute-start.1 = (bf16[16,1536]{1,0:T(8,128)(2,1)S(1)}, bf16[16,1536]{1,0:T(8,128)(2,1)S(1)}, u32[]{:S(2)}, u32[]{:S(2)}) collective-permute-start(bf16[16,1536]{1,0:T(8,128)(2,1)S(1)} %get-tuple-element.18), channel_id=1, source_target_pairs={{0,2},{2,4},{4,6},{6,0},{1,3},{3,5},{5,7},{7,1},{8,10},{10,12},{12... | collective-permute-start | bytes 147464 | tf_op jit(solution)/shard_map/ppermute | solution.py:32
  72.1 7.0 %collective-permute-start.2 = (bf16[16,1536]{1,0:T(8,128)(2,1)S(1)}, bf16[16,1536]{1,0:T(8,128)(2,1)S(1)}, u32[]{:S(2)}, u32[]{:S(2)}) collective-permute-start(bf16[16,1536]{1,0:T(8,128)(2,1)S(1)} %get-tuple-element.19), channel_id=1, source_target_pairs={{0,4},{2,6},{4,0},{6,2},{1,5},{3,7},{5,1},{7,3},{8,12},{10,14},{12... | collective-permute-start | bytes 147464 | tf_op jit(solution)/shard_map/ppermute | solution.py:32
  76.2 5.1 %collective-permute-start.3 = (bf16[16,1536]{1,0:T(8,128)(2,1)S(1)}, bf16[16,1536]{1,0:T(8,128)(2,1)S(1)}, u32[]{:S(2)}, u32[]{:S(2)}) collective-permute-start(bf16[16,1536]{1,0:T(8,128)(2,1)S(1)} %get-tuple-element.20), channel_id=1, source_target_pairs={{0,6},{2,0},{4,2},{6,4},{1,7},{3,1},{5,3},{7,5},{8,14},{10,8},{12,... | collective-permute-start | bytes 147464 | tf_op jit(solution)/shard_map/ppermute | solution.py:32
  81.4 2.7 %copy-start = (bf16[4,32,3072]{2,1,0:T(8,128)(2,1)}, bf16[4,32,3072]{2,1,0:T(8,128)(2,1)S(1)}, u32[]{:S(2)}) copy-start(bf16[4,32,3072]{2,1,0:T(8,128)(2,1)S(1)} %collective-permute-done.6.refs_5_) | copy-start | bytes 2359300
  82.4 1.7 copy-start.3
  82.4 1.7 copy-start.6
  84.1 6.1 %collective-permute-start.7 = (f32[192,1536]{1,0:T(8,128)S(1)}, f32[192,1536]{1,0:T(8,128)S(1)}, u32[]{:S(2)}, u32[]{:S(2)}) collective-permute-start(f32[192,1536]{1,0:T(8,128)S(1)} %get-tuple-element.22), channel_id=1, source_target_pairs={{0,1},{1,0},{2,3},{3,2},{4,5},{5,4},{6,7},{7,6},{8,9},{9,8},{10,11... | collective-permute-start | bytes 3538952 | tf_op jit(solution)/shard_map/ppermute | solution.py:32
  130.3 5.8 %copy-start.13 = (s32[9]{0:T(128)S(1)}, s32[9]{0:T(128)}, u32[]{:S(2)}) copy-start(s32[9]{0:T(128)} %refs_0_.8) | copy-start | bytes 112
  130.3 30.6 %all-to-all-start.1 = ((bf16[16,32,1536]{2,1,0:T(8,128)(2,1)}), bf16[16,32,1536]{2,1,0:T(8,128)(2,1)S(1)}, u32[]{:S(2)}, u32[]{:S(2)}) async-start(bf16[16,32,1536]{2,1,0:T(8,128)(2,1)} %shard_map.90.refs_1_), calls=%async_computation.1 | async-start | bytes 3145728 | tf_op jit(solution)/shard_map/all_to_all | solution.py:249
  136.1 1.1 copy-start.1
  137.2 1.1 copy-start.4
  138.4 1.1 copy-start.7
  141.5 26.6 %copy-start.2 = (bf16[4,32,3072]{2,1,0:T(8,128)(2,1)S(1)}, bf16[4,32,3072]{2,1,0:T(8,128)(2,1)}, u32[]{:S(2)}) copy-start(bf16[4,32,3072]{2,1,0:T(8,128)(2,1)} %copy-done) | copy-start | bytes 2359300
  141.5 26.6 %copy-start.15 = (s32[9]{0:T(128)S(1)}, s32[9]{0:T(128)}, u32[]{:S(2)}) copy-start(s32[9]{0:T(128)} %refs_0_.9) | copy-start | bytes 112
  161.7 19.0 %all-to-all-start.2 = ((bf16[4,8,1536]{2,1,0:T(8,128)(2,1)}), bf16[4,8,1536]{2,1,0:T(8,128)(2,1)S(1)}, u32[]{:S(2)}, u32[]{:S(2)}) async-start(bf16[4,8,1536]{2,1,0:T(8,128)(2,1)} %bitcast.8), calls=%async_computation.2 | async-start | bytes 196608 | tf_op jit(solution)/shard_map/all_to_all | solution.py:258
  168.1 1.1 copy-start.5
  169.2 1.1 copy-start.8
  170.3 1.4 copy-start.9
Sparse Core Ops, SparseCore 0:
  130.4 35.8 all-gather.3

commit v9 on v7

--- a/solution.py
+++ b/solution.py
@@ -16,7 +16,7 @@
 NJ = HT // BS
 NB = 9
 Q = TOK // 8
-STEPS = (0, 1, 3, 2)
+STEPS = (0, 2, 1, 3)
 FIRST = Q // 4
 W1_COLS = 384
 W2_COLS = 96

time: 177 us -> 175 us (0.989)
  starting transfers between devices: 49 us -> 45.8 us
  waiting for transfers between devices: 17.2 us -> 19 us
    ppermute x8, starting transfers between devices: 35.8 us -> 33.5 us  [shift(): return lax.ppermute(value, axis, [(i, (i + step) % n) for i in range(n)])]
  transfers between devices with their start and end apart: 10 -> 10, of which waited for: 6 -> 7; matrix products, arithmetic and copies ran while one was open for 0% -> 0% of each run, Pallas kernels for 3% -> 3%
where the time goes in v9:
time: 175 us; the launch traced here: 174 us
  blocking collectives  86.4 us (49%)
  starting transfers between devices  45.8 us (26%)
  waiting for transfers between devices  19 us (11%)
  Pallas kernels  12.1 us (7%)
  local copies, waits for them, and re-layouts  8.46 us (5%)
    ppermute x8, starting transfers between devices, shift(): return lax.ppermute(value, axis, [(i, (i + step) % n) for i in range(n)])  33.5 us
    all_gather x1, blocking collectives, shards(): near = lax.all_gather(both, 'zh', axis=0, tiled=True)  24.5 us
    all_to_all x1, blocking collectives, column_sums_at_once(): return (mine, lax.all_to_all(sums, 'zl', 0, 0, tiled=True))  18 us
    all_gather x1, blocking collectives, shards(): lax.all_gather(hidden_grad, ('zl', 'core'), axis=0, tiled=True)  17 us
    all_gather x1, blocking collectives, shards(): lax.all_gather(activated, ('zl', 'core'), axis=0, tiled=True)  15.7 us
    pallas_call x9, Pallas kernels, call(): pl.pallas_call(lambda *refs: body(*refs[:n], *refs[m:]), out_shape=[shape...  12.1 us
    all_gather x1, blocking collectives, shards(): along = lax.all_gather(near, 'x', axis=0)  11.1 us
    ppermute x8, waiting for transfers between devices, shift(): return lax.ppermute(value, axis, [(i, (i + step) % n) for i in range(n)])  8.67 us
  transfers between devices with their start and end apart: 10, of which 7 were waited for; matrix products, arithmetic and copies ran while one was open for 0% of the time, Pallas kernels for 3%

profile of v9, /device:TPU:1, one launch (start us, length us, event | category | flops | bytes accessed | tf_op | source)
XLA Modules:
  0.0 174.1 jit_solution(7424138813666279781)
XLA Ops:
  1.5 24.5 %all_gather.15 = bf16[32,3072]{1,0:T(8,128)(2,1)S(1)} all-gather(bf16[8,3072]{1,0:T(8,128)(2,1)S(1)} %pad_maximum_fusion), channel_id=1, replica_groups=mesh['x'=4,'zh'=4,'y'=4,'zl'=4,'core'=2] {'zh'}, dimensions={0}, use_global_device_ids=true | all-gather | bytes 245760 | tf_op jit(solution)/shard_map/all_gather | solution.py:257
  26.0 11.1 %all-gather = bf16[128,3072]{1,0:T(8,128)(2,1)S(1)} all-gather(bf16[32,3072]{1,0:T(8,128)(2,1)S(1)} %all_gather.15), channel_id=2, replica_groups=mesh['x'=4,'zh'=4,'y'=4,'zl'=4,'core'=2] {'x'}, dimensions={0}, use_global_device_ids=true | all-gather | bytes 983040 | tf_op jit(solution)/shard_map/all_gather | solution.py:258
  37.1 4.8 %collective-permute-start.4 = (bf16[4,32,3072]{2,1,0:T(8,128)(2,1)S(1)}, bf16[4,32,3072]{2,1,0:T(8,128)(2,1)S(1)}, u32[]{:S(2)}, u32[]{:S(2)}) collective-permute-start(bf16[4,32,3072]{2,1,0:T(8,128)(2,1)S(1)} %bitcast.13), channel_id=1, source_target_pairs={{0,16},{8,24},{16,0},{24,8},{1,17},{9,25},{17,1},{25,9},{2,18},{10... | collective-permute-start | bytes 2359304 | tf_op jit(solution)/shard_map/ppermute | solution.py:32
  41.9 2.3 %collective-permute-start.5 = (bf16[4,32,3072]{2,1,0:T(8,128)(2,1)S(1)}, bf16[4,32,3072]{2,1,0:T(8,128)(2,1)S(1)}, u32[]{:S(2)}, u32[]{:S(2)}) collective-permute-start(bf16[4,32,3072]{2,1,0:T(8,128)(2,1)S(1)} %bitcast.14), channel_id=1, source_target_pairs={{0,8},{8,16},{16,24},{24,0},{1,9},{9,17},{17,25},{25,1},{2,10},{10... | collective-permute-start | bytes 2359304 | tf_op jit(solution)/shard_map/ppermute | solution.py:32
  44.2 4.2 %collective-permute-start.6 = (bf16[4,32,3072]{2,1,0:T(8,128)(2,1)S(1)}, bf16[4,32,3072]{2,1,0:T(8,128)(2,1)S(1)}, u32[]{:S(2)}, u32[]{:S(2)}) collective-permute-start(bf16[4,32,3072]{2,1,0:T(8,128)(2,1)S(1)} %bitcast.15), channel_id=1, source_target_pairs={{0,24},{8,0},{16,8},{24,16},{1,25},{9,1},{17,9},{25,17},{2,26},{10... | collective-permute-start | bytes 2359304 | tf_op jit(solution)/shard_map/ppermute | solution.py:32
  49.5 1.0 shard_map.85
  50.5 9.6 %collective-permute-start = (f32[64,1536]{1,0:T(8,128)S(1)}, f32[64,1536]{1,0:T(8,128)S(1)}, u32[]{:S(2)}, u32[]{:S(2)}) collective-permute-start(f32[64,1536]{1,0:T(8,128)S(1)} %get-tuple-element.16), channel_id=1, source_target_pairs={{0,1},{1,0},{2,3},{3,2},{4,5},{5,4},{6,7},{7,6},{8,9},{9,8},{10,11... | collective-permute-start | bytes 1179656 | tf_op jit(solution)/shard_map/ppermute | solution.py:32
  60.1 1.3 collective-permute-done.refs_2_
  62.0 2.5 %collective-permute-start.1 = (bf16[16,1536]{1,0:T(8,128)(2,1)S(1)}, bf16[16,1536]{1,0:T(8,128)(2,1)S(1)}, u32[]{:S(2)}, u32[]{:S(2)}) collective-permute-start(bf16[16,1536]{1,0:T(8,128)(2,1)S(1)} %get-tuple-element.18), channel_id=1, source_target_pairs={{0,2},{2,4},{4,6},{6,0},{1,3},{3,5},{5,7},{7,1},{8,10},{10,12},{12... | collective-permute-start | bytes 147464 | tf_op jit(solution)/shard_map/ppermute | solution.py:32
  64.5 3.2 %collective-permute-start.2 = (bf16[16,1536]{1,0:T(8,128)(2,1)S(1)}, bf16[16,1536]{1,0:T(8,128)(2,1)S(1)}, u32[]{:S(2)}, u32[]{:S(2)}) collective-permute-start(bf16[16,1536]{1,0:T(8,128)(2,1)S(1)} %get-tuple-element.19), channel_id=1, source_target_pairs={{0,4},{2,6},{4,0},{6,2},{1,5},{3,7},{5,1},{7,3},{8,12},{10,14},{12... | collective-permute-start | bytes 147464 | tf_op jit(solution)/shard_map/ppermute | solution.py:32
  68.7 2.9 %collective-permute-start.3 = (bf16[16,1536]{1,0:T(8,128)(2,1)S(1)}, bf16[16,1536]{1,0:T(8,128)(2,1)S(1)}, u32[]{:S(2)}, u32[]{:S(2)}) collective-permute-start(bf16[16,1536]{1,0:T(8,128)(2,1)S(1)} %get-tuple-element.20), channel_id=1, source_target_pairs={{0,6},{2,0},{4,2},{6,4},{1,7},{3,1},{5,3},{7,5},{8,14},{10,8},{12,... | collective-permute-start | bytes 147464 | tf_op jit(solution)/shard_map/ppermute | solution.py:32
  71.6 2.2 %collective-permute-done.3.refs_10_.refs_4_ = bf16[16,1536]{1,0:T(8,128)(2,1)S(1)} collective-permute-done((bf16[16,1536]{1,0:T(8,128)(2,1)S(1)}, bf16[16,1536]{1,0:T(8,128)(2,1)S(1)}, u32[]{:S(2)}, u32[]{:S(2)}) %collective-permute-start.3) | collective-permute-done | bytes 49184 | tf_op jit(solution)/shard_map/ppermute | solution.py:32
  73.8 1.7 %collective-permute-done.5.refs_4_ = bf16[4,32,3072]{2,1,0:T(8,128)(2,1)S(1)} collective-permute-done((bf16[4,32,3072]{2,1,0:T(8,128)(2,1)S(1)}, bf16[4,32,3072]{2,1,0:T(8,128)(2,1)S(1)}, u32[]{:S(2)}, u32[]{:S(2)}) %collective-permute-start.5) | collective-permute-done | bytes 786464 | tf_op jit(solution)/shard_map/ppermute | solution.py:32
  75.5 1.7 shard_map.87
  77.2 4.1 %collective-permute-start.7 = (f32[192,1536]{1,0:T(8,128)S(1)}, f32[192,1536]{1,0:T(8,128)S(1)}, u32[]{:S(2)}, u32[]{:S(2)}) collective-permute-start(f32[192,1536]{1,0:T(8,128)S(1)} %get-tuple-element.22), channel_id=1, source_target_pairs={{0,1},{1,0},{2,3},{3,2},{4,5},{5,4},{6,7},{7,6},{8,9},{9,8},{10,11... | collective-permute-start | bytes 3538952 | tf_op jit(solution)/shard_map/ppermute | solution.py:32
  81.3 2.5 %collective-permute-done.7.refs_2_ = f32[192,1536]{1,0:T(8,128)S(1)} collective-permute-done((f32[192,1536]{1,0:T(8,128)S(1)}, f32[192,1536]{1,0:T(8,128)S(1)}, u32[]{:S(2)}, u32[]{:S(2)}) %collective-permute-start.7) | collective-permute-done | bytes 1179680 | tf_op jit(solution)/shard_map/ppermute | solution.py:32
  84.4 18.0 %all_to_all.25 = bf16[4,48,1536]{2,1,0:T(8,128)(2,1)S(1)} all-to-all(bf16[4,48,1536]{2,1,0:T(8,128)(2,1)S(1)} %bitcast.24), channel_id=1, replica_groups=mesh['x'=4,'zh'=4,'y'=4,'zl'=4,'core'=2] {'zl'}, dimensions={0} | all-to-all | bytes 1179648 | tf_op jit(solution)/shard_map/all_to_all | solution.py:146
  103.3 17.0 %all_gather.18 = bf16[512,768]{1,0:T(8,128)(2,1)S(1)} all-gather(bf16[64,768]{1,0:T(8,128)(2,1)S(1)} %get-tuple-element.25), channel_id=1, replica_groups=mesh['x'=4,'zh'=4,'y'=4,'zl'=4,'core'=2] {'zl','core'}, dimensions={0}, use_global_device_ids=true | all-gather | bytes 884736 | tf_op jit(solution)/shard_map/all_gather | solution.py:268
  120.3 2.5 %shard_map.90 = bf16[16,32,1536]{2,1,0:T(8,128)(2,1)} custom-call(s32[9]{0:T(128)S(1)} %copy-done.11, s32[3]{0:T(128)S(1)} %pad_add_fusion.refs_2_.refs_0_.refs_1_, bf16[8,64,768]{2,1,0:T(8,128)(2,1)S(1)} %bitcast.19, bf16[9,128,128]{2,1,0:T(8,128)(2,1)S(1)} %copy-done.9), custom_call_target="tpu_custom_call" | custom-call | flops 603979776 | bytes 4194304 | tf_op jit(solution)/shard_map/pallas_call | solution.py:38
  122.8 5.9 %all-to-all-start.1 = ((bf16[16,32,1536]{2,1,0:T(8,128)(2,1)}), bf16[16,32,1536]{2,1,0:T(8,128)(2,1)S(1)}, u32[]{:S(2)}, u32[]{:S(2)}) async-start(bf16[16,32,1536]{2,1,0:T(8,128)(2,1)} %shard_map.90), calls=%async_computation.1 | async-start | bytes 3145728 | tf_op jit(solution)/shard_map/all_to_all | solution.py:241
  128.8 1.1 copy-done.1
  129.9 1.1 copy-done.4
  131.0 1.1 copy-done.7
  132.1 2.0 %shard_map.91 = f32[9,128,128]{2,1,0:T(8,128)} custom-call(s32[9]{0:T(128)S(1)} %copy-done.11, bf16[8,64,768]{2,1,0:T(8,128)(2,1)S(1)} %bitcast.20, bf16[4,32,3072]{2,1,0:T(8,128)(2,1)S(1)} %bitcast.17, bf16[4,32,3072]{2,1,0:T(8,128)(2,1)S(1)} %copy-done.1, bf16[4,32,3072]{2,1,0:T(8,128)(2,1)S(1)} %copy-done.4, bf16[4,32,3072]{2,1,0:T(8,128)(2,1)S(1)} %copy-done.7), custom_call_target="tpu_custom_call" | custom-call | flops 603979776 | bytes 4194304 | tf_op jit(solution)/shard_map/pallas_call | solution.py:38
  134.8 15.7 %all_gather.19 = bf16[512,768]{1,0:T(8,128)(2,1)S(1)} all-gather(bf16[64,768]{1,0:T(8,128)(2,1)S(1)} %get-tuple-element.26), channel_id=1, replica_groups=mesh['x'=4,'zh'=4,'y'=4,'zl'=4,'core'=2] {'zl','core'}, dimensions={0}, use_global_device_ids=true | all-gather | bytes 884736 | tf_op jit(solution)/shard_map/all_gather | solution.py:269
  150.6 3.0 %all-to-all-done.1.refs_0_ = bf16[16,32,1536]{2,1,0:T(8,128)(2,1)S(1)} async-done(((bf16[16,32,1536]{2,1,0:T(8,128)(2,1)}), bf16[16,32,1536]{2,1,0:T(8,128)(2,1)S(1)}, u32[]{:S(2)}, u32[]{:S(2)}) %all-to-all-start.1) | async-done | bytes 1572896 | tf_op jit(solution)/shard_map/all_to_all | solution.py:241
  154.4 6.4 %all-to-all-start.2 = ((bf16[4,8,1536]{2,1,0:T(8,128)(2,1)}), bf16[4,8,1536]{2,1,0:T(8,128)(2,1)S(1)}, u32[]{:S(2)}, u32[]{:S(2)}) async-start(bf16[4,8,1536]{2,1,0:T(8,128)(2,1)} %bitcast.10), calls=%async_computation.2 | async-start | bytes 196608 | tf_op jit(solution)/shard_map/all_to_all | solution.py:250
  160.8 1.1 copy-done.2
  161.9 1.1 copy-done.5
  163.1 1.1 copy-done.8
  164.2 2.0 %shard_map.93 = f32[9,128,128]{2,1,0:T(8,128)} custom-call(s32[9]{0:T(128)S(1)} %copy-done.12, bf16[8,64,768]{2,1,0:T(8,128)(2,1)S(1)} %bitcast.22, bf16[4,32,3072]{2,1,0:T(8,128)(2,1)S(1)} %bitcast.18, bf16[4,32,3072]{2,1,0:T(8,128)(2,1)S(1)} %copy-done.2, bf16[4,32,3072]{2,1,0:T(8,128)(2,1)S(1)} %copy-done.5, bf16[4,32,3072]{2,1,0:T(8,128)(2,1)S(1)} %copy-done.8), custom_call_target="tpu_custom_call" | custom-call | flops 603979776 | bytes 4194304 | tf_op jit(solution)/shard_map/pallas_call | solution.py:38
  166.2 7.3 %all-to-all-done.2 = bf16[4,8,1536]{2,1,0:T(8,128)(2,1)S(1)} async-done(((bf16[4,8,1536]{2,1,0:T(8,128)(2,1)}), bf16[4,8,1536]{2,1,0:T(8,128)(2,1)S(1)}, u32[]{:S(2)}, u32[]{:S(2)}) %all-to-all-start.2) | async-done | bytes 98336 | tf_op jit(solution)/shard_map/all_to_all | solution.py:250
  (33 shorter events, 7.0 us)
Async XLA Ops:
  0.6 47.9 %copy-start.12 = (s32[9]{0:T(128)S(1)}, s32[9]{0:T(128)}, u32[]{:S(2)}) copy-start(s32[9]{0:T(128)} %refs_0_.9) | copy-start | bytes 112
  0.6 47.9 %copy-start.9 = (bf16[9,128,128]{2,1,0:T(8,128)(2,1)S(1)}, bf16[9,128,128]{2,1,0:T(8,128)(2,1)}, u32[]{:S(2)}) copy-start(bf16[9,128,128]{2,1,0:T(8,128)(2,1)} %refs_3_.1) | copy-start | bytes 884740
  0.7 47.9 %copy-start.11 = (s32[9]{0:T(128)S(1)}, s32[9]{0:T(128)}, u32[]{:S(2)}) copy-start(s32[9]{0:T(128)} %refs_0_.8) | copy-start | bytes 112
  37.1 36.7 %collective-permute-start.4 = (bf16[4,32,3072]{2,1,0:T(8,128)(2,1)S(1)}, bf16[4,32,3072]{2,1,0:T(8,128)(2,1)S(1)}, u32[]{:S(2)}, u32[]{:S(2)}) collective-permute-start(bf16[4,32,3072]{2,1,0:T(8,128)(2,1)S(1)} %bitcast.13), channel_id=1, source_target_pairs={{0,16},{8,24},{16,0},{24,8},{1,17},{9,25},{17,1},{25,9},{2,18},{10... | collective-permute-start | bytes 2359304 | tf_op jit(solution)/shard_map/ppermute | solution.py:32
  41.9 33.6 %collective-permute-start.5 = (bf16[4,32,3072]{2,1,0:T(8,128)(2,1)S(1)}, bf16[4,32,3072]{2,1,0:T(8,128)(2,1)S(1)}, u32[]{:S(2)}, u32[]{:S(2)}) collective-permute-start(bf16[4,32,3072]{2,1,0:T(8,128)(2,1)S(1)} %bitcast.14), channel_id=1, source_target_pairs={{0,8},{8,16},{16,24},{24,0},{1,9},{9,17},{17,25},{25,1},{2,10},{10... | collective-permute-start | bytes 2359304 | tf_op jit(solution)/shard_map/ppermute | solution.py:32
  44.2 31.3 %collective-permute-start.6 = (bf16[4,32,3072]{2,1,0:T(8,128)(2,1)S(1)}, bf16[4,32,3072]{2,1,0:T(8,128)(2,1)S(1)}, u32[]{:S(2)}, u32[]{:S(2)}) collective-permute-start(bf16[4,32,3072]{2,1,0:T(8,128)(2,1)S(1)} %bitcast.15), channel_id=1, source_target_pairs={{0,24},{8,0},{16,8},{24,16},{1,25},{9,1},{17,9},{25,17},{2,26},{10... | collective-permute-start | bytes 2359304 | tf_op jit(solution)/shard_map/ppermute | solution.py:32
  48.5 1.0 copy-start.10
  50.5 10.9 %collective-permute-start = (f32[64,1536]{1,0:T(8,128)S(1)}, f32[64,1536]{1,0:T(8,128)S(1)}, u32[]{:S(2)}, u32[]{:S(2)}) collective-permute-start(f32[64,1536]{1,0:T(8,128)S(1)} %get-tuple-element.16), channel_id=1, source_target_pairs={{0,1},{1,0},{2,3},{3,2},{4,5},{5,4},{6,7},{7,6},{8,9},{9,8},{10,11... | collective-permute-start | bytes 1179656 | tf_op jit(solution)/shard_map/ppermute | solution.py:32
  62.0 6.6 %collective-permute-start.1 = (bf16[16,1536]{1,0:T(8,128)(2,1)S(1)}, bf16[16,1536]{1,0:T(8,128)(2,1)S(1)}, u32[]{:S(2)}, u32[]{:S(2)}) collective-permute-start(bf16[16,1536]{1,0:T(8,128)(2,1)S(1)} %get-tuple-element.18), channel_id=1, source_target_pairs={{0,2},{2,4},{4,6},{6,0},{1,3},{3,5},{5,7},{7,1},{8,10},{10,12},{12... | collective-permute-start | bytes 147464 | tf_op jit(solution)/shard_map/ppermute | solution.py:32
  64.5 7.0 %collective-permute-start.2 = (bf16[16,1536]{1,0:T(8,128)(2,1)S(1)}, bf16[16,1536]{1,0:T(8,128)(2,1)S(1)}, u32[]{:S(2)}, u32[]{:S(2)}) collective-permute-start(bf16[16,1536]{1,0:T(8,128)(2,1)S(1)} %get-tuple-element.19), channel_id=1, source_target_pairs={{0,4},{2,6},{4,0},{6,2},{1,5},{3,7},{5,1},{7,3},{8,12},{10,14},{12... | collective-permute-start | bytes 147464 | tf_op jit(solution)/shard_map/ppermute | solution.py:32
  68.7 5.1 %collective-permute-start.3 = (bf16[16,1536]{1,0:T(8,128)(2,1)S(1)}, bf16[16,1536]{1,0:T(8,128)(2,1)S(1)}, u32[]{:S(2)}, u32[]{:S(2)}) collective-permute-start(bf16[16,1536]{1,0:T(8,128)(2,1)S(1)} %get-tuple-element.20), channel_id=1, source_target_pairs={{0,6},{2,0},{4,2},{6,4},{1,7},{3,1},{5,3},{7,5},{8,14},{10,8},{12,... | collective-permute-start | bytes 147464 | tf_op jit(solution)/shard_map/ppermute | solution.py:32
  73.8 3.4 %copy-start = (bf16[4,32,3072]{2,1,0:T(8,128)(2,1)}, bf16[4,32,3072]{2,1,0:T(8,128)(2,1)S(1)}, u32[]{:S(2)}) copy-start(bf16[4,32,3072]{2,1,0:T(8,128)(2,1)S(1)} %collective-permute-done.4.refs_3_) | copy-start | bytes 2359300
  75.5 1.7 copy-start.3
  75.5 1.7 copy-start.6
  77.2 6.5 %collective-permute-start.7 = (f32[192,1536]{1,0:T(8,128)S(1)}, f32[192,1536]{1,0:T(8,128)S(1)}, u32[]{:S(2)}, u32[]{:S(2)}) collective-permute-start(f32[192,1536]{1,0:T(8,128)S(1)} %get-tuple-element.22), channel_id=1, source_target_pairs={{0,1},{1,0},{2,3},{3,2},{4,5},{5,4},{6,7},{7,6},{8,9},{9,8},{10,11... | collective-permute-start | bytes 3538952 | tf_op jit(solution)/shard_map/ppermute | solution.py:32
  122.8 30.8 %all-to-all-start.1 = ((bf16[16,32,1536]{2,1,0:T(8,128)(2,1)}), bf16[16,32,1536]{2,1,0:T(8,128)(2,1)S(1)}, u32[]{:S(2)}, u32[]{:S(2)}) async-start(bf16[16,32,1536]{2,1,0:T(8,128)(2,1)} %shard_map.90), calls=%async_computation.1 | async-start | bytes 3145728 | tf_op jit(solution)/shard_map/all_to_all | solution.py:241
  128.7 1.1 copy-start.1
  129.9 1.1 copy-start.4
  131.0 1.1 copy-start.7
  154.4 19.1 %all-to-all-start.2 = ((bf16[4,8,1536]{2,1,0:T(8,128)(2,1)}), bf16[4,8,1536]{2,1,0:T(8,128)(2,1)S(1)}, u32[]{:S(2)}, u32[]{:S(2)}) async-start(bf16[4,8,1536]{2,1,0:T(8,128)(2,1)} %bitcast.10), calls=%async_computation.2 | async-start | bytes 196608 | tf_op jit(solution)/shard_map/all_to_all | solution.py:250
  160.8 1.1 copy-start.2
  161.9 1.1 copy-start.5
  163.1 1.1 copy-start.8

commit v10 on v9

--- a/solution.py
+++ b/solution.py
@@ -209,25 +209,24 @@
     return out
 
 
-def block_grad_body(pos, first, where, hid, *refs):
-    parts, out = refs[:4], refs[4]
+def block_grad_body(where1, where2, hg, av, *refs):
+    parts, (out1, out2) = refs[:4], refs[4:]
     for b in range(NB):
-        i, j = pos(where[b])
-        left, right = rows_of(parts, first, i), tokens_of(hid, j)
-        if first:
-            left, right = right, left
-        out[b] = dot(left, right, TN)
-
-
-def block_grads(pos, first, where, hid, parts):
-    (out,) = call(
-        lambda *refs: block_grad_body(pos, first, *refs),
-        (where, hid, *parts),
-        [((NB, BS, BS), F32)],
-        flops=2 * NB * TOK * BS * BS * 4,
-        nbytes=4 << 20,
-    )
-    return out
+        i, j = w1_pos(where1[b])
+        out1[b] = dot(rows_of(parts, 0, i), tokens_of(hg, j), TN)
+        i, j = w2_pos(where2[b])
+        out2[b] = dot(tokens_of(av, j), rows_of(parts, NI, i), TN)
+
+
+def block_grads(where1, where2, hg, av, parts):
+    return call(
+        block_grad_body,
+        (where1, where2, hg, av, *parts),
+        [((NB, BS, BS), F32)] * 2,
+        flops=2 * NB * TOK * BS * BS * 8,
+        nbytes=8 << 20,
+        vmem=20,
+    )
 
 
 def sum_body(parts, out):
@@ -268,9 +267,8 @@
     whole_hg = lax.all_gather(hidden_grad, ("zl", "core"), axis=0, tiled=True).reshape(8, Q, HT)
     whole_av = lax.all_gather(activated, ("zl", "core"), axis=0, tiled=True).reshape(8, Q, HT)
     partial = input_grad_partial(w1_where, ids, whole_hg, w1_blocks)
-    w1_grad = block_grads(w1_pos, 0, w1_where, whole_hg, parts)
-    w2_grad = block_grads(w2_pos, NI, w2_where, whole_av, parts)
-    input_grad = row_reduce(partial, (whole_av[0, :16, :BS], w1_grad[0, :8]))
+    w1_grad, w2_grad = block_grads(w1_where, w2_where, whole_hg, whole_av, parts)
+    input_grad = row_reduce(partial, (w2_grad[0, :8],))
     return input_grad, w1_grad, w2_grad
 
 

time: 175 us -> 176 us (level)
  blocking collectives: 86.4 us -> 105 us
  waiting for transfers between devices: 19 us -> 9.17 us
  local copies, waits for them, and re-layouts: 8.46 us -> 5.07 us
  starting transfers between devices: 45.8 us -> 42.9 us
  Pallas kernels: 12.1 us -> 10.1 us
    all_to_all x0 -> x1, blocking collectives: none -> 18.9 us  [row_reduce(): last = lax.all_to_all(mine, 'zh', 0, 0, tiled=True)]
    all_to_all x1 -> x0, waiting for transfers between devices: 7.29 us -> none  [row_reduce(): last = lax.all_to_all(mine, 'zh', 0, 0, tiled=True)]
    all_to_all x1 -> x0, starting transfers between devices: 6.35 us -> none  [row_reduce(): last = lax.all_to_all(mine, 'zh', 0, 0, tiled=True)]
    ppermute x8, starting transfers between devices: 33.5 us -> 39.2 us  [shift(): return lax.ppermute(value, axis, [(i, (i + step) % n) for i in range(n)])]
    unnamed x26 -> x20, local copies, waits for them, and re-layouts: 7.77 us -> 4.38 us
    all_to_all x1, starting transfers between devices: 5.93 us -> 3.72 us  [row_reduce(): parts = lax.all_to_all(partial, ('y', 'x'), 0, 0, tiled=True)]
    pallas_call x9 -> x8, Pallas kernels: 12.1 us -> 10.1 us  [call(): pl.pallas_call(lambda *refs: body(*refs[:n], *refs[m:]), out_shape=[shape...]
  transfers between devices with their start and end apart: 10 -> 9, of which waited for: 7 -> 5; matrix products, arithmetic and copies ran while one was open for 0% -> 0% of each run, Pallas kernels for 3% -> 2%
where the time goes in v10:
time: 176 us; the launch traced here: 175 us
  blocking collectives  105 us (60%)
  starting transfers between devices  42.9 us (24%)
  Pallas kernels  10.1 us (6%)
  waiting for transfers between devices  9.17 us (5%)
  local copies, waits for them, and re-layouts  5.07 us (3%)
    ppermute x8, starting transfers between devices, shift(): return lax.ppermute(value, axis, [(i, (i + step) % n) for i in range(n)])  39.2 us
    all_gather x1, blocking collectives, shards(): near = lax.all_gather(both, 'zh', axis=0, tiled=True)  24.5 us
    all_to_all x1, blocking collectives, row_reduce(): last = lax.all_to_all(mine, 'zh', 0, 0, tiled=True)  18.9 us
    all_to_all x1, blocking collectives, column_sums_at_once(): return (mine, lax.all_to_all(sums, 'zl', 0, 0, tiled=True))  18 us
    all_gather x1, blocking collectives, shards(): lax.all_gather(hidden_grad, ('zl', 'core'), axis=0, tiled=True)  17 us
    all_gather x1, blocking collectives, shards(): lax.all_gather(activated, ('zl', 'core'), axis=0, tiled=True)  15.9 us
    all_gather x1, blocking collectives, shards(): along = lax.all_gather(near, 'x', axis=0)  11.1 us
    pallas_call x8, Pallas kernels, call(): pl.pallas_call(lambda *refs: body(*refs[:n], *refs[m:]), out_shape=[shape...  10.1 us
  transfers between devices with their start and end apart: 9, of which 5 were waited for; matrix products, arithmetic and copies ran while one was open for 0% of the time, Pallas kernels for 2%

profile of v10, /device:TPU:1, one launch (start us, length us, event | category | flops | bytes accessed | tf_op | source)
XLA Modules:
  0.0 175.0 jit_solution(10646967947003318302)
XLA Ops:
  0.7 0.8 pad_maximum_fusion
  1.5 24.5 %all_gather.15 = bf16[32,3072]{1,0:T(8,128)(2,1)S(1)} all-gather(bf16[8,3072]{1,0:T(8,128)(2,1)S(1)} %pad_maximum_fusion), channel_id=1, replica_groups=mesh['x'=4,'zh'=4,'y'=4,'zl'=4,'core'=2] {'zh'}, dimensions={0}, use_global_device_ids=true | all-gather | bytes 245760 | tf_op jit(solution)/shard_map/all_gather | solution.py:256
  26.0 11.1 %all-gather = bf16[128,3072]{1,0:T(8,128)(2,1)S(1)} all-gather(bf16[32,3072]{1,0:T(8,128)(2,1)S(1)} %all_gather.15), channel_id=2, replica_groups=mesh['x'=4,'zh'=4,'y'=4,'zl'=4,'core'=2] {'x'}, dimensions={0}, use_global_device_ids=true | all-gather | bytes 983040 | tf_op jit(solution)/shard_map/all_gather | solution.py:257
  37.1 4.6 %collective-permute-start.6 = (bf16[4,32,3072]{2,1,0:T(8,128)(2,1)S(1)}, bf16[4,32,3072]{2,1,0:T(8,128)(2,1)S(1)}, u32[]{:S(2)}, u32[]{:S(2)}) collective-permute-start(bf16[4,32,3072]{2,1,0:T(8,128)(2,1)S(1)} %bitcast.11), channel_id=1, source_target_pairs={{0,24},{8,0},{16,8},{24,16},{1,25},{9,1},{17,9},{25,17},{2,26},{10... | collective-permute-start | bytes 2359304 | tf_op jit(solution)/shard_map/ppermute | solution.py:32
  41.7 1.9 %collective-permute-start.5 = (bf16[4,32,3072]{2,1,0:T(8,128)(2,1)S(1)}, bf16[4,32,3072]{2,1,0:T(8,128)(2,1)S(1)}, u32[]{:S(2)}, u32[]{:S(2)}) collective-permute-start(bf16[4,32,3072]{2,1,0:T(8,128)(2,1)S(1)} %bitcast.12), channel_id=1, source_target_pairs={{0,8},{8,16},{16,24},{24,0},{1,9},{9,17},{17,25},{25,1},{2,10},{10... | collective-permute-start | bytes 2359304 | tf_op jit(solution)/shard_map/ppermute | solution.py:32
  43.7 3.5 %collective-permute-start.4 = (bf16[4,32,3072]{2,1,0:T(8,128)(2,1)S(1)}, bf16[4,32,3072]{2,1,0:T(8,128)(2,1)S(1)}, u32[]{:S(2)}, u32[]{:S(2)}) collective-permute-start(bf16[4,32,3072]{2,1,0:T(8,128)(2,1)S(1)} %bitcast.13), channel_id=1, source_target_pairs={{0,16},{8,24},{16,0},{24,8},{1,17},{9,25},{17,1},{25,9},{2,18},{10... | collective-permute-start | bytes 2359304 | tf_op jit(solution)/shard_map/ppermute | solution.py:32
  47.3 1.0 copy-done.7
  48.3 1.0 shard_map.85
  49.3 9.6 %collective-permute-start = (f32[64,1536]{1,0:T(8,128)S(1)}, f32[64,1536]{1,0:T(8,128)S(1)}, u32[]{:S(2)}, u32[]{:S(2)}) collective-permute-start(f32[64,1536]{1,0:T(8,128)S(1)} %get-tuple-element.18), channel_id=1, source_target_pairs={{0,1},{1,0},{2,3},{3,2},{4,5},{5,4},{6,7},{7,6},{8,9},{9,8},{10,11... | collective-permute-start | bytes 1179656 | tf_op jit(solution)/shard_map/ppermute | solution.py:32
  58.9 1.3 collective-permute-done.refs_2_
  60.8 2.5 %collective-permute-start.1 = (bf16[16,1536]{1,0:T(8,128)(2,1)S(1)}, bf16[16,1536]{1,0:T(8,128)(2,1)S(1)}, u32[]{:S(2)}, u32[]{:S(2)}) collective-permute-start(bf16[16,1536]{1,0:T(8,128)(2,1)S(1)} %get-tuple-element.20), channel_id=1, source_target_pairs={{0,2},{2,4},{4,6},{6,0},{1,3},{3,5},{5,7},{7,1},{8,10},{10,12},{12... | collective-permute-start | bytes 147464 | tf_op jit(solution)/shard_map/ppermute | solution.py:32
  63.3 3.2 %collective-permute-start.2 = (bf16[16,1536]{1,0:T(8,128)(2,1)S(1)}, bf16[16,1536]{1,0:T(8,128)(2,1)S(1)}, u32[]{:S(2)}, u32[]{:S(2)}) collective-permute-start(bf16[16,1536]{1,0:T(8,128)(2,1)S(1)} %get-tuple-element.21), channel_id=1, source_target_pairs={{0,4},{2,6},{4,0},{6,2},{1,5},{3,7},{5,1},{7,3},{8,12},{10,14},{12... | collective-permute-start | bytes 147464 | tf_op jit(solution)/shard_map/ppermute | solution.py:32
  66.5 0.9 collective-permute-done.1.refs_8_.refs_2_
  67.5 2.9 %collective-permute-start.3 = (bf16[16,1536]{1,0:T(8,128)(2,1)S(1)}, bf16[16,1536]{1,0:T(8,128)(2,1)S(1)}, u32[]{:S(2)}, u32[]{:S(2)}) collective-permute-start(bf16[16,1536]{1,0:T(8,128)(2,1)S(1)} %get-tuple-element.22), channel_id=1, source_target_pairs={{0,6},{2,0},{4,2},{6,4},{1,7},{3,1},{5,3},{7,5},{8,14},{10,8},{12,... | collective-permute-start | bytes 147464 | tf_op jit(solution)/shard_map/ppermute | solution.py:32
  70.3 2.2 %collective-permute-done.3.refs_10_.refs_4_ = bf16[16,1536]{1,0:T(8,128)(2,1)S(1)} collective-permute-done((bf16[16,1536]{1,0:T(8,128)(2,1)S(1)}, bf16[16,1536]{1,0:T(8,128)(2,1)S(1)}, u32[]{:S(2)}, u32[]{:S(2)}) %collective-permute-start.3) | collective-permute-done | bytes 49184 | tf_op jit(solution)/shard_map/ppermute | solution.py:32
  72.7 1.7 shard_map.87
  74.3 10.9 %collective-permute-start.7 = (f32[192,1536]{1,0:T(8,128)S(1)}, f32[192,1536]{1,0:T(8,128)S(1)}, u32[]{:S(2)}, u32[]{:S(2)}) collective-permute-start(f32[192,1536]{1,0:T(8,128)S(1)} %get-tuple-element.24), channel_id=1, source_target_pairs={{0,1},{1,0},{2,3},{3,2},{4,5},{5,4},{6,7},{7,6},{8,9},{9,8},{10,11... | collective-permute-start | bytes 3538952 | tf_op jit(solution)/shard_map/ppermute | solution.py:32
  85.3 2.5 %collective-permute-done.7.refs_2_ = f32[192,1536]{1,0:T(8,128)S(1)} collective-permute-done((f32[192,1536]{1,0:T(8,128)S(1)}, f32[192,1536]{1,0:T(8,128)S(1)}, u32[]{:S(2)}, u32[]{:S(2)}) %collective-permute-start.7) | collective-permute-done | bytes 1179680 | tf_op jit(solution)/shard_map/ppermute | solution.py:32
  87.7 0.7 shard_map.88
  88.4 18.0 %all_to_all.25 = bf16[4,48,1536]{2,1,0:T(8,128)(2,1)S(1)} all-to-all(bf16[4,48,1536]{2,1,0:T(8,128)(2,1)S(1)} %bitcast.20), channel_id=1, replica_groups=mesh['x'=4,'zh'=4,'y'=4,'zl'=4,'core'=2] {'zl'}, dimensions={0} | all-to-all | bytes 1179648 | tf_op jit(solution)/shard_map/all_to_all | solution.py:146
  106.4 0.8 shard_map.89
  107.3 17.0 %all_gather.18 = bf16[512,768]{1,0:T(8,128)(2,1)S(1)} all-gather(bf16[64,768]{1,0:T(8,128)(2,1)S(1)} %get-tuple-element.27), channel_id=1, replica_groups=mesh['x'=4,'zh'=4,'y'=4,'zl'=4,'core'=2] {'zl','core'}, dimensions={0}, use_global_device_ids=true | all-gather | bytes 884736 | tf_op jit(solution)/shard_map/all_gather | solution.py:267
  124.3 2.5 %shard_map.90 = bf16[16,32,1536]{2,1,0:T(8,128)(2,1)} custom-call(s32[9]{0:T(128)S(1)} %copy-done.8, s32[3]{0:T(128)S(1)} %pad_add_fusion.refs_2_.refs_0_.refs_1_, bf16[8,64,768]{2,1,0:T(8,128)(2,1)S(1)} %bitcast.16, bf16[9,128,128]{2,1,0:T(8,128)(2,1)S(1)} %copy-done), custom_call_target="tpu_custom_call" | custom-call | flops 603979776 | bytes 4194304 | tf_op jit(solution)/shard_map/pallas_call | solution.py:38
  126.8 3.7 %all-to-all-start.1 = ((bf16[16,32,1536]{2,1,0:T(8,128)(2,1)}), bf16[16,32,1536]{2,1,0:T(8,128)(2,1)S(1)}, u32[]{:S(2)}, u32[]{:S(2)}) async-start(bf16[16,32,1536]{2,1,0:T(8,128)(2,1)} %shard_map.90), calls=%async_computation.1 | async-start | bytes 3145728 | tf_op jit(solution)/shard_map/all_to_all | solution.py:240
  130.5 15.9 %all_gather.19 = bf16[512,768]{1,0:T(8,128)(2,1)S(1)} all-gather(bf16[64,768]{1,0:T(8,128)(2,1)S(1)} %get-tuple-element.28), channel_id=1, replica_groups=mesh['x'=4,'zh'=4,'y'=4,'zl'=4,'core'=2] {'zl','core'}, dimensions={0}, use_global_device_ids=true | all-gather | bytes 884736 | tf_op jit(solution)/shard_map/all_gather | solution.py:268
  146.4 1.1 copy-done.2
  147.5 1.1 copy-done.4
  148.6 1.1 copy-done.6
  149.8 2.7 %shard_map.91 = (f32[9,128,128]{2,1,0:T(8,128)}, f32[9,128,128]{2,1,0:T(8,128)}) custom-call(s32[9]{0:T(128)S(1)} %copy-done.8, s32[9]{0:T(128)S(1)} %copy-done.9, bf16[8,64,768]{2,1,0:T(8,128)(2,1)S(1)} %bitcast.17, bf16[8,64,768]{2,1,0:T(8,128)(2,1)S(1)} %bitcast.18, bf16[4,32,3072]{2,1,0:T(8,128)(2,1)S(1)} %bitcast.15, ...), custom_call_target="tpu_custom_call" | custom-call | flops 1207959552 | bytes 8388608 | tf_op jit(solution)/shard_map/pallas_call | solution.py:38
  152.5 0.7 slice_bitcast_fusion.refs_1_
  153.1 2.2 %all-to-all-done.1.refs_0_ = bf16[16,32,1536]{2,1,0:T(8,128)(2,1)S(1)} async-done(((bf16[16,32,1536]{2,1,0:T(8,128)(2,1)}), bf16[16,32,1536]{2,1,0:T(8,128)(2,1)S(1)}, u32[]{:S(2)}, u32[]{:S(2)}) %all-to-all-start.1) | async-done | bytes 1572896 | tf_op jit(solution)/shard_map/all_to_all | solution.py:240
  155.5 18.9 %all_to_all.26 = bf16[4,8,1536]{2,1,0:T(8,128)(2,1)S(1)} all-to-all(bf16[4,8,1536]{2,1,0:T(8,128)(2,1)S(1)} %bitcast.21), channel_id=1, replica_groups=mesh['x'=4,'zh'=4,'y'=4,'zl'=4,'core'=2] {'zh'}, dimensions={0} | all-to-all | bytes 196608 | tf_op jit(solution)/shard_map/all_to_all | solution.py:249
  (24 shorter events, 1.6 us)
Async XLA Ops:
  0.6 46.7 %copy-start.8 = (s32[9]{0:T(128)S(1)}, s32[9]{0:T(128)}, u32[]{:S(2)}) copy-start(s32[9]{0:T(128)} %refs_0_.7) | copy-start | bytes 112
  0.6 46.7 %copy-start.9 = (s32[9]{0:T(128)S(1)}, s32[9]{0:T(128)}, u32[]{:S(2)}) copy-start(s32[9]{0:T(128)} %refs_1_.5) | copy-start | bytes 112
  0.7 46.7 %copy-start = (bf16[9,128,128]{2,1,0:T(8,128)(2,1)S(1)}, bf16[9,128,128]{2,1,0:T(8,128)(2,1)}, u32[]{:S(2)}) copy-start(bf16[9,128,128]{2,1,0:T(8,128)(2,1)} %refs_3_.1) | copy-start | bytes 884740
  37.1 35.5 %collective-permute-start.6 = (bf16[4,32,3072]{2,1,0:T(8,128)(2,1)S(1)}, bf16[4,32,3072]{2,1,0:T(8,128)(2,1)S(1)}, u32[]{:S(2)}, u32[]{:S(2)}) collective-permute-start(bf16[4,32,3072]{2,1,0:T(8,128)(2,1)S(1)} %bitcast.11), channel_id=1, source_target_pairs={{0,24},{8,0},{16,8},{24,16},{1,25},{9,1},{17,9},{25,17},{2,26},{10... | collective-permute-start | bytes 2359304 | tf_op jit(solution)/shard_map/ppermute | solution.py:32
  41.7 30.8 %collective-permute-start.5 = (bf16[4,32,3072]{2,1,0:T(8,128)(2,1)S(1)}, bf16[4,32,3072]{2,1,0:T(8,128)(2,1)S(1)}, u32[]{:S(2)}, u32[]{:S(2)}) collective-permute-start(bf16[4,32,3072]{2,1,0:T(8,128)(2,1)S(1)} %bitcast.12), channel_id=1, source_target_pairs={{0,8},{8,16},{16,24},{24,0},{1,9},{9,17},{17,25},{25,1},{2,10},{10... | collective-permute-start | bytes 2359304 | tf_op jit(solution)/shard_map/ppermute | solution.py:32
  43.7 29.0 %collective-permute-start.4 = (bf16[4,32,3072]{2,1,0:T(8,128)(2,1)S(1)}, bf16[4,32,3072]{2,1,0:T(8,128)(2,1)S(1)}, u32[]{:S(2)}, u32[]{:S(2)}) collective-permute-start(bf16[4,32,3072]{2,1,0:T(8,128)(2,1)S(1)} %bitcast.13), channel_id=1, source_target_pairs={{0,16},{8,24},{16,0},{24,8},{1,17},{9,25},{17,1},{25,9},{2,18},{10... | collective-permute-start | bytes 2359304 | tf_op jit(solution)/shard_map/ppermute | solution.py:32
  47.3 1.0 copy-start.7
  49.3 10.9 %collective-permute-start = (f32[64,1536]{1,0:T(8,128)S(1)}, f32[64,1536]{1,0:T(8,128)S(1)}, u32[]{:S(2)}, u32[]{:S(2)}) collective-permute-start(f32[64,1536]{1,0:T(8,128)S(1)} %get-tuple-element.18), channel_id=1, source_target_pairs={{0,1},{1,0},{2,3},{3,2},{4,5},{5,4},{6,7},{7,6},{8,9},{9,8},{10,11... | collective-permute-start | bytes 1179656 | tf_op jit(solution)/shard_map/ppermute | solution.py:32
  60.8 6.6 %collective-permute-start.1 = (bf16[16,1536]{1,0:T(8,128)(2,1)S(1)}, bf16[16,1536]{1,0:T(8,128)(2,1)S(1)}, u32[]{:S(2)}, u32[]{:S(2)}) collective-permute-start(bf16[16,1536]{1,0:T(8,128)(2,1)S(1)} %get-tuple-element.20), channel_id=1, source_target_pairs={{0,2},{2,4},{4,6},{6,0},{1,3},{3,5},{5,7},{7,1},{8,10},{10,12},{12... | collective-permute-start | bytes 147464 | tf_op jit(solution)/shard_map/ppermute | solution.py:32
  63.3 7.0 %collective-permute-start.2 = (bf16[16,1536]{1,0:T(8,128)(2,1)S(1)}, bf16[16,1536]{1,0:T(8,128)(2,1)S(1)}, u32[]{:S(2)}, u32[]{:S(2)}) collective-permute-start(bf16[16,1536]{1,0:T(8,128)(2,1)S(1)} %get-tuple-element.21), channel_id=1, source_target_pairs={{0,4},{2,6},{4,0},{6,2},{1,5},{3,7},{5,1},{7,3},{8,12},{10,14},{12... | collective-permute-start | bytes 147464 | tf_op jit(solution)/shard_map/ppermute | solution.py:32
  67.5 5.1 %collective-permute-start.3 = (bf16[16,1536]{1,0:T(8,128)(2,1)S(1)}, bf16[16,1536]{1,0:T(8,128)(2,1)S(1)}, u32[]{:S(2)}, u32[]{:S(2)}) collective-permute-start(bf16[16,1536]{1,0:T(8,128)(2,1)S(1)} %get-tuple-element.22), channel_id=1, source_target_pairs={{0,6},{2,0},{4,2},{6,4},{1,7},{3,1},{5,3},{7,5},{8,14},{10,8},{12,... | collective-permute-start | bytes 147464 | tf_op jit(solution)/shard_map/ppermute | solution.py:32
  72.6 1.7 copy-start.1
  72.6 1.7 copy-start.3
  72.6 1.7 copy-start.5
  74.3 13.4 %collective-permute-start.7 = (f32[192,1536]{1,0:T(8,128)S(1)}, f32[192,1536]{1,0:T(8,128)S(1)}, u32[]{:S(2)}, u32[]{:S(2)}) collective-permute-start(f32[192,1536]{1,0:T(8,128)S(1)} %get-tuple-element.24), channel_id=1, source_target_pairs={{0,1},{1,0},{2,3},{3,2},{4,5},{5,4},{6,7},{7,6},{8,9},{9,8},{10,11... | collective-permute-start | bytes 3538952 | tf_op jit(solution)/shard_map/ppermute | solution.py:32
  126.8 28.6 %all-to-all-start.1 = ((bf16[16,32,1536]{2,1,0:T(8,128)(2,1)}), bf16[16,32,1536]{2,1,0:T(8,128)(2,1)S(1)}, u32[]{:S(2)}, u32[]{:S(2)}) async-start(bf16[16,32,1536]{2,1,0:T(8,128)(2,1)} %shard_map.90), calls=%async_computation.1 | async-start | bytes 3145728 | tf_op jit(solution)/shard_map/all_to_all | solution.py:240
  146.4 1.1 copy-start.2
  147.5 1.1 copy-start.4
  148.6 1.1 copy-start.6

commit v11 on v10

--- a/solution.py
+++ b/solution.py
@@ -16,7 +16,7 @@
 NJ = HT // BS
 NB = 9
 Q = TOK // 8
-STEPS = (0, 2, 1, 3)
+STEPS = (0, 3, 1, 2)
 FIRST = Q // 4
 W1_COLS = 384
 W2_COLS = 96

time: 176 us -> 174 us (0.989)
  starting transfers between devices: 42.9 us -> 39.5 us
    ppermute x8, starting transfers between devices: 39.2 us -> 33.5 us  [shift(): return lax.ppermute(value, axis, [(i, (i + step) % n) for i in range(n)])]
    all_to_all x1, starting transfers between devices: 3.72 us -> 5.97 us  [row_reduce(): parts = lax.all_to_all(partial, ('y', 'x'), 0, 0, tiled=True)]
  transfers between devices with their start and end apart: 9 -> 9, of which waited for: 5 -> 6; matrix products, arithmetic and copies ran while one was open for 0% -> 0% of each run, Pallas kernels for 2% -> 3%
where the time goes in v11:
time: 174 us; the launch traced here: 173 us
  blocking collectives  105 us (60%)
  starting transfers between devices  39.5 us (23%)
  waiting for transfers between devices  10.8 us (6%)
  Pallas kernels  10.2 us (6%)
  local copies, waits for them, and re-layouts  5.07 us (3%)
    ppermute x8, starting transfers between devices, shift(): return lax.ppermute(value, axis, [(i, (i + step) % n) for i in range(n)])  33.5 us
    all_gather x1, blocking collectives, shards(): near = lax.all_gather(both, 'zh', axis=0, tiled=True)  24.5 us
    all_to_all x1, blocking collectives, row_reduce(): last = lax.all_to_all(mine, 'zh', 0, 0, tiled=True)  18.8 us
    all_to_all x1, blocking collectives, column_sums_at_once(): return (mine, lax.all_to_all(sums, 'zl', 0, 0, tiled=True))  18 us
    all_gather x1, blocking collectives, shards(): lax.all_gather(hidden_grad, ('zl', 'core'), axis=0, tiled=True)  17 us
    all_gather x1, blocking collectives, shards(): lax.all_gather(activated, ('zl', 'core'), axis=0, tiled=True)  15.9 us
    all_gather x1, blocking collectives, shards(): along = lax.all_gather(near, 'x', axis=0)  11.1 us
    pallas_call x8, Pallas kernels, call(): pl.pallas_call(lambda *refs: body(*refs[:n], *refs[m:]), out_shape=[shape...  10.2 us
  transfers between devices with their start and end apart: 9, of which 6 were waited for; matrix products, arithmetic and copies ran while one was open for 0% of the time, Pallas kernels for 3%

profile of v11, /device:TPU:1, one launch (start us, length us, event | category | flops | bytes accessed | tf_op | source)
XLA Modules:
  0.0 173.3 jit_solution(492084188730811745)
XLA Ops:
  0.7 0.8 pad_maximum_fusion
  1.5 24.5 %all_gather.15 = bf16[32,3072]{1,0:T(8,128)(2,1)S(1)} all-gather(bf16[8,3072]{1,0:T(8,128)(2,1)S(1)} %pad_maximum_fusion), channel_id=1, replica_groups=mesh['x'=4,'zh'=4,'y'=4,'zl'=4,'core'=2] {'zh'}, dimensions={0}, use_global_device_ids=true | all-gather | bytes 245760 | tf_op jit(solution)/shard_map/all_gather | solution.py:256
  26.0 11.1 %all-gather = bf16[128,3072]{1,0:T(8,128)(2,1)S(1)} all-gather(bf16[32,3072]{1,0:T(8,128)(2,1)S(1)} %all_gather.15), channel_id=2, replica_groups=mesh['x'=4,'zh'=4,'y'=4,'zl'=4,'core'=2] {'x'}, dimensions={0}, use_global_device_ids=true | all-gather | bytes 983040 | tf_op jit(solution)/shard_map/all_gather | solution.py:257
  37.1 4.8 %collective-permute-start.6 = (bf16[4,32,3072]{2,1,0:T(8,128)(2,1)S(1)}, bf16[4,32,3072]{2,1,0:T(8,128)(2,1)S(1)}, u32[]{:S(2)}, u32[]{:S(2)}) collective-permute-start(bf16[4,32,3072]{2,1,0:T(8,128)(2,1)S(1)} %bitcast.11), channel_id=1, source_target_pairs={{0,16},{8,24},{16,0},{24,8},{1,17},{9,25},{17,1},{25,9},{2,18},{10... | collective-permute-start | bytes 2359304 | tf_op jit(solution)/shard_map/ppermute | solution.py:32
  41.9 2.3 %collective-permute-start.5 = (bf16[4,32,3072]{2,1,0:T(8,128)(2,1)S(1)}, bf16[4,32,3072]{2,1,0:T(8,128)(2,1)S(1)}, u32[]{:S(2)}, u32[]{:S(2)}) collective-permute-start(bf16[4,32,3072]{2,1,0:T(8,128)(2,1)S(1)} %bitcast.12), channel_id=1, source_target_pairs={{0,8},{8,16},{16,24},{24,0},{1,9},{9,17},{17,25},{25,1},{2,10},{10... | collective-permute-start | bytes 2359304 | tf_op jit(solution)/shard_map/ppermute | solution.py:32
  44.2 4.2 %collective-permute-start.4 = (bf16[4,32,3072]{2,1,0:T(8,128)(2,1)S(1)}, bf16[4,32,3072]{2,1,0:T(8,128)(2,1)S(1)}, u32[]{:S(2)}, u32[]{:S(2)}) collective-permute-start(bf16[4,32,3072]{2,1,0:T(8,128)(2,1)S(1)} %bitcast.13), channel_id=1, source_target_pairs={{0,24},{8,0},{16,8},{24,16},{1,25},{9,1},{17,9},{25,17},{2,26},{10... | collective-permute-start | bytes 2359304 | tf_op jit(solution)/shard_map/ppermute | solution.py:32
  48.5 1.0 copy-done.7
  49.5 1.0 shard_map.85
  50.5 9.6 %collective-permute-start = (f32[64,1536]{1,0:T(8,128)S(1)}, f32[64,1536]{1,0:T(8,128)S(1)}, u32[]{:S(2)}, u32[]{:S(2)}) collective-permute-start(f32[64,1536]{1,0:T(8,128)S(1)} %get-tuple-element.18), channel_id=1, source_target_pairs={{0,1},{1,0},{2,3},{3,2},{4,5},{5,4},{6,7},{7,6},{8,9},{9,8},{10,11... | collective-permute-start | bytes 1179656 | tf_op jit(solution)/shard_map/ppermute | solution.py:32
  60.1 1.3 collective-permute-done.refs_2_
  62.0 2.5 %collective-permute-start.1 = (bf16[16,1536]{1,0:T(8,128)(2,1)S(1)}, bf16[16,1536]{1,0:T(8,128)(2,1)S(1)}, u32[]{:S(2)}, u32[]{:S(2)}) collective-permute-start(bf16[16,1536]{1,0:T(8,128)(2,1)S(1)} %get-tuple-element.20), channel_id=1, source_target_pairs={{0,2},{2,4},{4,6},{6,0},{1,3},{3,5},{5,7},{7,1},{8,10},{10,12},{12... | collective-permute-start | bytes 147464 | tf_op jit(solution)/shard_map/ppermute | solution.py:32
  64.5 3.2 %collective-permute-start.2 = (bf16[16,1536]{1,0:T(8,128)(2,1)S(1)}, bf16[16,1536]{1,0:T(8,128)(2,1)S(1)}, u32[]{:S(2)}, u32[]{:S(2)}) collective-permute-start(bf16[16,1536]{1,0:T(8,128)(2,1)S(1)} %get-tuple-element.21), channel_id=1, source_target_pairs={{0,4},{2,6},{4,0},{6,2},{1,5},{3,7},{5,1},{7,3},{8,12},{10,14},{12... | collective-permute-start | bytes 147464 | tf_op jit(solution)/shard_map/ppermute | solution.py:32
  67.8 0.9 collective-permute-done.1.refs_8_.refs_2_
  68.7 2.9 %collective-permute-start.3 = (bf16[16,1536]{1,0:T(8,128)(2,1)S(1)}, bf16[16,1536]{1,0:T(8,128)(2,1)S(1)}, u32[]{:S(2)}, u32[]{:S(2)}) collective-permute-start(bf16[16,1536]{1,0:T(8,128)(2,1)S(1)} %get-tuple-element.22), channel_id=1, source_target_pairs={{0,6},{2,0},{4,2},{6,4},{1,7},{3,1},{5,3},{7,5},{8,14},{10,8},{12,... | collective-permute-start | bytes 147464 | tf_op jit(solution)/shard_map/ppermute | solution.py:32
  71.6 2.2 %collective-permute-done.3.refs_10_.refs_4_ = bf16[16,1536]{1,0:T(8,128)(2,1)S(1)} collective-permute-done((bf16[16,1536]{1,0:T(8,128)(2,1)S(1)}, bf16[16,1536]{1,0:T(8,128)(2,1)S(1)}, u32[]{:S(2)}, u32[]{:S(2)}) %collective-permute-start.3) | collective-permute-done | bytes 49184 | tf_op jit(solution)/shard_map/ppermute | solution.py:32
  73.8 1.8 %collective-permute-done.5.refs_4_.refs_6_ = bf16[4,32,3072]{2,1,0:T(8,128)(2,1)S(1)} collective-permute-done((bf16[4,32,3072]{2,1,0:T(8,128)(2,1)S(1)}, bf16[4,32,3072]{2,1,0:T(8,128)(2,1)S(1)}, u32[]{:S(2)}, u32[]{:S(2)}) %collective-permute-start.5) | collective-permute-done | bytes 786464 | tf_op jit(solution)/shard_map/ppermute | solution.py:32
  75.5 1.7 shard_map.87
  77.2 4.0 %collective-permute-start.7 = (f32[192,1536]{1,0:T(8,128)S(1)}, f32[192,1536]{1,0:T(8,128)S(1)}, u32[]{:S(2)}, u32[]{:S(2)}) collective-permute-start(f32[192,1536]{1,0:T(8,128)S(1)} %get-tuple-element.24), channel_id=1, source_target_pairs={{0,1},{1,0},{2,3},{3,2},{4,5},{5,4},{6,7},{7,6},{8,9},{9,8},{10,11... | collective-permute-start | bytes 3538952 | tf_op jit(solution)/shard_map/ppermute | solution.py:32
  81.3 2.5 %collective-permute-done.7.refs_2_ = f32[192,1536]{1,0:T(8,128)S(1)} collective-permute-done((f32[192,1536]{1,0:T(8,128)S(1)}, f32[192,1536]{1,0:T(8,128)S(1)}, u32[]{:S(2)}, u32[]{:S(2)}) %collective-permute-start.7) | collective-permute-done | bytes 1179680 | tf_op jit(solution)/shard_map/ppermute | solution.py:32
  84.4 18.0 %all_to_all.25 = bf16[4,48,1536]{2,1,0:T(8,128)(2,1)S(1)} all-to-all(bf16[4,48,1536]{2,1,0:T(8,128)(2,1)S(1)} %bitcast.20), channel_id=1, replica_groups=mesh['x'=4,'zh'=4,'y'=4,'zl'=4,'core'=2] {'zl'}, dimensions={0} | all-to-all | bytes 1179648 | tf_op jit(solution)/shard_map/all_to_all | solution.py:146
  102.5 0.8 shard_map.89
  103.3 17.0 %all_gather.18 = bf16[512,768]{1,0:T(8,128)(2,1)S(1)} all-gather(bf16[64,768]{1,0:T(8,128)(2,1)S(1)} %get-tuple-element.27), channel_id=1, replica_groups=mesh['x'=4,'zh'=4,'y'=4,'zl'=4,'core'=2] {'zl','core'}, dimensions={0}, use_global_device_ids=true | all-gather | bytes 884736 | tf_op jit(solution)/shard_map/all_gather | solution.py:267
  120.3 2.5 %shard_map.90 = bf16[16,32,1536]{2,1,0:T(8,128)(2,1)} custom-call(s32[9]{0:T(128)S(1)} %copy-done.8, s32[3]{0:T(128)S(1)} %pad_add_fusion.refs_2_.refs_0_.refs_1_, bf16[8,64,768]{2,1,0:T(8,128)(2,1)S(1)} %bitcast.16, bf16[9,128,128]{2,1,0:T(8,128)(2,1)S(1)} %copy-done), custom_call_target="tpu_custom_call" | custom-call | flops 603979776 | bytes 4194304 | tf_op jit(solution)/shard_map/pallas_call | solution.py:38
  122.8 6.0 %all-to-all-start.1 = ((bf16[16,32,1536]{2,1,0:T(8,128)(2,1)}), bf16[16,32,1536]{2,1,0:T(8,128)(2,1)S(1)}, u32[]{:S(2)}, u32[]{:S(2)}) async-start(bf16[16,32,1536]{2,1,0:T(8,128)(2,1)} %shard_map.90), calls=%async_computation.1 | async-start | bytes 3145728 | tf_op jit(solution)/shard_map/all_to_all | solution.py:240
  128.8 15.9 %all_gather.19 = bf16[512,768]{1,0:T(8,128)(2,1)S(1)} all-gather(bf16[64,768]{1,0:T(8,128)(2,1)S(1)} %get-tuple-element.28), channel_id=1, replica_groups=mesh['x'=4,'zh'=4,'y'=4,'zl'=4,'core'=2] {'zl','core'}, dimensions={0}, use_global_device_ids=true | all-gather | bytes 884736 | tf_op jit(solution)/shard_map/all_gather | solution.py:268
  144.7 1.1 copy-done.2
  145.8 1.1 copy-done.4
  146.9 1.1 copy-done.6
  148.1 2.7 %shard_map.91 = (f32[9,128,128]{2,1,0:T(8,128)}, f32[9,128,128]{2,1,0:T(8,128)}) custom-call(s32[9]{0:T(128)S(1)} %copy-done.8, s32[9]{0:T(128)S(1)} %copy-done.9, bf16[8,64,768]{2,1,0:T(8,128)(2,1)S(1)} %bitcast.17, bf16[8,64,768]{2,1,0:T(8,128)(2,1)S(1)} %bitcast.18, bf16[4,32,3072]{2,1,0:T(8,128)(2,1)S(1)} %bitcast.15, ...), custom_call_target="tpu_custom_call" | custom-call | flops 1207959552 | bytes 8388608 | tf_op jit(solution)/shard_map/pallas_call | solution.py:38
  150.8 0.7 slice_bitcast_fusion.refs_1_
  151.5 2.2 %all-to-all-done.1.refs_0_ = bf16[16,32,1536]{2,1,0:T(8,128)(2,1)S(1)} async-done(((bf16[16,32,1536]{2,1,0:T(8,128)(2,1)}), bf16[16,32,1536]{2,1,0:T(8,128)(2,1)S(1)}, u32[]{:S(2)}, u32[]{:S(2)}) %all-to-all-start.1) | async-done | bytes 1572896 | tf_op jit(solution)/shard_map/all_to_all | solution.py:240
  153.8 18.8 %all_to_all.26 = bf16[4,8,1536]{2,1,0:T(8,128)(2,1)S(1)} all-to-all(bf16[4,8,1536]{2,1,0:T(8,128)(2,1)S(1)} %bitcast.21), channel_id=1, replica_groups=mesh['x'=4,'zh'=4,'y'=4,'zl'=4,'core'=2] {'zh'}, dimensions={0} | all-to-all | bytes 196608 | tf_op jit(solution)/shard_map/all_to_all | solution.py:249
  (24 shorter events, 2.2 us)
Async XLA Ops:
  0.6 47.9 %copy-start.8 = (s32[9]{0:T(128)S(1)}, s32[9]{0:T(128)}, u32[]{:S(2)}) copy-start(s32[9]{0:T(128)} %refs_0_.7) | copy-start | bytes 112
  0.6 47.9 %copy-start.9 = (s32[9]{0:T(128)S(1)}, s32[9]{0:T(128)}, u32[]{:S(2)}) copy-start(s32[9]{0:T(128)} %refs_1_.5) | copy-start | bytes 112
  0.7 47.9 %copy-start = (bf16[9,128,128]{2,1,0:T(8,128)(2,1)S(1)}, bf16[9,128,128]{2,1,0:T(8,128)(2,1)}, u32[]{:S(2)}) copy-start(bf16[9,128,128]{2,1,0:T(8,128)(2,1)} %refs_3_.1) | copy-start | bytes 884740
  37.1 36.7 %collective-permute-start.6 = (bf16[4,32,3072]{2,1,0:T(8,128)(2,1)S(1)}, bf16[4,32,3072]{2,1,0:T(8,128)(2,1)S(1)}, u32[]{:S(2)}, u32[]{:S(2)}) collective-permute-start(bf16[4,32,3072]{2,1,0:T(8,128)(2,1)S(1)} %bitcast.11), channel_id=1, source_target_pairs={{0,16},{8,24},{16,0},{24,8},{1,17},{9,25},{17,1},{25,9},{2,18},{10... | collective-permute-start | bytes 2359304 | tf_op jit(solution)/shard_map/ppermute | solution.py:32
  41.9 33.6 %collective-permute-start.5 = (bf16[4,32,3072]{2,1,0:T(8,128)(2,1)S(1)}, bf16[4,32,3072]{2,1,0:T(8,128)(2,1)S(1)}, u32[]{:S(2)}, u32[]{:S(2)}) collective-permute-start(bf16[4,32,3072]{2,1,0:T(8,128)(2,1)S(1)} %bitcast.12), channel_id=1, source_target_pairs={{0,8},{8,16},{16,24},{24,0},{1,9},{9,17},{17,25},{25,1},{2,10},{10... | collective-permute-start | bytes 2359304 | tf_op jit(solution)/shard_map/ppermute | solution.py:32
  44.2 31.3 %collective-permute-start.4 = (bf16[4,32,3072]{2,1,0:T(8,128)(2,1)S(1)}, bf16[4,32,3072]{2,1,0:T(8,128)(2,1)S(1)}, u32[]{:S(2)}, u32[]{:S(2)}) collective-permute-start(bf16[4,32,3072]{2,1,0:T(8,128)(2,1)S(1)} %bitcast.13), channel_id=1, source_target_pairs={{0,24},{8,0},{16,8},{24,16},{1,25},{9,1},{17,9},{25,17},{2,26},{10... | collective-permute-start | bytes 2359304 | tf_op jit(solution)/shard_map/ppermute | solution.py:32
  48.5 1.0 copy-start.7
  50.5 10.9 %collective-permute-start = (f32[64,1536]{1,0:T(8,128)S(1)}, f32[64,1536]{1,0:T(8,128)S(1)}, u32[]{:S(2)}, u32[]{:S(2)}) collective-permute-start(f32[64,1536]{1,0:T(8,128)S(1)} %get-tuple-element.18), channel_id=1, source_target_pairs={{0,1},{1,0},{2,3},{3,2},{4,5},{5,4},{6,7},{7,6},{8,9},{9,8},{10,11... | collective-permute-start | bytes 1179656 | tf_op jit(solution)/shard_map/ppermute | solution.py:32
  62.0 6.6 %collective-permute-start.1 = (bf16[16,1536]{1,0:T(8,128)(2,1)S(1)}, bf16[16,1536]{1,0:T(8,128)(2,1)S(1)}, u32[]{:S(2)}, u32[]{:S(2)}) collective-permute-start(bf16[16,1536]{1,0:T(8,128)(2,1)S(1)} %get-tuple-element.20), channel_id=1, source_target_pairs={{0,2},{2,4},{4,6},{6,0},{1,3},{3,5},{5,7},{7,1},{8,10},{10,12},{12... | collective-permute-start | bytes 147464 | tf_op jit(solution)/shard_map/ppermute | solution.py:32
  64.5 7.0 %collective-permute-start.2 = (bf16[16,1536]{1,0:T(8,128)(2,1)S(1)}, bf16[16,1536]{1,0:T(8,128)(2,1)S(1)}, u32[]{:S(2)}, u32[]{:S(2)}) collective-permute-start(bf16[16,1536]{1,0:T(8,128)(2,1)S(1)} %get-tuple-element.21), channel_id=1, source_target_pairs={{0,4},{2,6},{4,0},{6,2},{1,5},{3,7},{5,1},{7,3},{8,12},{10,14},{12... | collective-permute-start | bytes 147464 | tf_op jit(solution)/shard_map/ppermute | solution.py:32
  68.7 5.1 %collective-permute-start.3 = (bf16[16,1536]{1,0:T(8,128)(2,1)S(1)}, bf16[16,1536]{1,0:T(8,128)(2,1)S(1)}, u32[]{:S(2)}, u32[]{:S(2)}) collective-permute-start(bf16[16,1536]{1,0:T(8,128)(2,1)S(1)} %get-tuple-element.22), channel_id=1, source_target_pairs={{0,6},{2,0},{4,2},{6,4},{1,7},{3,1},{5,3},{7,5},{8,14},{10,8},{12,... | collective-permute-start | bytes 147464 | tf_op jit(solution)/shard_map/ppermute | solution.py:32
  73.8 3.4 %copy-start.1 = (bf16[4,32,3072]{2,1,0:T(8,128)(2,1)}, bf16[4,32,3072]{2,1,0:T(8,128)(2,1)S(1)}, u32[]{:S(2)}) copy-start(bf16[4,32,3072]{2,1,0:T(8,128)(2,1)S(1)} %collective-permute-done.6.refs_5_.refs_7_) | copy-start | bytes 2359300
  75.5 1.7 copy-start.3
  75.5 1.7 copy-start.5
  77.2 6.5 %collective-permute-start.7 = (f32[192,1536]{1,0:T(8,128)S(1)}, f32[192,1536]{1,0:T(8,128)S(1)}, u32[]{:S(2)}, u32[]{:S(2)}) collective-permute-start(f32[192,1536]{1,0:T(8,128)S(1)} %get-tuple-element.24), channel_id=1, source_target_pairs={{0,1},{1,0},{2,3},{3,2},{4,5},{5,4},{6,7},{7,6},{8,9},{9,8},{10,11... | collective-permute-start | bytes 3538952 | tf_op jit(solution)/shard_map/ppermute | solution.py:32
  122.8 30.8 %all-to-all-start.1 = ((bf16[16,32,1536]{2,1,0:T(8,128)(2,1)}), bf16[16,32,1536]{2,1,0:T(8,128)(2,1)S(1)}, u32[]{:S(2)}, u32[]{:S(2)}) async-start(bf16[16,32,1536]{2,1,0:T(8,128)(2,1)} %shard_map.90), calls=%async_computation.1 | async-start | bytes 3145728 | tf_op jit(solution)/shard_map/all_to_all | solution.py:240
  144.7 1.1 copy-start.2
  145.8 1.1 copy-start.4
  146.9 1.1 copy-start.6
